TPU v7x, 32 devices: a whole 2x2x4 slice. The times are simulated.
32 devices in a mesh: dp: 8 (over y, x, core), fsdp: 4 (over z).
Axes of the slice: x: 2, y: 2, z: 4, core: 2. Of those that a mesh axis runs over, the one named last changes fastest.
Arguments:
- hidden_in: bfloat16 [2, 2, 256, 64, 768], P(None, None, ('dp', 'fsdp')), may hold values from -6 to 6
- lengths: int32 [2, 2, 256], P(None, None, ('dp', 'fsdp')), may hold values from 4 to 64, as said below
- partner: int32 [2, 256], replicated, may hold values from 0 to 255, each once within a row
- language: int32 [2, 256], replicated, may hold values from 0 to 7
- token_cotangent: bfloat16 [2, 2, 256, 64, 768], P(None, None, ('dp', 'fsdp')), may hold values from -6 to 6
- query_weight: bfloat16 [768, 768], P(('dp', 'fsdp')), may hold values from -0.21875 to 0.21875
- key_weight: bfloat16 [768, 768], P(('dp', 'fsdp')), may hold values from -0.21875 to 0.21875
- value_weight: bfloat16 [768, 768], P(('dp', 'fsdp')), may hold values from -0.21875 to 0.21875
- attn_out_weight: bfloat16 [768, 768], P(('dp', 'fsdp')), may hold values from -0.875 to 0.875
- query_bias: bfloat16 [768], P(('dp', 'fsdp')), may hold values from -3 to 3
- value_bias: bfloat16 [768], P(('dp', 'fsdp')), may hold values from -3 to 3
- attn_out_bias: bfloat16 [768], P(('dp', 'fsdp')), may hold values from -3 to 3
- ln1_gain: bfloat16 [768], P(('dp', 'fsdp')), may hold values from 0.5 to 1.5
- ln1_shift: bfloat16 [768], P(('dp', 'fsdp')), may hold values from -3 to 3
- in_weight: bfloat16 [768, 3072], P(('dp', 'fsdp')), may hold values from -0.21875 to 0.21875
- in_bias: bfloat16 [3072], P(('dp', 'fsdp')), may hold values from -3 to 3
- out_weight: bfloat16 [3072, 768], P(('dp', 'fsdp')), may hold values from -0.109375 to 0.109375
- out_bias: bfloat16 [768], P(('dp', 'fsdp')), may hold values from -3 to 3
- ln2_gain: bfloat16 [768], P(('dp', 'fsdp')), may hold values from 0.5 to 1.5
- ln2_shift: bfloat16 [768], P(('dp', 'fsdp')), may hold values from -3 to 3
- pool_weight: bfloat16 [768, 768], P(('dp', 'fsdp')), may hold values from -0.21875 to 0.21875
- pool_bias: bfloat16 [768], P(('dp', 'fsdp')), may hold values from -3 to 3
Outputs:
- block_out: bfloat16 [2, 2, 256, 64, 768], P(None, None, ('dp', 'fsdp'))
- input_grad: float32 [2, 2, 256, 64, 768], P(None, None, ('dp', 'fsdp'))
- grad_query_weight: float32 [768, 768], P(('dp', 'fsdp'))
- grad_key_weight: float32 [768, 768], P(('dp', 'fsdp'))
- grad_value_weight: float32 [768, 768], P(('dp', 'fsdp'))
- grad_attn_out_weight: float32 [768, 768], P(('dp', 'fsdp'))
- grad_query_bias: float32 [768], P(('dp', 'fsdp'))
- grad_value_bias: float32 [768], P(('dp', 'fsdp'))
- grad_attn_out_bias: float32 [768], P(('dp', 'fsdp'))
- grad_ln1_gain: float32 [768], P(('dp', 'fsdp'))
- grad_ln1_shift: float32 [768], P(('dp', 'fsdp'))
- grad_in_weight: float32 [768, 3072], P(('dp', 'fsdp'))
- grad_in_bias: float32 [3072], P(('dp', 'fsdp'))
- grad_out_weight: float32 [3072, 768], P(('dp', 'fsdp'))
- grad_out_bias: float32 [768], P(('dp', 'fsdp'))
- grad_ln2_gain: float32 [768], P(('dp', 'fsdp'))
- grad_ln2_shift: float32 [768], P(('dp', 'fsdp'))
- grad_pool_weight: float32 [768, 768], P(('dp', 'fsdp'))
- grad_pool_bias: float32 [768], P(('dp', 'fsdp'))
Inputs may be any that keep to these rules, and one draw needn't show every extreme that they name: `lengths`: positions at or past a sentence's length are padding; position 0 is its first token, which the pooler reads. Each row is a permutation: source sentence i of micro-batch m translates to target sentence partner[m, i] of the same micro-batch. language[m, i] is the language of source sentence i and of its translation.
All inputs are finite; a program needn't handle non-finite values.
Results may differ from a plain program's by a relative error of at most 0.018.
The roundings to bfloat16 on the way count: a program that leaves them out, or rounds other values in their place, can miss the bound.
Values may be sent and summed in bfloat16 or wider, within the bound.
A program may use at most 320 MiB of HBM per device.

v0:
```python
import jax
import jax.numpy as jnp
from jax import lax
from jax.sharding import PartitionSpec as P

HEAD_DIM = 64


LN_EPS = 1e-06
UNIT_EPS = 1e-06
SIM_SCALE = 10.0
MARGIN = 0.3
MASKED = -1e30


def dot_plain(first_mat, second_mat):
    return jnp.dot(first_mat, second_mat, preferred_element_type=jnp.float32)


def dot_left_t(first_mat, second_mat):
    return lax.dot_general(
        first_mat, second_mat, (((0,), (0,)), ((), ())), preferred_element_type=jnp.float32
    )


def dot_right_t(first_mat, second_mat):
    return lax.dot_general(
        first_mat, second_mat, (((1,), (1,)), ((), ())), preferred_element_type=jnp.float32
    )


def norm_forward(row_data, gain_vec, shift_vec):
    centred = row_data - jnp.mean(row_data, -1, keepdims=True)
    inverse = lax.rsqrt(jnp.mean(centred * centred, -1, keepdims=True) + LN_EPS)
    normed = centred * inverse
    return (normed * gain_vec + shift_vec, normed, inverse)


def norm_backward(upstream, normed, inverse, gain_vec):
    scaled = upstream * gain_vec
    back = inverse * (
        scaled
        - jnp.mean(scaled, -1, keepdims=True)
        - normed * jnp.mean(scaled * normed, -1, keepdims=True)
    )
    return (back, jnp.sum(upstream * normed, 0), jnp.sum(upstream, 0))


def gelu_slope(inner_act):
    return (
        0.5 * (1.0 + lax.erf(inner_act * 0.7071067811865476))
        + inner_act * jnp.exp(-0.5 * inner_act * inner_act) * 0.3989422804014327
    )


def attention_scores(queries, key_rows, sent_lengths):
    seq_len = queries.shape[1]
    scores = jnp.einsum("gqhe,gkhe->ghqk", queries, key_rows, preferred_element_type=jnp.float32)
    scores = scores * queries.shape[3] ** (-0.5)
    key_valid = jnp.arange(seq_len)[None, :] < sent_lengths[:, None]
    return jnp.where(key_valid[:, None, None, :], scores, MASKED)


def on_device(
    hidden_in,
    lengths,
    partner,
    language,
    token_cotangent,
    query_weight,
    key_weight,
    value_weight,
    attn_out_weight,
    query_bias,
    value_bias,
    attn_out_bias,
    ln1_gain,
    ln1_shift,
    in_weight,
    in_bias,
    out_weight,
    out_bias,
    ln2_gain,
    ln2_shift,
    pool_weight,
    pool_bias,
):
    micro_count, sides, pair_dev, seq_len, model_width = hidden_in.shape
    sent_count = sides * pair_dev
    row_count = sent_count * seq_len
    head_shape = (sent_count, seq_len, model_width // HEAD_DIM, HEAD_DIM)
    head_scale = HEAD_DIM ** (-0.5)
    pair_count = partner.shape[1]
    offset = lax.axis_index(("dp", "fsdp")) * pair_dev
    local_pairs = offset + jnp.arange(pair_dev, dtype=jnp.int32)
    all_pairs = jnp.arange(pair_count, dtype=jnp.int32)
    pool_full, pool_shift_b = (
        lax.all_gather(pool_weight, ("dp", "fsdp"), axis=0, tiled=True),
        lax.all_gather(pool_bias, ("dp", "fsdp"), axis=0, tiled=True),
    )
    pool_shift = pool_shift_b.astype(jnp.float32)
    block_outs = []
    input_grads = []
    for micro_step in range(micro_count):
        attn_full = (
            lax.all_gather(query_weight, ("dp", "fsdp"), axis=0, tiled=True),
            lax.all_gather(key_weight, ("dp", "fsdp"), axis=0, tiled=True),
            lax.all_gather(value_weight, ("dp", "fsdp"), axis=0, tiled=True),
            lax.all_gather(attn_out_weight, ("dp", "fsdp"), axis=0, tiled=True),
            lax.all_gather(query_bias, ("dp", "fsdp"), axis=0, tiled=True),
            lax.all_gather(value_bias, ("dp", "fsdp"), axis=0, tiled=True),
            lax.all_gather(attn_out_bias, ("dp", "fsdp"), axis=0, tiled=True),
            lax.all_gather(ln1_gain, ("dp", "fsdp"), axis=0, tiled=True),
            lax.all_gather(ln1_shift, ("dp", "fsdp"), axis=0, tiled=True),
        )
        (
            query_full,
            key_full,
            value_full,
            proj_full,
            query_shift,
            value_shift,
            proj_shift,
            gain_first,
            shift_first,
        ) = attn_full
        tokens = hidden_in[micro_step].reshape(row_count, model_width)
        sent_lengths = lengths[micro_step].reshape(sent_count)
        queries = (dot_plain(tokens, query_full) + query_shift.astype(jnp.float32)).astype(
            jnp.bfloat16
        )
        queries = queries.reshape(head_shape)
        key_rows = dot_plain(tokens, key_full).astype(jnp.bfloat16).reshape(head_shape)
        values = (dot_plain(tokens, value_full) + value_shift.astype(jnp.float32)).astype(
            jnp.bfloat16
        )
        values = values.reshape(head_shape)
        scores = attention_scores(queries, key_rows, sent_lengths)
        peak = jnp.max(scores, -1, keepdims=True)
        log_totals = jnp.log(jnp.sum(jnp.exp(scores - peak), -1, keepdims=True)) + peak
        probs_b = jnp.exp(scores - log_totals).astype(jnp.bfloat16)
        mixture = jnp.einsum("ghqk,gkhe->gqhe", probs_b, values, preferred_element_type=jnp.float32)
        mixture = mixture.reshape(row_count, model_width).astype(jnp.bfloat16)
        first_sum = (
            tokens.astype(jnp.float32)
            + dot_plain(mixture, proj_full)
            + proj_shift.astype(jnp.float32)
        )
        hidden, normed_one, inverse_one = norm_forward(
            first_sum, gain_first.astype(jnp.float32), shift_first.astype(jnp.float32)
        )
        hidden_b = hidden.astype(jnp.bfloat16)
        ffn_full = (
            lax.all_gather(in_weight, ("dp", "fsdp"), axis=0, tiled=True),
            lax.all_gather(in_bias, ("dp", "fsdp"), axis=0, tiled=True),
            lax.all_gather(out_weight, ("dp", "fsdp"), axis=0, tiled=True),
            lax.all_gather(out_bias, ("dp", "fsdp"), axis=0, tiled=True),
            lax.all_gather(ln2_gain, ("dp", "fsdp"), axis=0, tiled=True),
            lax.all_gather(ln2_shift, ("dp", "fsdp"), axis=0, tiled=True),
        )
        inner_full, inner_shift, outer_full, outer_shift, gain_second, shift_second = ffn_full
        inner_act = dot_plain(hidden_b, inner_full) + inner_shift.astype(jnp.float32)
        active = jax.nn.gelu(inner_act, approximate=False).astype(jnp.bfloat16)
        second_sum = hidden + dot_plain(active, outer_full) + outer_shift.astype(jnp.float32)
        output, normed_two, inverse_two = norm_forward(
            second_sum, gain_second.astype(jnp.float32), shift_second.astype(jnp.float32)
        )
        block_outs.append(
            output.astype(jnp.bfloat16).reshape(sides, pair_dev, seq_len, model_width)
        )
        cls_rows = output.reshape(sent_count, seq_len, model_width)[:, 0].astype(jnp.bfloat16)
        pooled = jnp.tanh(dot_plain(cls_rows, pool_full) + pool_shift)
        scale_inv = lax.rsqrt(jnp.sum(pooled * pooled, -1, keepdims=True) + UNIT_EPS)
        unit_vec = pooled * scale_inv
        unit_b = unit_vec.astype(jnp.bfloat16)
        local_sources = unit_b[:pair_dev]
        local_targets = unit_b[pair_dev:]
        all_sources, all_targets = (
            lax.all_gather(local_sources, ("dp", "fsdp"), axis=0, tiled=True),
            lax.all_gather(local_targets, ("dp", "fsdp"), axis=0, tiled=True),
        )
        partner_row = partner[micro_step]
        language_row = language[micro_step]
        target_language = jnp.zeros((pair_count,), jnp.int32).at[partner_row].set(language_row)
        partner_local = lax.dynamic_slice_in_dim(partner_row, offset, pair_dev)
        language_local = lax.dynamic_slice_in_dim(language_row, offset, pair_dev)
        target_local = lax.dynamic_slice_in_dim(target_language, offset, pair_dev)
        row_positive = partner_local[:, None] == all_pairs[None, :]
        row_include = language_local[:, None] == target_language[None, :]
        row_scores = jnp.where(
            row_include,
            SIM_SCALE * dot_right_t(local_sources, all_targets) - SIM_SCALE * MARGIN * row_positive,
            MASKED,
        )
        col_positive = partner_row[:, None] == local_pairs[None, :]
        col_include = language_row[:, None] == target_local[None, :]
        col_scores = jnp.where(
            col_include,
            SIM_SCALE * dot_right_t(all_sources, local_targets) - SIM_SCALE * MARGIN * col_positive,
            MASKED,
        )
        row_lse = jax.nn.logsumexp(row_scores, axis=1)
        col_lse = jax.nn.logsumexp(col_scores, axis=0)
        every_row, every_col = (
            lax.all_gather(row_lse, ("dp", "fsdp"), axis=0, tiled=True),
            lax.all_gather(col_lse, ("dp", "fsdp"), axis=0, tiled=True),
        )
        row_grad = (
            jnp.where(
                row_include,
                jnp.exp(row_scores - row_lse[:, None]) + jnp.exp(row_scores - every_col[None, :]),
                0.0,
            )
            - 2.0 * row_positive
        )
        col_grad = (
            jnp.where(
                col_include,
                jnp.exp(col_scores - every_row[:, None]) + jnp.exp(col_scores - col_lse[None, :]),
                0.0,
            )
            - 2.0 * col_positive
        )
        row_grad_b = row_grad.astype(jnp.bfloat16)
        col_grad_b = col_grad.astype(jnp.bfloat16)
        unit_grad = SIM_SCALE * jnp.concatenate(
            [dot_plain(row_grad_b, all_targets), dot_left_t(col_grad_b, all_sources)], 0
        )
        pooled_grad = scale_inv * (
            unit_grad - unit_vec * jnp.sum(unit_grad * unit_vec, -1, keepdims=True)
        )
        pre_grad = pooled_grad * (1.0 - pooled * pooled)
        pre_grad_b = pre_grad.astype(jnp.bfloat16)
        grad_pool = dot_left_t(cls_rows, pre_grad_b)
        grad_pool_shift = jnp.sum(pre_grad, 0)
        cls_grad = dot_right_t(pre_grad_b, pool_full)
        out_grad = (
            token_cotangent[micro_step]
            .reshape(sent_count, seq_len, model_width)
            .astype(jnp.float32)
        )
        out_grad = out_grad.at[:, 0].add(cls_grad).reshape(row_count, model_width)
        ffn_full = (
            lax.all_gather(in_weight, ("dp", "fsdp"), axis=0, tiled=True),
            lax.all_gather(in_bias, ("dp", "fsdp"), axis=0, tiled=True),
            lax.all_gather(out_weight, ("dp", "fsdp"), axis=0, tiled=True),
            lax.all_gather(out_bias, ("dp", "fsdp"), axis=0, tiled=True),
            lax.all_gather(ln2_gain, ("dp", "fsdp"), axis=0, tiled=True),
            lax.all_gather(ln2_shift, ("dp", "fsdp"), axis=0, tiled=True),
        )
        inner_full, inner_shift, outer_full, outer_shift, gain_second, shift_second = ffn_full
        second_grad, grad_gain_two, grad_shift_two = norm_backward(
            out_grad, normed_two, inverse_two, gain_second.astype(jnp.float32)
        )
        second_b = second_grad.astype(jnp.bfloat16)
        grad_outer = dot_left_t(active, second_b)
        grad_outer_shift = jnp.sum(second_grad, 0)
        inner_grad = dot_right_t(second_b, outer_full) * gelu_slope(inner_act)
        grad_inner_shift = jnp.sum(inner_grad, 0)
        inner_b = inner_grad.astype(jnp.bfloat16)
        grad_inner = dot_left_t(hidden_b, inner_b)
        hidden_grad = second_grad + dot_right_t(inner_b, inner_full)
        first_grad, grad_gain_one, grad_shift_one = norm_backward(
            hidden_grad, normed_one, inverse_one, gain_first.astype(jnp.float32)
        )
        grad_proj_shift = jnp.sum(first_grad, 0)
        first_b = first_grad.astype(jnp.bfloat16)
        attn_full = (
            lax.all_gather(query_weight, ("dp", "fsdp"), axis=0, tiled=True),
            lax.all_gather(key_weight, ("dp", "fsdp"), axis=0, tiled=True),
            lax.all_gather(value_weight, ("dp", "fsdp"), axis=0, tiled=True),
            lax.all_gather(attn_out_weight, ("dp", "fsdp"), axis=0, tiled=True),
            lax.all_gather(query_bias, ("dp", "fsdp"), axis=0, tiled=True),
            lax.all_gather(value_bias, ("dp", "fsdp"), axis=0, tiled=True),
            lax.all_gather(attn_out_bias, ("dp", "fsdp"), axis=0, tiled=True),
            lax.all_gather(ln1_gain, ("dp", "fsdp"), axis=0, tiled=True),
            lax.all_gather(ln1_shift, ("dp", "fsdp"), axis=0, tiled=True),
        )
        (
            query_full,
            key_full,
            value_full,
            proj_full,
            query_shift,
            value_shift,
            proj_shift,
            gain_first,
            shift_first,
        ) = attn_full
        grad_proj = dot_left_t(mixture, first_b)
        mixture_grad = dot_right_t(first_b, proj_full).astype(jnp.bfloat16).reshape(head_shape)
        scores = attention_scores(queries, key_rows, sent_lengths)
        probs_full = jnp.exp(scores - log_totals)
        prob_grad = jnp.einsum(
            "gqhe,gkhe->ghqk", mixture_grad, values, preferred_element_type=jnp.float32
        )
        value_grad = jnp.einsum(
            "ghqk,gqhe->gkhe", probs_b, mixture_grad, preferred_element_type=jnp.float32
        )
        value_grad = value_grad.astype(jnp.bfloat16).reshape(row_count, model_width)
        score_grad = probs_full * (prob_grad - jnp.sum(prob_grad * probs_full, -1, keepdims=True))
        score_grad = score_grad.astype(jnp.bfloat16)
        query_grad = jnp.einsum(
            "ghqk,gkhe->gqhe", score_grad, key_rows, preferred_element_type=jnp.float32
        )
        query_grad = (query_grad * head_scale).astype(jnp.bfloat16).reshape(row_count, model_width)
        key_grad = jnp.einsum(
            "ghqk,gqhe->gkhe", score_grad, queries, preferred_element_type=jnp.float32
        )
        key_grad = (key_grad * head_scale).astype(jnp.bfloat16).reshape(row_count, model_width)
        grad_query = dot_left_t(tokens, query_grad)
        grad_key = dot_left_t(tokens, key_grad)
        grad_value = dot_left_t(tokens, value_grad)
        grad_query_shift = jnp.sum(query_grad.astype(jnp.float32), 0)
        grad_value_shift = jnp.sum(value_grad.astype(jnp.float32), 0)
        token_grad = (
            first_grad
            + dot_right_t(query_grad, query_full)
            + dot_right_t(key_grad, key_full)
            + dot_right_t(value_grad, value_full)
        )
        input_grads.append(token_grad.reshape(sides, pair_dev, seq_len, model_width))
        step_sum = (
            grad_query,
            grad_key,
            grad_value,
            grad_proj,
            grad_query_shift,
            grad_value_shift,
            grad_proj_shift,
            grad_gain_one,
            grad_shift_one,
            grad_inner,
            grad_inner_shift,
            grad_outer,
            grad_outer_shift,
            grad_gain_two,
            grad_shift_two,
            grad_pool,
            grad_pool_shift,
        )
        if micro_step == 0:
            totals_all = tuple(step_sum)
        else:
            totals_all = tuple(jax.tree.map(jnp.add, tuple(totals_all), tuple(step_sum)))
    (
        sum_query,
        sum_key,
        sum_value,
        sum_proj,
        sum_query_shift,
        sum_value_shift,
        sum_proj_shift,
        sum_gain_one,
        sum_shift_one,
        sum_inner,
        sum_inner_shift,
        sum_outer,
        sum_outer_shift,
        sum_gain_two,
        sum_shift_two,
        sum_pool,
        sum_pool_shift,
    ) = totals_all
    totals_all = (
        lax.psum_scatter(sum_query, ("dp", "fsdp"), scatter_dimension=0, tiled=True),
        lax.psum_scatter(sum_key, ("dp", "fsdp"), scatter_dimension=0, tiled=True),
        lax.psum_scatter(sum_value, ("dp", "fsdp"), scatter_dimension=0, tiled=True),
        lax.psum_scatter(sum_proj, ("dp", "fsdp"), scatter_dimension=0, tiled=True),
        lax.psum_scatter(sum_query_shift, ("dp", "fsdp"), scatter_dimension=0, tiled=True),
        lax.psum_scatter(sum_value_shift, ("dp", "fsdp"), scatter_dimension=0, tiled=True),
        lax.psum_scatter(sum_proj_shift, ("dp", "fsdp"), scatter_dimension=0, tiled=True),
        lax.psum_scatter(sum_gain_one, ("dp", "fsdp"), scatter_dimension=0, tiled=True),
        lax.psum_scatter(sum_shift_one, ("dp", "fsdp"), scatter_dimension=0, tiled=True),
        lax.psum_scatter(sum_inner, ("dp", "fsdp"), scatter_dimension=0, tiled=True),
        lax.psum_scatter(sum_inner_shift, ("dp", "fsdp"), scatter_dimension=0, tiled=True),
        lax.psum_scatter(sum_outer, ("dp", "fsdp"), scatter_dimension=0, tiled=True),
        lax.psum_scatter(sum_outer_shift, ("dp", "fsdp"), scatter_dimension=0, tiled=True),
        lax.psum_scatter(sum_gain_two, ("dp", "fsdp"), scatter_dimension=0, tiled=True),
        lax.psum_scatter(sum_shift_two, ("dp", "fsdp"), scatter_dimension=0, tiled=True),
        lax.psum_scatter(sum_pool, ("dp", "fsdp"), scatter_dimension=0, tiled=True),
        lax.psum_scatter(sum_pool_shift, ("dp", "fsdp"), scatter_dimension=0, tiled=True),
    )
    return (jnp.stack(block_outs), jnp.stack(input_grads)) + tuple(totals_all)


def solution(mesh):
    placed = (
        P(None, None, ("dp", "fsdp"), None, None),
        P(None, None, ("dp", "fsdp")),
        P(),
        P(),
        P(None, None, ("dp", "fsdp"), None, None),
        P(("dp", "fsdp"), None),
        P(("dp", "fsdp"), None),
        P(("dp", "fsdp"), None),
        P(("dp", "fsdp"), None),
        P(("dp", "fsdp")),
        P(("dp", "fsdp")),
        P(("dp", "fsdp")),
        P(("dp", "fsdp")),
        P(("dp", "fsdp")),
        P(("dp", "fsdp"), None),
        P(("dp", "fsdp")),
        P(("dp", "fsdp"), None),
        P(("dp", "fsdp")),
        P(("dp", "fsdp")),
        P(("dp", "fsdp")),
        P(("dp", "fsdp"), None),
        P(("dp", "fsdp")),
    )
    return jax.shard_map(
        on_device,
        mesh=mesh,
        in_specs=placed,
        out_specs=(
            P(None, None, ("dp", "fsdp"), None, None),
            P(None, None, ("dp", "fsdp"), None, None),
            P(("dp", "fsdp"), None),
            P(("dp", "fsdp"), None),
            P(("dp", "fsdp"), None),
            P(("dp", "fsdp"), None),
            P(("dp", "fsdp")),
            P(("dp", "fsdp")),
            P(("dp", "fsdp")),
            P(("dp", "fsdp")),
            P(("dp", "fsdp")),
            P(("dp", "fsdp"), None),
            P(("dp", "fsdp")),
            P(("dp", "fsdp"), None),
            P(("dp", "fsdp")),
            P(("dp", "fsdp")),
            P(("dp", "fsdp")),
            P(("dp", "fsdp"), None),
            P(("dp", "fsdp")),
        ),
        check_vma=False,
    )
```

profile of v0, /device:TPU:0, one launch (start us, length us, event | category | flops | bytes accessed | tf_op | source)
XLA Modules:
  0.0 1576.4 jit_solution(15992525543545984243)
XLA Ops:
  30.6 43.0 %all-reduce.26 = (bf16[768]{0:T(1024)(128)(2,1)S(1)}, bf16[768]{0:T(1024)(128)(2,1)S(1)}, bf16[768]{0:T(1024)(128)(2,1)S(1)}, bf16[768]{0:T(1024)(128)(2,1)S(1)}...) all-reduce(bf16[768]{0:T(1024)(128)(2,1)S(1)} %dynamic-update-slice, ...), channel_id=1, replica_groups=mesh['dp'=8,'fsdp'=4] {'dp','fsdp'}, use_global_device_ids=true, to_apply=%add | all-reduce | flops 9984 | bytes 39936
  80.3 6.4 copy_bitcast_fusion
  86.7 4.3 convolution_convert_fusion.3
  90.9 5.9 reshape.556
  96.8 26.7 %all-gather.8.cloned.1.call-done = bf16[768,768]{1,0:T(8,128)(2,1)} async-done(((bf16[24,768]{1,0:T(8,128)(2,1)}), bf16[768,768]{1,0:T(8,128)(2,1)}) %all-gather.8.cloned.1.call-update) | async-done | bytes 1179664 | tf_op jit(solution)/shard_map/all_gather | solution.py:108
  123.5 4.3 add_convert_fusion.5
  127.8 6.0 reshape.560
  136.3 6.0 reshape.562
  144.8 6.1 reshape.557
  150.9 28.5 %all-gather.10.cloned.1.call-done = bf16[768,768]{1,0:T(8,128)(2,1)} async-done(((bf16[24,768]{1,0:T(8,128)(2,1)}), bf16[768,768]{1,0:T(8,128)(2,1)}) %all-gather.10.cloned.1.call-update) | async-done | bytes 1179664 | tf_op jit(solution)/shard_map/all_gather | solution.py:106
  179.4 4.3 add_convert_fusion.4
  183.7 5.9 reshape.561
  189.6 6.6 copy.247
  198.8 5.9 reshape.563
  204.6 6.4 copy.263
  211.1 4.7 fusion.31
  228.5 6.7 all-gather.14.cloned.1.call-done
  235.2 4.0 fusion.203
  250.8 4.2 copy.228
  254.9 5.4 convert_element_type.252
  260.3 4.1 fusion.202
  266.6 33.7 %all-gather.16.cloned.1.call-done = bf16[768,3072]{1,0:T(8,128)(2,1)} async-done(((bf16[24,3072]{1,0:T(8,128)(2,1)}), bf16[768,3072]{1,0:T(8,128)(2,1)}) %all-gather.16.cloned.1.call-update) | async-done | bytes 4718608 | tf_op jit(solution)/shard_map/all_gather | solution.py:154
  300.3 7.9 fusion.179
  308.2 4.5 copy-done.117
  312.7 61.6 %fusion.2 = (bf16[1024,3072]{1,0:T(8,128)(2,1)}, bf16[1024,3072]{1,0:T(8,128)(2,1)}, f32[1024,3072]{1,0:T(8,128)}) fusion(f32[3072]{0:T(1024)S(1)} %convert_element_type.257, f32[1024,3072]{1,0:T(8,128)S(1)} %fusion.179, bf16[768,3072]{1,0:T(8,128)(2,1)S(1)} %copy-done.100, f32[1024,768]{1,0:T(8,128)S(1)} %copy-done.20, f32[768]{0:T(1024)S(1)} %convert_element_type.255, ...), kind=kOutput, calls=%fused_computation.8 | convolution fusion | flops 5251006464 | bytes 45639680 | tf_op jit(solution)/shard_map/dot_general | solution.py:17
  374.4 10.6 fusion.204
  386.9 5.4 fusion.205
  396.1 25.0 %all-gather.20.cloned.1.call-done = bf16[768,768]{1,0:T(8,128)(2,1)} async-done(((bf16[24,768]{1,0:T(8,128)(2,1)}), bf16[768,768]{1,0:T(8,128)(2,1)}) %all-gather.20.cloned.1.call-update) | async-done | bytes 1179664 | tf_op jit(solution)/shard_map/all_gather | solution.py:98
  424.6 69.7 %all_gather.125 = bf16[256,768]{1,0:T(8,128)(2,1)S(1)} all-gather(bf16[8,768]{1,0:T(8,128)(2,1)S(1)} %get-tuple-element.204), channel_id=1, replica_groups=mesh['dp'=8,'fsdp'=4] {'dp','fsdp'}, dimensions={0}, use_global_device_ids=true | all-gather | bytes 405504 | tf_op jit(solution)/shard_map/all_gather | solution.py:180
  495.5 66.7 %all_gather.122 = bf16[256,768]{1,0:T(8,128)(2,1)S(1)} all-gather(bf16[8,768]{1,0:T(8,128)(2,1)S(1)} %get-tuple-element.202), channel_id=1, replica_groups=mesh['dp'=8,'fsdp'=4] {'dp','fsdp'}, dimensions={0}, use_global_device_ids=true | all-gather | bytes 405504 | tf_op jit(solution)/shard_map/all_gather | solution.py:179
  563.0 68.5 %all_gather.126 = bf16[256,768]{1,0:T(8,128)(2,1)S(1)} all-gather(bf16[8,768]{1,0:T(8,128)(2,1)S(1)} %get-tuple-element.205), channel_id=1, replica_groups=mesh['dp'=8,'fsdp'=4] {'dp','fsdp'}, dimensions={0}, use_global_device_ids=true | all-gather | bytes 405504 | tf_op jit(solution)/shard_map/all_gather | solution.py:179
  632.6 66.5 %all_gather.121 = bf16[256,768]{1,0:T(8,128)(2,1)S(1)} all-gather(bf16[8,768]{1,0:T(8,128)(2,1)S(1)} %get-tuple-element.203), channel_id=1, replica_groups=mesh['dp'=8,'fsdp'=4] {'dp','fsdp'}, dimensions={0}, use_global_device_ids=true | all-gather | bytes 405504 | tf_op jit(solution)/shard_map/all_gather | solution.py:180
  701.5 40.0 %all-reduce.25 = (f32[256]{0:T(256)S(1)}, f32[256]{0:T(256)S(1)}, f32[256]{0:T(256)S(1)}, f32[256]{0:T(256)S(1)}) all-reduce(f32[256]{0:T(256)S(1)} %get-tuple-element.196, f32[256]{0:T(256)S(1)} %get-tuple-element.194, f32[256]{0:T(256)S(1)} %get-tuple-element.192, ...), channel_id=1, replica_groups=mesh['dp'=8,'fsdp'=4] {'dp','fsdp'}, use_global_device_ids=true, to_apply=%add.13 | all-reduce | flops 1024 | bytes 8192
  749.8 5.5 copy.255
  762.9 5.5 fusion.39
  770.3 6.4 fusion.189
  776.8 14.8 fusion.210
  791.6 8.1 multiply_reduce_fusion.3
  799.8 12.7 fusion.211
  812.5 14.1 fusion.191
  826.6 4.9 fusion.89
  834.1 6.0 reshape.558
  840.2 9.1 multiply_reduce_fusion.1
  866.0 4.2 copy.250
  873.4 6.0 reshape.559
  879.5 9.3 multiply_reduce_fusion
  896.4 4.2 copy.266
  913.9 5.7 convert_reduce_fusion.2
  919.5 4.2 copy.262
  926.9 6.7 convert_reduce_fusion.3
  933.6 4.2 copy.246
  948.1 8.2 convert_reduce_fusion
  956.4 4.2 copy.268
  963.7 8.2 convert_reduce_fusion.1
  972.0 4.2 copy.252
  986.5 8.5 fusion.92
  995.0 10.5 convolution_add_fusion
  1006.2 9.3 fusion.43
  1015.6 11.1 convolution_add_fusion.1
  1027.5 40.6 %all-reduce.24 = (f32[768]{0:T(1024)S(1)}, f32[768]{0:T(1024)S(1)}, f32[768]{0:T(1024)S(1)}, f32[768]{0:T(1024)S(1)}, f32[768]{0:T(1024)S(1)}, /*index=5*/f32[30...) all-reduce(f32[768]{0:T(1024)S(1)} %add.491, ...), channel_id=6, replica_groups=mesh['dp'=8,'fsdp'=4] {'dp','fsdp'}, use_global_device_ids=true, to_apply=%region_42.43.clone | all-reduce | flops 9984 | bytes 79872
  1091.6 91.1 %reduce-scatter.22.cloned.1.call-done = f32[24,768]{1,0:T(8,128)} async-done(((f32[768,768]{1,0:T(8,128)}), f32[24,768]{1,0:T(8,128)}) %reduce-scatter.22.cloned.1.call-update) | async-done | bytes 73744
  1182.6 103.8 %reduce-scatter.26.cloned.1.call-done = f32[24,768]{1,0:T(8,128)} async-done(((f32[768,768]{1,0:T(8,128)}), f32[24,768]{1,0:T(8,128)}) %reduce-scatter.26.cloned.1.call-update) | async-done | bytes 73744
  1286.5 142.1 %reduce-scatter.18.cloned.1.call-done = f32[96,768]{1,0:T(8,128)} async-done(((f32[3072,768]{1,0:T(8,128)}), f32[96,768]{1,0:T(8,128)}) %reduce-scatter.18.cloned.1.call-update) | async-done | bytes 294928 | tf_op jit(solution)/shard_map/reduce_scatter | solution.py:377
  1428.6 140.8 %reduce-scatter.16.cloned.1.call-done = f32[24,3072]{1,0:T(8,128)} async-done(((f32[768,3072]{1,0:T(8,128)}), f32[24,3072]{1,0:T(8,128)}) %reduce-scatter.16.cloned.1.call-update) | async-done | bytes 294928 | tf_op jit(solution)/shard_map/reduce_scatter | solution.py:375
  (475 shorter events, 190.5 us)
Async XLA Ops:
  7.2 79.5 %all-gather.12.cloned.1.call-start = ((), (), s32[]{:S(2)}) async-start(), calls=%async_computation.9 | async-start | bytes 1216512 | tf_op jit(solution)/shard_map/all_gather | solution.py:107
  7.9 115.6 %all-gather.8.cloned.1.call-start = ((), (), s32[]{:S(2)}) async-start(), calls=%async_computation.7 | async-start | bytes 1216512 | tf_op jit(solution)/shard_map/all_gather | solution.py:108
  8.7 170.7 %all-gather.10.cloned.1.call-start = ((), (), s32[]{:S(2)}) async-start(), calls=%async_computation.8 | async-start | bytes 1216512 | tf_op jit(solution)/shard_map/all_gather | solution.py:106
  9.4 225.8 %all-gather.14.cloned.1.call-start = ((), (), s32[]{:S(2)}) async-start(), calls=%async_computation.10 | async-start | bytes 1216512 | tf_op jit(solution)/shard_map/all_gather | solution.py:109
  10.0 290.3 %all-gather.16.cloned.1.call-start = ((), (), s32[]{:S(2)}) async-start(), calls=%async_computation.11 | async-start | bytes 4866048 | tf_op jit(solution)/shard_map/all_gather | solution.py:154
  10.6 363.8 %all-gather.18.cloned.1.call-start = ((), (), s32[]{:S(2)}) async-start(), calls=%async_computation.12 | async-start | bytes 4866048 | tf_op jit(solution)/shard_map/all_gather | solution.py:156
  11.1 409.9 %all-gather.20.cloned.1.call-start = ((), (), s32[]{:S(2)}) async-start(), calls=%async_computation.13 | async-start | bytes 1216512 | tf_op jit(solution)/shard_map/all_gather | solution.py:98
  11.9 1079.7 %reduce-scatter.20.cloned.1.call-start = ((), (), s32[]{:S(2)}) async-start(), calls=%async_computation.17 | async-start | bytes 2433024 | tf_op jit(solution)/shard_map/reduce_scatter | solution.py:381
  13.5 14.5 copy-start.92
  13.5 15.4 copy-start.94
  14.9 202.7 %copy-start.75 = (pred[16,64]{1,0:T(8,128)(4,1)}, pred[16,64]{1,0:T(8,128)(4,1)S(1)}, u32[]{:S(2)}) copy-start(pred[16,64]{1,0:T(8,128)(4,1)S(1)} %iota_compare_fusion.2) | copy-start | bytes 3076
  15.0 230.8 %copy-start.73 = (pred[16,64]{1,0:T(8,128)(4,1)}, pred[16,64]{1,0:T(8,128)(4,1)S(1)}, u32[]{:S(2)}) copy-start(pred[16,64]{1,0:T(8,128)(4,1)S(1)} %iota_compare_fusion.3) | copy-start | bytes 3076
  15.8 13.1 copy-start.96
  73.6 311.9 %copy-start.62 = (f32[768]{0:T(1024)}, f32[768]{0:T(1024)S(1)}, u32[]{:S(2)}) copy-start(f32[768]{0:T(1024)S(1)} %convert_element_type.255) | copy-start | bytes 9220
  79.5 116.7 %copy-start.51 = (bf16[1,2,8,64,768]{4,3,2,1,0:T(8,128)(2,1)}, bf16[1,2,8,64,768]{4,3,2,1,0:T(8,128)(2,1)S(1)}, u32[]{:S(2)}) copy-start(bf16[1,2,8,64,768]{4,3,2,1,0:T(8,128)(2,1)S(1)} %get-tuple-element.201) | copy-start | bytes 4718596
  189.6 6.6 copy-start.103
  239.2 61.1 %copy-start.9 = (f32[1024,768]{1,0:T(8,128)}, f32[1024,768]{1,0:T(8,128)S(1)}, u32[]{:S(2)}) copy-start(f32[1024,768]{1,0:T(8,128)S(1)} %get-tuple-element.235) | copy-start | bytes 9437188
  239.2 61.1 %copy-start.68 = (f32[1024]{0:T(1024)}, f32[1024]{0:T(1024)S(1)}, u32[]{:S(2)}) copy-start(f32[1024]{0:T(1024)S(1)} %broadcast_multiply_fusion.9) | copy-start | bytes 12292
  242.2 58.1 %copy-start.70 = (f32[1024]{0:T(1024)}, f32[1024]{0:T(1024)S(1)}, u32[]{:S(2)}) copy-start(f32[1024]{0:T(1024)S(1)} %add_rsqrt_fusion.1) | copy-start | bytes 12292
  300.3 12.4 copy-start.20
  300.3 12.4 copy-start.100
  312.7 61.6 %copy-start.91 = (f32[768]{0:T(1024)S(1)}, f32[768]{0:T(1024)}, u32[]{:S(2)}) copy-start(f32[768]{0:T(1024)} %convert_element_type.259) | copy-start | bytes 9220
  374.3 11.2 slice-start.6
  374.3 11.2 slice-start.8
  374.3 11.2 slice-start.7
  374.3 11.2 slice-start.9
  393.0 28.1 %copy-start.77 = (f32[768]{0:T(1024)S(1)}, f32[768]{0:T(1024)}, u32[]{:S(2)}) copy-start(f32[768]{0:T(1024)} %convert_element_type.277) | copy-start | bytes 9220
  394.3 100.8 %copy-start.107 = (s32[256]{0:T(256)S(1)}, s32[256]{0:T(256)}, u32[]{:S(2)}) copy-start(s32[256]{0:T(256)} %copy-done.106) | copy-start | bytes 3076
  394.3 100.8 %copy-start.111 = (s32[8]{0:T(128)S(1)}, s32[8]{0:T(128)}, u32[]{:S(2)}) copy-start(s32[8]{0:T(128)} %fusion.152) | copy-start | bytes 100
  394.3 100.8 %copy-start.112 = (s32[8]{0:T(128)S(1)}, s32[8]{0:T(128)}, u32[]{:S(2)}) copy-start(s32[8]{0:T(128)} %fusion.153) | copy-start | bytes 100
  394.3 167.9 %copy-start.95 = (s32[1,256]{1,0:T(1,128)S(1)}, s32[1,256]{1,0:T(1,128)}, u32[]{:S(2)}) copy-start(s32[1,256]{1,0:T(1,128)} %copy-done.94) | copy-start | bytes 3076
  394.3 167.9 %copy-start.99 = (s32[1,256]{1,0:T(1,128)S(1)}, s32[1,256]{1,0:T(1,128)}, u32[]{:S(2)}) copy-start(s32[1,256]{1,0:T(1,128)} %copy-done.98) | copy-start | bytes 3076
  394.3 167.9 %copy-start.113 = (s32[8]{0:T(128)S(1)}, s32[8]{0:T(128)}, u32[]{:S(2)}) copy-start(s32[8]{0:T(128)} %dynamic_slice.20) | copy-start | bytes 100
  394.4 167.9 %copy-start.116 = (s32[8]{0:T(128)S(1)}, s32[8]{0:T(128)}, u32[]{:S(2)}) copy-start(s32[8]{0:T(128)} %iota_add_fusion) | copy-start | bytes 100
  394.4 237.9 %copy-start.93 = (s32[1,256]{1,0:T(1,128)S(1)}, s32[1,256]{1,0:T(1,128)}, u32[]{:S(2)}) copy-start(s32[1,256]{1,0:T(1,128)} %copy-done.92) | copy-start | bytes 3076
  394.4 237.9 %copy-start.97 = (s32[1,256]{1,0:T(1,128)S(1)}, s32[1,256]{1,0:T(1,128)}, u32[]{:S(2)}) copy-start(s32[1,256]{1,0:T(1,128)} %copy-done.96) | copy-start | bytes 3076
  394.4 237.8 %copy-start.110 = (s32[8]{0:T(128)S(1)}, s32[8]{0:T(128)}, u32[]{:S(2)}) copy-start(s32[8]{0:T(128)} %dynamic_slice.23) | copy-start | bytes 100
  394.4 305.5 %copy-start.109 = (s32[256]{0:T(256)S(1)}, s32[256]{0:T(256)}, u32[]{:S(2)}) copy-start(s32[256]{0:T(256)} %copy-done.108) | copy-start | bytes 3076
  394.4 305.5 %copy-start.114 = (s32[8]{0:T(128)S(1)}, s32[8]{0:T(128)}, u32[]{:S(2)}) copy-start(s32[8]{0:T(128)} %fusion.150) | copy-start | bytes 100
  394.4 305.5 %copy-start.115 = (s32[8]{0:T(128)S(1)}, s32[8]{0:T(128)}, u32[]{:S(2)}) copy-start(s32[8]{0:T(128)} %fusion.151) | copy-start | bytes 100
  747.4 8.0 copy-start.18
  770.3 321.3 %reduce-scatter.14.cloned.1.call-start = ((), (), s32[]{:S(2)}) async-start(), calls=%async_computation.14 | async-start | bytes 2433024 | tf_op jit(solution)/shard_map/reduce_scatter | solution.py:369
  770.3 21.3 %slice-start.4 = ((s8[4718592]{0:T(1024)(128)(4,1)}), s8[4194304]{0:T(1024)(128)(4,1)S(1)}, s32[]{:S(2)}) async-start(s8[4718592]{0:T(1024)(128)(4,1)} %bitcast.254), calls=%async_computation.25 | async-start | bytes 8388608
  776.7 14.9 copy-start.41
  776.7 23.0 %copy-start.39 = (f32[1024,768]{1,0:T(8,128)}, f32[1024,768]{1,0:T(8,128)S(1)}, u32[]{:S(2)}) copy-start(f32[1024,768]{1,0:T(8,128)S(1)} %get-tuple-element.215) | copy-start | bytes 9437188
  776.8 14.9 copy-start.21
  776.8 14.9 slice-start.5
  791.6 8.1 copy-start.27
  799.8 12.7 copy-start.11
  812.5 14.2 copy-start.36
  812.5 14.2 copy-start.55
  834.1 15.1 slice-start.2
  840.2 9.1 slice-start.3
  862.0 229.5 %reduce-scatter.24.cloned.1.call-start = ((), (), s32[]{:S(2)}) async-start(), calls=%async_computation.19 | async-start | bytes 2433024
  873.4 15.3 slice-start
  879.4 9.3 slice-start.1
  913.4 269.2 %reduce-scatter.22.cloned.1.call-start = ((), (), s32[]{:S(2)}) async-start(), calls=%async_computation.18 | async-start | bytes 2433024
  947.9 338.6 %reduce-scatter.26.cloned.1.call-start = ((), (), s32[]{:S(2)}) async-start(), calls=%async_computation.20 | async-start | bytes 2433024
  986.2 8.8 copy-start.40
  986.2 442.4 %reduce-scatter.18.cloned.1.call-start = ((), (), s32[]{:S(2)}) async-start(), calls=%async_computation.16 | async-start | bytes 9732096 | tf_op jit(solution)/shard_map/reduce_scatter | solution.py:377
  1005.5 10.0 copy-start.13
  1005.6 563.9 %reduce-scatter.16.cloned.1.call-start = ((), (), s32[]{:S(2)}) async-start(), calls=%async_computation.15 | async-start | bytes 9732096 | tf_op jit(solution)/shard_map/reduce_scatter | solution.py:375
  1026.7 47.2 %copy-start.29 = (bf16[1024,768]{1,0:T(8,128)(2,1)S(1)}, bf16[1024,768]{1,0:T(8,128)(2,1)}, u32[]{:S(2)}) copy-start(bf16[1024,768]{1,0:T(8,128)(2,1)} %copy-done.28) | copy-start | bytes 4718596
  1026.7 47.2 %copy-start.31 = (bf16[1024,768]{1,0:T(8,128)(2,1)S(1)}, bf16[1024,768]{1,0:T(8,128)(2,1)}, u32[]{:S(2)}) copy-start(bf16[1024,768]{1,0:T(8,128)(2,1)} %copy-done.30) | copy-start | bytes 4718596
  (78 other events, 217.5 us)
Sparse Core Ops, SparseCore 0:
  10.8 56.7 all-gather.11
  70.5 53.0 all-gather.7
  126.3 53.0 all-gather.9
  182.1 53.0 all-gather.13
  237.8 62.4 all-gather.15
  303.0 62.3 all-gather.17
  368.1 52.9 all-gather.19
  770.4 98.7 reduce-scatter.19
  875.9 98.0 reduce-scatter.13
  979.7 98.0 reduce-scatter.23
  1084.6 98.0 reduce-scatter.21
  1188.4 98.0 reduce-scatter.25
  1294.0 134.5 reduce-scatter.17
  1434.9 134.4 reduce-scatter.15
where the time goes:
time: 1580 us
  waiting for transfers between devices  603 us (38%)
  blocking collectives  395 us (25%)
  matrix products  324 us (21%)
  local copies, waits for them, and re-layouts  198 us (13%)
  other arithmetic  38.8 us (2%)
  between operations  16 us (1%)
    unnamed x17, waiting for transfers between devices  199 us
    reduce_scatter x1, waiting for transfers between devices, on_device(): lax.psum_scatter(sum_outer, ('dp', 'fsdp'), scatter_dimension=0, tiled=True)  142 us
    reduce_scatter x1, waiting for transfers between devices, on_device(): lax.psum_scatter(sum_inner, ('dp', 'fsdp'), scatter_dimension=0, tiled=True)  141 us
    all_gather x2, blocking collectives, on_device(): lax.all_gather(local_targets, ('dp', 'fsdp'), axis=0, tiled=True)  136 us
    all_gather x2, blocking collectives, on_device(): lax.all_gather(local_sources, ('dp', 'fsdp'), axis=0, tiled=True)  135 us
    unnamed x3, blocking collectives  124 us
    dot_general x16, matrix products, dot_plain(): return jnp.dot(first_mat, second_mat, preferred_element_type=jnp.float32)  120 us
    dot_general x18, matrix products, dot_right_t(): lax.dot_general(first_mat, second_mat, (((1,), (1,)), ((), ())), preferre...  69.7 us
  transfers between devices with their start and end apart: 14, of which 9 were waited for; matrix products, arithmetic and copies ran while one was open for 32% of the time, Pallas kernels for 0%

commit v1 on v0

v1 whole, which is shorter than its diff:
```python
import functools

import jax
import jax.numpy as jnp
from jax import lax
from jax.experimental import pallas as pl
from jax.experimental.pallas import tpu as pltpu
from jax.sharding import PartitionSpec as P

HEAD_DIM = 64


LN_EPS = 1e-06
UNIT_EPS = 1e-06
SIM_SCALE = 10.0
MARGIN = 0.3
MASKED = -1e30
MIB = 1024 * 1024


MESH_ID = pl.DeviceIdType.MESH
AXES = ("dp", "fsdp")


class Layout:
    def __init__(self, mesh_shape):
        slow, fast = mesh_shape["dp"], mesh_shape["fsdp"]
        self.slow, self.count = slow, slow * fast
        if slow == 8:
            self.dims = (2, 2, 2, fast)
            self.orders = ((3, 1, 0, 2), (3, 0, 1, 2))
        else:
            self.dims = (slow, fast)
            self.orders = ((1, 0), (1, 0))
        self.sends = sum(size - 1 for size in self.dims)

    def own(self):
        digits = [lax.axis_index("fsdp")]
        rest = lax.axis_index("dp")
        for size in self.dims[-2::-1]:
            digits.insert(0, rest % size)
            rest = rest // size
        return digits

    def device(self, digits):
        slow = digits[0]
        for size, digit in zip(self.dims[1:-1], digits[1:-1]):
            slow = slow * size + digit
        return (slow, digits[-1])

    def shifted(self, own, dim, step):
        size = self.dims[dim]
        out = list(own)
        out[dim] = (own[dim] + step) % size
        return out

    def first_slot(self, order, stage):
        return sum(self.dims[dim] - 1 for dim in order[:stage])

    def greet(self, own):
        barrier = pltpu.get_barrier_semaphore()
        for dim, size in enumerate(self.dims):
            for step in range(1, size):
                pl.semaphore_signal(
                    barrier,
                    inc=1,
                    device_id=self.device(self.shifted(own, dim, step)),
                    device_id_type=MESH_ID,
                )
        pl.semaphore_wait(barrier, self.sends)


class GatherJob:
    def __init__(self, layout, own, order, shard, full, sems, columns=None):
        self.layout, self.own, self.order = layout, own, order
        self.shard, self.full, self.columns = shard, full, columns
        self.send_sems, self.recv_sems, self.local_sem = sems

    def block(self, digits, done):
        index = tuple(
            slice(None) if dim in done else digits[dim] for dim in range(len(self.layout.dims))
        )
        if self.columns is not None:
            index = index + (slice(None), pl.ds(*self.columns))
        return self.full.at[index]

    def piece(self):
        if self.columns is not None:
            return self.shard.at[:, pl.ds(*self.columns)]
        return self.shard

    def copies(self, stage, sending):
        dim, done = self.order[stage], self.order[:stage]
        base = self.layout.first_slot(self.order, stage)
        out = []
        for step in range(1, self.layout.dims[dim]):
            slot = base + step - 1
            other = self.layout.shifted(self.own, dim, step if sending else -step)
            target = self.block(self.own if sending else other, done)
            source = self.piece() if sending and stage == 0 else target
            out.append(
                pltpu.make_async_remote_copy(
                    src_ref=source,
                    dst_ref=target,
                    send_sem=self.send_sems.at[slot],
                    recv_sem=self.recv_sems.at[slot],
                    device_id=self.layout.device(other),
                    device_id_type=MESH_ID,
                )
            )
        return out

    def local(self):
        return pltpu.make_async_copy(self.piece(), self.block(self.own, ()), self.local_sem)

    def advance(self, stage):
        if stage == 0:
            self.local().start()
        else:
            for copy in self.copies(stage - 1, False):
                copy.wait_recv()
            if stage == 1:
                self.local().wait()
        if stage < len(self.order):
            for copy in self.copies(stage, True):
                copy.start()

    def finish(self):
        for stage in range(len(self.order)):
            for copy in self.copies(stage, True):
                copy.wait_send()


def run_rounds(jobs, stages, width=2):
    rounds = []
    last = stages + (len(jobs) - 1) // width
    for step in range(last + 1):
        todo = []
        for index, job in enumerate(jobs):
            stage = step - index // width
            if 0 <= stage <= stages:
                todo.append((job, stage))
        rounds.append(todo)
    return rounds


class ScatterJob:
    def __init__(self, layout, own, order, part, sums, lands, result, sems, columns=None):
        self.layout, self.own, self.order = layout, own, order
        self.part, self.sums, self.lands, self.result = part, sums, lands, result
        self.send_sems, self.recv_sems, self.local_sem = sems
        self.columns = columns

    def tail(self):
        if self.columns is not None:
            return (slice(None), pl.ds(*self.columns))
        return ()

    def local(self):
        dim = self.order[0]
        index = [slice(None)] * len(self.layout.dims)
        index[dim] = self.own[dim]
        return pltpu.make_async_copy(
            self.part.at[tuple(index) + self.tail()], self.sums[0], self.local_sem
        )

    def copies(self, stage):
        dim = self.order[stage]
        base = self.layout.first_slot(self.order, stage)
        left = [d for d in range(len(self.layout.dims)) if d not in self.order[:stage]]
        out = []
        for step in range(1, self.layout.dims[dim]):
            slot = base + step - 1
            there = self.layout.shifted(self.own, dim, step)
            index = tuple(there[dim] if d == dim else slice(None) for d in left)
            if stage == 0:
                source = self.part.at[index + self.tail()]
            else:
                source = self.sums[stage - 1].at[index]
            out.append(
                pltpu.make_async_remote_copy(
                    src_ref=source,
                    dst_ref=self.lands[stage].at[step - 1],
                    send_sem=self.send_sems.at[slot],
                    recv_sem=self.recv_sems.at[slot],
                    device_id=self.layout.device(there),
                    device_id_type=MESH_ID,
                )
            )
        return out

    def add(self, stage):
        dim = self.order[stage]
        left = [d for d in range(len(self.layout.dims)) if d not in self.order[:stage]]
        rest = [d for d in left if d != dim]
        sizes = [self.layout.dims[d] for d in rest]
        total = 1
        for size in sizes:
            total *= size

        def body(flat):
            digits = []
            for size in reversed(sizes):
                digits.insert(0, flat % size)
                flat = flat // size
            if stage == 0:
                own_index = tuple(digits)
                value = self.sums[0][own_index].astype(jnp.float32)
            else:
                where = dict(zip(rest, digits))
                where[dim] = self.own[dim]
                value = self.sums[stage - 1][tuple(where[d] for d in left)].astype(jnp.float32)
            for step in range(1, self.layout.dims[dim]):
                value = value + self.lands[stage][(step - 1,) + tuple(digits)].astype(jnp.float32)
            if rest:
                target = self.sums[stage]
                target[tuple(digits)] = value.astype(target.dtype)
            elif self.columns is not None:
                self.result[:, pl.ds(*self.columns)] = value
            else:
                self.result[...] = value

        if total == 1:
            body(0)
        else:
            pl.loop(0, total)(body)

    def advance(self, stage):
        if stage == 0:
            self.local().start()
        else:
            for copy in self.copies(stage - 1):
                copy.wait_recv()
            if stage == 1:
                self.local().wait()
            self.add(stage - 1)
        if stage < len(self.order):
            for copy in self.copies(stage):
                copy.start()

    def finish(self):
        for stage in range(len(self.order)):
            for copy in self.copies(stage):
                copy.wait_send()


def scatter_buffers(layout, order, rows, columns, dtype):
    sums, lands = [], []
    for stage, dim in enumerate(order):
        rest = tuple(
            size for d, size in enumerate(layout.dims) if d not in order[: stage + 1]
        )
        lands.append(pltpu.VMEM((layout.dims[dim] - 1,) + rest + (rows, columns), dtype))
        if stage < len(order) - 1:
            sums.append(pltpu.VMEM(rest + (rows, columns), dtype))
    return sums + lands


def gather_kernel(layout, plan, count, *refs):
    shards, fulls = refs[:count], refs[count : 2 * count]
    send_sems, recv_sems, local_sems = refs[2 * count :]
    own = layout.own()
    layout.greet(own)
    jobs = [
        GatherJob(
            layout,
            own,
            layout.orders[way],
            shards[which],
            fulls[which],
            (send_sems.at[at], recv_sems.at[at], local_sems.at[at]),
            columns,
        )
        for at, (which, way, columns) in enumerate(plan)
    ]
    for todo in run_rounds(jobs, len(layout.dims)):
        for job, stage in todo:
            job.advance(stage)
    for job in jobs:
        job.finish()


def gather_all(layout, arrays, plan, collective_id):
    anywhere = pl.BlockSpec(memory_space=pl.ANY)
    return pl.pallas_call(
        functools.partial(gather_kernel, layout, plan, len(arrays)),
        out_shape=[jax.ShapeDtypeStruct(layout.dims + a.shape, a.dtype) for a in arrays],
        in_specs=[anywhere] * len(arrays),
        out_specs=[anywhere] * len(arrays),
        scratch_shapes=[
            pltpu.SemaphoreType.DMA((len(plan), layout.sends)),
            pltpu.SemaphoreType.DMA((len(plan), layout.sends)),
            pltpu.SemaphoreType.DMA((len(plan),)),
        ],
        compiler_params=pltpu.CompilerParams(
            collective_id=collective_id, has_side_effects=True, vmem_limit_bytes=16 * MIB
        ),
    )(*arrays)


def scatter_kernel(layout, plan, count, buffers, *refs):
    parts, results = refs[:count], refs[count : 2 * count]
    scratch, (send_sems, recv_sems, local_sems) = refs[2 * count : -3], refs[-3:]
    own = layout.own()
    layout.greet(own)
    jobs = []
    stages = len(layout.dims)
    for at, (which, way, columns) in enumerate(plan):
        mine = scratch[at * buffers : (at + 1) * buffers]
        jobs.append(
            ScatterJob(
                layout,
                own,
                layout.orders[way][::-1],
                parts[which],
                mine[: stages - 1],
                mine[stages - 1 :],
                results[which],
                (send_sems.at[at], recv_sems.at[at], local_sems.at[at]),
                columns,
            )
        )
    for todo in run_rounds(jobs, stages):
        for job, stage in todo:
            job.advance(stage)
    for job in jobs:
        job.finish()


def scatter_all(layout, arrays, plan, collective_id):
    stages = len(layout.dims)
    scratch = []
    for which, way, columns in plan:
        rows, width = arrays[which].shape[-2:]
        width = width if columns is None else columns[1]
        scratch += scatter_buffers(
            layout, layout.orders[way][::-1], rows, width, arrays[which].dtype
        )
    return pl.pallas_call(
        functools.partial(scatter_kernel, layout, plan, len(arrays), 2 * stages - 1),
        out_shape=[jax.ShapeDtypeStruct(a.shape[-2:], jnp.float32) for a in arrays],
        in_specs=[pl.BlockSpec(memory_space=pl.ANY)] * len(arrays),
        out_specs=[pl.BlockSpec(memory_space=pltpu.VMEM)] * len(arrays),
        scratch_shapes=scratch
        + [
            pltpu.SemaphoreType.DMA((len(plan), layout.sends)),
            pltpu.SemaphoreType.DMA((len(plan), layout.sends)),
            pltpu.SemaphoreType.DMA((len(plan),)),
        ],
        compiler_params=pltpu.CompilerParams(
            collective_id=collective_id, has_side_effects=True, vmem_limit_bytes=60 * MIB
        ),
    )(*arrays)


def cut(which, way, width, pieces):
    if width % (pieces * 128):
        return [(which, way, None)]
    step = width // pieces
    return [(which, way, (at * step, step)) for at in range(pieces)]


def weave(first, second):
    out = []
    for at in range(max(len(first), len(second))):
        out += first[at : at + 1] + second[at : at + 1]
    return out


def small_pack(layout, vectors):
    flat = jnp.concatenate([v.astype(jnp.float32).reshape(v.shape[0], -1) for v in vectors], 1)
    width = -(-flat.shape[1] // 1024) * 1024
    flat = jnp.pad(flat, ((0, 0), (0, width - flat.shape[1])))
    return flat.reshape(flat.shape[0], width // 128, 128)


def dot_plain(first_mat, second_mat):
    return jnp.dot(first_mat, second_mat, preferred_element_type=jnp.float32)


def dot_left_t(first_mat, second_mat):
    return lax.dot_general(
        first_mat, second_mat, (((0,), (0,)), ((), ())), preferred_element_type=jnp.float32
    )


def dot_right_t(first_mat, second_mat):
    return lax.dot_general(
        first_mat, second_mat, (((1,), (1,)), ((), ())), preferred_element_type=jnp.float32
    )


def norm_forward(row_data, gain_vec, shift_vec):
    centred = row_data - jnp.mean(row_data, -1, keepdims=True)
    inverse = lax.rsqrt(jnp.mean(centred * centred, -1, keepdims=True) + LN_EPS)
    normed = centred * inverse
    return (normed * gain_vec + shift_vec, normed, inverse)


def norm_backward(upstream, normed, inverse, gain_vec):
    scaled = upstream * gain_vec
    back = inverse * (
        scaled
        - jnp.mean(scaled, -1, keepdims=True)
        - normed * jnp.mean(scaled * normed, -1, keepdims=True)
    )
    return (back, jnp.sum(upstream * normed, 0), jnp.sum(upstream, 0))


def gelu_slope(inner_act):
    return (
        0.5 * (1.0 + lax.erf(inner_act * 0.7071067811865476))
        + inner_act * jnp.exp(-0.5 * inner_act * inner_act) * 0.3989422804014327
    )


def attention_scores(queries, key_rows, sent_lengths):
    seq_len = queries.shape[1]
    scores = jnp.einsum("gqhe,gkhe->ghqk", queries, key_rows, preferred_element_type=jnp.float32)
    scores = scores * queries.shape[3] ** (-0.5)
    key_valid = jnp.arange(seq_len)[None, :] < sent_lengths[:, None]
    return jnp.where(key_valid[:, None, None, :], scores, MASKED)


def on_device(
    layout,
    hidden_in,
    lengths,
    partner,
    language,
    token_cotangent,
    query_weight,
    key_weight,
    value_weight,
    attn_out_weight,
    query_bias,
    value_bias,
    attn_out_bias,
    ln1_gain,
    ln1_shift,
    in_weight,
    in_bias,
    out_weight,
    out_bias,
    ln2_gain,
    ln2_shift,
    pool_weight,
    pool_bias,
):
    micro_count, sides, pair_dev, seq_len, model_width = hidden_in.shape
    inner_width = in_weight.shape[1]
    count = layout.count
    node_dev = sides * pair_dev
    sent_count = micro_count * node_dev
    row_count = sent_count * seq_len
    head_shape = (sent_count, seq_len, model_width // HEAD_DIM, HEAD_DIM)
    head_scale = HEAD_DIM ** (-0.5)
    pair_count = partner.shape[1]
    device = lax.axis_index("dp") * (count // layout.slow) + lax.axis_index("fsdp")

    vectors = (
        query_bias,
        value_bias,
        attn_out_bias,
        ln1_gain,
        ln1_shift,
        out_bias,
        ln2_gain,
        ln2_shift,
        pool_bias,
        in_bias,
    )
    small = small_pack(layout, [v[None] for v in vectors])[0]
    arrays = [
        query_weight,
        key_weight,
        value_weight,
        attn_out_weight,
        small,
        pool_weight,
        in_weight,
        out_weight,
    ]
    plan = [(4, 0, None), (0, 1, None), (1, 0, None), (2, 1, None), (3, 0, None), (5, 1, None)]
    plan += weave(cut(6, 0, inner_width, 4), cut(7, 1, model_width, 3))
    gathered = gather_all(layout, arrays, tuple(plan), 0)
    query_full, key_full, value_full, proj_full, small_full, pool_full, inner_full, outer_full = [
        full.reshape((count * array.shape[0],) + array.shape[1:])
        for full, array in zip(gathered, arrays)
    ]
    small_rows = small_full.reshape(count, -1)
    wide = []
    at = 0
    for v in vectors:
        wide.append(small_rows[:, at : at + v.shape[0]].reshape(-1))
        at += v.shape[0]
    (
        query_shift,
        value_shift,
        proj_shift,
        gain_first,
        shift_first,
        outer_shift,
        gain_second,
        shift_second,
        pool_shift,
        inner_shift,
    ) = wide

    tokens = hidden_in.reshape(row_count, model_width)
    sent_lengths = lengths.reshape(sent_count)
    queries = (dot_plain(tokens, query_full) + query_shift).astype(jnp.bfloat16)
    queries = queries.reshape(head_shape)
    key_rows = dot_plain(tokens, key_full).astype(jnp.bfloat16).reshape(head_shape)
    values = (dot_plain(tokens, value_full) + value_shift).astype(jnp.bfloat16)
    values = values.reshape(head_shape)
    scores = attention_scores(queries, key_rows, sent_lengths)
    peak = jnp.max(scores, -1, keepdims=True)
    log_totals = jnp.log(jnp.sum(jnp.exp(scores - peak), -1, keepdims=True)) + peak
    probs_b = jnp.exp(scores - log_totals).astype(jnp.bfloat16)
    mixture = jnp.einsum("ghqk,gkhe->gqhe", probs_b, values, preferred_element_type=jnp.float32)
    mixture = mixture.reshape(row_count, model_width).astype(jnp.bfloat16)
    first_sum = tokens.astype(jnp.float32) + dot_plain(mixture, proj_full) + proj_shift
    hidden, normed_one, inverse_one = norm_forward(first_sum, gain_first, shift_first)
    hidden_b = hidden.astype(jnp.bfloat16)
    inner_act = dot_plain(hidden_b, inner_full) + inner_shift
    active = jax.nn.gelu(inner_act, approximate=False).astype(jnp.bfloat16)
    second_sum = hidden + dot_plain(active, outer_full) + outer_shift
    output, normed_two, inverse_two = norm_forward(second_sum, gain_second, shift_second)
    block_out = output.astype(jnp.bfloat16).reshape(hidden_in.shape)

    cls_rows = output.reshape(sent_count, seq_len, model_width)[:, 0].astype(jnp.bfloat16)
    pooled = jnp.tanh(dot_plain(cls_rows, pool_full) + pool_shift)
    scale_inv = lax.rsqrt(jnp.sum(pooled * pooled, -1, keepdims=True) + UNIT_EPS)
    unit_vec = pooled * scale_inv
    unit_b = unit_vec.astype(jnp.bfloat16)
    (units,) = gather_all(layout, [unit_b], ((0, 0, None),), 1)
    units = units.reshape(count, micro_count, node_dev, model_width)
    units = jnp.moveaxis(units, 1, 0).reshape(micro_count, count * node_dev, model_width)
    pair_ids = jnp.arange(pair_count, dtype=jnp.int32)
    hit = partner[:, :, None] == pair_ids[None, None, :]
    target_language = jnp.sum(jnp.where(hit, language[:, :, None], 0), 1)

    def nodes(first, second):
        shape = (micro_count, count, 1, pair_dev)
        joined = jnp.concatenate([first.reshape(shape), second.reshape(shape)], 2)
        return joined.reshape(micro_count, count * node_dev)

    tongue = nodes(language, target_language)
    place = nodes(partner, jnp.broadcast_to(pair_ids, partner.shape))
    side = nodes(jnp.zeros_like(partner), jnp.ones_like(partner))
    across = side[:, :, None] != side[:, None, :]
    positive = across & (place[:, :, None] == place[:, None, :])
    include = across & (tongue[:, :, None] == tongue[:, None, :])
    similar = jnp.einsum("mid,mjd->mij", units, units, preferred_element_type=jnp.float32)
    scored = jnp.where(include, SIM_SCALE * similar - SIM_SCALE * MARGIN * positive, MASKED)
    totals = jax.nn.logsumexp(scored, axis=2)
    grad_sim = jnp.where(
        include,
        jnp.exp(scored - totals[:, :, None]) + jnp.exp(scored - totals[:, None, :]),
        0.0,
    )
    grad_sim = (grad_sim - 2.0 * positive).astype(jnp.bfloat16)
    grad_sim = lax.dynamic_slice_in_dim(grad_sim, device * node_dev, node_dev, 1)
    unit_grad = SIM_SCALE * jnp.einsum(
        "mij,mjd->mid", grad_sim, units, preferred_element_type=jnp.float32
    )
    unit_grad = unit_grad.reshape(sent_count, model_width)
    pooled_grad = scale_inv * (
        unit_grad - unit_vec * jnp.sum(unit_grad * unit_vec, -1, keepdims=True)
    )
    pre_grad = pooled_grad * (1.0 - pooled * pooled)
    pre_grad_b = pre_grad.astype(jnp.bfloat16)
    grad_pool = dot_left_t(cls_rows, pre_grad_b)
    grad_pool_shift = jnp.sum(pre_grad, 0)
    cls_grad = dot_right_t(pre_grad_b, pool_full)
    out_grad = token_cotangent.reshape(sent_count, seq_len, model_width).astype(jnp.float32)
    first = jnp.arange(seq_len)[None, :, None] == 0
    out_grad = out_grad + jnp.where(first, cls_grad[:, None, :], 0.0)
    out_grad = out_grad.reshape(row_count, model_width)
    second_grad, grad_gain_two, grad_shift_two = norm_backward(
        out_grad, normed_two, inverse_two, gain_second
    )
    second_b = second_grad.astype(jnp.bfloat16)
    grad_outer = dot_left_t(active, second_b)
    grad_outer_shift = jnp.sum(second_grad, 0)
    inner_grad = dot_right_t(second_b, outer_full) * gelu_slope(inner_act)
    grad_inner_shift = jnp.sum(inner_grad, 0)
    inner_b = inner_grad.astype(jnp.bfloat16)
    grad_inner = dot_left_t(hidden_b, inner_b)
    hidden_grad = second_grad + dot_right_t(inner_b, inner_full)
    first_grad, grad_gain_one, grad_shift_one = norm_backward(
        hidden_grad, normed_one, inverse_one, gain_first
    )
    grad_proj_shift = jnp.sum(first_grad, 0)
    first_b = first_grad.astype(jnp.bfloat16)
    grad_proj = dot_left_t(mixture, first_b)
    mixture_grad = dot_right_t(first_b, proj_full).astype(jnp.bfloat16).reshape(head_shape)
    probs_full = jnp.exp(scores - log_totals)
    prob_grad = jnp.einsum(
        "gqhe,gkhe->ghqk", mixture_grad, values, preferred_element_type=jnp.float32
    )
    value_grad = jnp.einsum(
        "ghqk,gqhe->gkhe", probs_b, mixture_grad, preferred_element_type=jnp.float32
    )
    value_grad = value_grad.astype(jnp.bfloat16).reshape(row_count, model_width)
    score_grad = probs_full * (prob_grad - jnp.sum(prob_grad * probs_full, -1, keepdims=True))
    score_grad = score_grad.astype(jnp.bfloat16)
    query_grad = jnp.einsum(
        "ghqk,gkhe->gqhe", score_grad, key_rows, preferred_element_type=jnp.float32
    )
    query_grad = (query_grad * head_scale).astype(jnp.bfloat16).reshape(row_count, model_width)
    key_grad = jnp.einsum(
        "ghqk,gqhe->gkhe", score_grad, queries, preferred_element_type=jnp.float32
    )
    key_grad = (key_grad * head_scale).astype(jnp.bfloat16).reshape(row_count, model_width)
    grad_query = dot_left_t(tokens, query_grad)
    grad_key = dot_left_t(tokens, key_grad)
    grad_value = dot_left_t(tokens, value_grad)
    grad_query_shift = jnp.sum(query_grad.astype(jnp.float32), 0)
    grad_value_shift = jnp.sum(value_grad.astype(jnp.float32), 0)
    token_grad = (
        first_grad
        + dot_right_t(query_grad, query_full)
        + dot_right_t(key_grad, key_full)
        + dot_right_t(value_grad, value_full)
    )
    input_grad = token_grad.reshape(hidden_in.shape)

    small_grad = small_pack(
        layout,
        [
            v.reshape(count, -1)
            for v in (
                grad_query_shift,
                grad_value_shift,
                grad_proj_shift,
                grad_gain_one,
                grad_shift_one,
                grad_outer_shift,
                grad_gain_two,
                grad_shift_two,
                grad_pool_shift,
                grad_inner_shift,
            )
        ],
    )
    partial_sums = [
        grad_query,
        grad_key,
        grad_value,
        grad_proj,
        grad_pool,
        grad_inner,
        grad_outer,
    ]
    parts = [
        part.astype(jnp.bfloat16).reshape(layout.dims + (-1, part.shape[1]))
        for part in partial_sums
    ]
    parts.append(small_grad.reshape(layout.dims + small_grad.shape[1:]))
    plan = weave(cut(5, 0, inner_width, 4), cut(6, 1, model_width, 3))
    plan += [(3, 1, None), (4, 0, None), (0, 1, None), (1, 0, None), (2, 1, None), (7, 0, None)]
    sums = scatter_all(layout, parts, tuple(plan), 2)
    small_sum = sums[7].reshape(-1)
    narrow = []
    at = 0
    for v in vectors:
        narrow.append(small_sum[at : at + v.shape[0]])
        at += v.shape[0]
    (
        sum_query_shift,
        sum_value_shift,
        sum_proj_shift,
        sum_gain_one,
        sum_shift_one,
        sum_outer_shift,
        sum_gain_two,
        sum_shift_two,
        sum_pool_shift,
        sum_inner_shift,
    ) = narrow
    return (
        block_out,
        input_grad,
        sums[0],
        sums[1],
        sums[2],
        sums[3],
        sum_query_shift,
        sum_value_shift,
        sum_proj_shift,
        sum_gain_one,
        sum_shift_one,
        sums[5],
        sum_inner_shift,
        sums[6],
        sum_outer_shift,
        sum_gain_two,
        sum_shift_two,
        sums[4],
        sum_pool_shift,
    )


def solution(mesh):
    rows = P(("dp", "fsdp"), None)
    vector = P(("dp", "fsdp"))
    sentences = P(None, None, ("dp", "fsdp"), None, None)
    placed = (
        (sentences, P(None, None, ("dp", "fsdp")), P(), P(), sentences)
        + (rows,) * 4
        + (vector,) * 5
        + (rows, vector, rows)
        + (vector,) * 3
        + (rows, vector)
    )
    return jax.shard_map(
        functools.partial(on_device, Layout(mesh.shape)),
        mesh=mesh,
        in_specs=placed,
        out_specs=(sentences, sentences)
        + (rows,) * 4
        + (vector,) * 5
        + (rows, vector, rows)
        + (vector,) * 3
        + (rows, vector),
        check_vma=False,
    )
```

time: 1580 us -> 741 us (0.47)
  waiting for transfers between devices: 603 us -> 0 us
  blocking collectives: 395 us -> 0 us
  Pallas kernels: 0 us -> 203 us
  local copies, waits for them, and re-layouts: 198 us -> 174 us
    reduce_scatter x4 -> x0, waiting for transfers between devices: 283 us -> none  [the longest x1 142 us: on_device(): lax.psum_scatter(sum_outer, ('dp', 'fsdp'), scatter_dimension=0, tiled=True)]
    all_gather x4 -> x0, blocking collectives: 271 us -> none  [the longest x2 136 us: on_device(): lax.all_gather(local_targets, ('dp', 'fsdp'), axis=0, tiled=True)]
    pallas_call x0 -> x3, Pallas kernels: none -> 203 us  [the longest x2 113 us: gather_all(): pl.pallas_call(functools.partial(gather_kernel, layout, plan, len(arrays)...]
    unnamed x17 -> x0, waiting for transfers between devices: 199 us -> none
    unnamed x3 -> x0, blocking collectives: 124 us -> none
    all_gather x7 -> x0, waiting for transfers between devices: 121 us -> none  [the longest x1 33.7 us: on_device(): lax.all_gather(in_weight, ('dp', 'fsdp'), axis=0, tiled=True)]
    unnamed x293 -> x146, local copies, waits for them, and re-layouts: 49.8 us -> 29.2 us
    dot_general x16 -> x7, matrix products: 69.3 us -> 58 us  [dot_left_t(): lax.dot_general(first_mat, second_mat, (((0,), (0,)), ((), ())), preferre...]
  transfers between devices with their start and end apart: 14 -> 0, of which waited for: 9 -> 0; matrix products, arithmetic and copies ran while one was open for 32% -> 0% of each run, Pallas kernels for 0% -> 0%
where the time goes in v1:
time: 741 us; the launch traced here: 732 us
  matrix products  309 us (42%)
  Pallas kernels  203 us (27%)
  local copies, waits for them, and re-layouts  174 us (23%)
  other arithmetic  43.7 us (6%)
    pallas_call x2, Pallas kernels, gather_all(): pl.pallas_call(functools.partial(gather_kernel, layout, plan, len(arrays)...  113 us
    dot_general x7, matrix products, dot_plain(): return jnp.dot(first_mat, second_mat, preferred_element_type=jnp.float32)  112 us
    pallas_call x1, Pallas kernels, scatter_all(): pl.pallas_call(functools.partial(scatter_kernel, layout, plan, len(arrays...  90.3 us
    dot_general x7, matrix products, dot_right_t(): lax.dot_general(first_mat, second_mat, (((1,), (1,)), ((), ())), preferre...  58.6 us
    dot_general x7, matrix products, dot_left_t(): lax.dot_general(first_mat, second_mat, (((0,), (0,)), ((), ())), preferre...  58 us
    unnamed x146, local copies, waits for them, and re-layouts  29.2 us
    reshape x2, local copies, waits for them, and re-layouts, on_device(): values = values.reshape(head_shape)  19.6 us
    reshape x2, local copies, waits for them, and re-layouts, on_device(): dot_plain(tokens, key_full).astype(jnp.bfloat16).reshape(head_shape)  19.4 us

profile of v1, /device:TPU:0, one launch (start us, length us, event | category | flops | bytes accessed | tf_op | source)
XLA Modules:
  0.0 731.6 jit_solution(14269384870338044112)
XLA Ops:
  7.2 87.1 %shard_map.357 = (bf16[2,2,2,4,24,768]{5,4,3,2,1,0:T(8,128)(2,1)S(1)}, bf16[2,2,2,4,24,768]{5,4,3,2,1,0:T(8,128)(2,1)S(1)}, bf16[2,2,2,4,24,768]{5,4,3,2,1,0:T(8...) custom-call(bf16[24,768]{1,0:T(8,128)(2,1)S(1)} %copy-done.4, ...), custom_call_target="tpu_custom_call" | custom-call | tf_op jit(solution)/shard_map/pallas_call | solution.py:285
  94.3 2.1 copy-done.9
  96.4 2.1 copy-done.10
  98.6 1.0 copy-done.13
  99.6 1.0 copy-done.15
  102.1 1.4 add.188
  103.5 6.8 fusion.46
  110.3 10.1 %reshape.374 = bf16[32,64,12,64]{1,0,3,2:T(8,128)(2,1)} reshape(bf16[2048,768]{0,1:T(8,128)(2,1)} %fusion.46) | data formatting | bytes 6291456 | tf_op jit(solution)/shard_map/reshape | solution.py:513
  120.4 6.0 fusion.44
  126.4 10.1 %reshape.376 = bf16[32,64,12,64]{1,0,3,2:T(8,128)(2,1)} reshape(bf16[2048,768]{0,1:T(8,128)(2,1)} %fusion.44) | data formatting | bytes 6291456 | tf_op jit(solution)/shard_map/reshape | solution.py:514
  136.5 9.3 %copy.102 = bf16[32,64,12,64]{3,1,2,0:T(8,128)(2,1)} copy(bf16[32,64,12,64]{1,0,3,2:T(8,128)(2,1)} %reshape.376) | data formatting | bytes 6291456 | tf_op jit(solution)/shard_map/reshape | solution.py:514
  146.0 17.5 %fusion.15 = (f32[32,12,64]{2,1,0:T(8,128)S(1)}, f32[32,12,64,64]{2,3,1,0:T(8,128)}) fusion(pred[32,64]{1,0:T(8,128)(4,1)S(1)} %iota_compare_fusion.1, bf16[32,64,12,64]{3,1,2,0:T(8,128)(2,1)} %copy.102, bf16[32,64,12,64]{1,0,3,2:T(8,128)(2,1)} %reshape.374), kind=kOutput, calls=%fused_computation.34 | convolution fusion | flops 206020608 | bytes 12683264 | tf_op jit(solution)/shard_map/gqhe,gkhe->ghqk/dot_general | solution.py:419
  163.4 6.8 exponential_reduce_fusion
  170.4 6.2 fusion.45
  176.6 10.1 %reshape.372 = bf16[32,64,12,64]{1,0,3,2:T(8,128)(2,1)} reshape(bf16[2048,768]{0,1:T(8,128)(2,1)} %fusion.45) | data formatting | bytes 6291456 | tf_op jit(solution)/shard_map/reshape | solution.py:516
  186.7 9.5 %copy.112 = bf16[32,64,12,64]{3,1,2,0:T(8,128)(2,1)} copy(bf16[32,64,12,64]{1,0,3,2:T(8,128)(2,1)} %reshape.372) | data formatting | bytes 6291456 | tf_op jit(solution)/shard_map/reshape | solution.py:516
  196.2 8.5 %convert_bitcast_fusion.1 = bf16[32,64,12,64]{1,3,2,0:T(8,128)(2,1)S(1)} fusion(bf16[32,64,12,64]{3,1,2,0:T(8,128)(2,1)} %copy.112, f32[32,12,64,64]{2,3,1,0:T(8,128)} %get-tuple-element.86, f32[32,12,64]{2,1,0:T(8,128)S(1)} %log_add_fusion, pred[32,64]{1,0:T(8,128)(4,1)S(1)} %iota_compare_fusion.1), kind=kOutput, calls=%fused_computation.60 | convolution fusion | flops 209190912 | bytes 12683264 | tf_op jit(solution)/shard_map/ghqk,gkhe->gqhe/dot_general | solution.py:521
  204.6 7.7 %copy.105 = bf16[32,64,12,64]{1,0,3,2:T(8,128)(2,1)} copy(bf16[32,64,12,64]{1,3,2,0:T(8,128)(2,1)S(1)} %convert_bitcast_fusion.1) | data formatting | bytes 6291456 | tf_op jit(solution)/shard_map/convert_element_type | solution.py:522
  212.4 9.8 %convert_element_type.208 = bf16[2048,768]{0,1:T(8,128)(2,1)} reshape(bf16[32,64,12,64]{1,0,3,2:T(8,128)(2,1)} %copy.105) | data formatting | bytes 6291456 | tf_op jit(solution)/shard_map/convert_element_type | solution.py:522
  222.3 6.0 fusion.87
  228.4 2.7 copy-done.22
  233.0 70.4 %fusion.2 = (bf16[2048,3072]{1,0:T(8,128)(2,1)}, f32[2048,3072]{1,0:T(8,128)}) fusion(f32[3072]{0:T(1024)S(1)} %add.200, bf16[768,3072]{1,0:T(8,128)(2,1)} %bitcast.175, f32[2048,768]{1,0:T(8,128)} %copy-done.22, f32[768]{0:T(1024)S(1)} %add.197, f32[768]{0:T(1024)S(1)} %mul.222, f32[2048]{0:T(1024)S(1)} %add_rsqrt_fusion.1, ...), kind=kOutput, calls=%fused_computation.4 | convolution fusion | flops 10086776832 | bytes 48793600 | tf_op jit(solution)/shard_map/dot_general | solution.py:378
  303.5 16.0 %fusion.88 = (f32[2048]{0:T(1024)S(1)}, f32[2048,768]{1,0:T(8,128)S(1)}) fusion(f32[768]{0:T(1024)S(1)} %add.204, bf16[2048,3072]{1,0:T(8,128)(2,1)} %get-tuple-element.89, bf16[3072,768]{1,0:T(8,128)(2,1)} %bitcast.179, f32[768]{0:T(1024)S(1)} %add.197, f32[768]{0:T(1024)S(1)} %mul.222, f32[2048]{0:T(1024)S(1)} %add_rsqrt_fusion.1, ...), kind=kOutput, calls=%fused_computation.155 | convolution fusion | flops 9674684416 | bytes 29918208 | tf_op jit(solution)/shard_map/dot_general | solution.py:378
  319.5 2.6 copy-done.18
  323.2 3.4 multiply_add_fusion
  326.7 1.7 copy-done.27
  329.0 25.9 %shard_map.358 = bf16[2,2,2,4,32,768]{5,4,3,2,1,0:T(8,128)(2,1)S(1)} custom-call(bf16[32,768]{1,0:T(8,128)(2,1)S(1)} %multiply_convert_fusion.3.refs_0_), custom_call_target="tpu_custom_call" | custom-call | tf_op jit(solution)/shard_map/pallas_call | solution.py:285
  356.0 1.9 fusion.89
  358.0 1.3 copy-done.30
  360.2 1.0 compare_and_fusion.1
  361.2 1.2 convolution_multiply_fusion
  363.2 1.7 fusion.25
  365.1 5.4 multiply_reduce_fusion.1
  370.6 6.0 fusion.83
  376.6 23.5 %fusion.90 = (f32[3072]{0:T(1024)S(1)}, bf16[2048,3072]{1,0:T(8,128)(2,1)}) fusion(f32[2048,3072]{1,0:T(8,128)} %get-tuple-element.90, f32[3072]{0:T(1024)S(1)} %add.200, bf16[3072,768]{1,0:T(8,128)(2,1)S(1)} %bitcast.182, f32[2048,768]{1,0:T(8,128)S(1)} %get-tuple-element.62), kind=kOutput, calls=%fused_computation.157 | convolution fusion | flops 9740743680 | bytes 48783360 | tf_op jit(solution)/shard_map/dot_general | solution.py:388
  400.1 18.0 %multiply_reduce_fusion.2 = (f32[768]{0:T(1024)S(1)}, f32[2048]{0:T(1024)S(1)}, f32[2048]{0:T(1024)S(1)}, f32[768]{0:T(1024)S(1)}, f32[2048,768]{1,0:T(8,128)}) fusion(f32[2048,768]{1,0:T(8,128)} %copy-done.22, f32[2048]{0:T(1024)S(1)} %add_rsqrt_fusion.1, f32[2048]{0:T(1024)S(1)} %broadcast_multiply_fusion.5, f32[768]{0:T(1024)S(1)} %mul.222, ...), kind=kOutput, calls=%fused_computation.41 | convolution fusion | flops 9679398912 | bytes 36217856 | tf_op jit(solution)/shard_map/dot_general | solution.py:388
  418.1 6.0 fusion.84
  424.2 2.6 copy-done.21
  426.8 4.2 convolution_convert_fusion.1
  431.0 10.6 %reshape.417 = bf16[32,64,12,64]{3,2,1,0:T(8,128)(2,1)} reshape(bf16[2048,768]{1,0:T(8,128)(2,1)} %convolution_convert_fusion.1) | data formatting | bytes 6291456 | tf_op jit(solution)/shard_map/reshape | solution.py:598
  441.6 13.0 %convert_reduce_fusion = (f32[12,64]{1,0:T(8,128)S(1)}, bf16[32,64,12,64]{3,1,2,0:T(8,128)(2,1)}) fusion(bf16[32,64,12,64]{3,2,1,0:T(8,128)(2,1)} %reshape.417, f32[32,12,64,64]{2,3,1,0:T(8,128)} %get-tuple-element.86, f32[32,12,64]{2,1,0:T(8,128)S(1)} %copy-done.26, pred[32,64]{1,0:T(8,128)(4,1)S(1)} %copy-done.39), kind=kOutput, calls=%fused_computation.25 | convolution fusion | flops 212335872 | bytes 12686336 | tf_op jit(solution)/shard_map/ghqk,gqhe->gkhe/dot_general | solution.py:603
  454.7 14.7 %multiply_reduce_fusion = (f32[32,12,64]{2,1,0:T(8,128)S(1)}, f32[32,12,64,64]{2,3,1,0:T(8,128)}) fusion(f32[32,12,64,64]{2,3,1,0:T(8,128)} %get-tuple-element.86, f32[32,12,64]{2,1,0:T(8,128)S(1)} %copy-done.26, pred[32,64]{1,0:T(8,128)(4,1)S(1)} %copy-done.39, bf16[32,64,12,64]{3,1,2,0:T(8,128)(2,1)} %copy.112, bf16[32,64,12,64]{3,2,1,0:T(8,128)(2,1)} %reshape.417), kind=kOutput, calls=%fused_computation.30 | convolution fusion | flops 209166336 | bytes 19073024 | tf_op jit(solution)/shard_map/gqhe,gkhe->ghqk/dot_general | solution.py:600
  469.4 10.1 %multiply_convert_fusion.2 = bf16[32,12,64,64]{2,3,1,0:T(8,128)(2,1)S(1)} fusion(f32[32,12,64,64]{2,3,1,0:T(8,128)} %get-tuple-element.99, f32[32,12,64,64]{2,3,1,0:T(8,128)} %get-tuple-element.86, f32[32,12,64]{2,1,0:T(8,128)S(1)} %get-tuple-element.98, f32[32,12,64]{2,1,0:T(8,128)S(1)} %copy-done.26, pred[32,64]{1,0:T(8,128)(4,1)S(1)} %copy-done.39), kind=kLoop, calls=%fused_computation.29 | loop fusion | flops 9437184 | bytes 15927296 | tf_op jit(solution)/shard_map/convert_element_type | solution.py:608
  479.5 9.1 %convert_reduce_fusion.1 = (f32[12,64]{1,0:T(8,128)S(1)}, bf16[32,64,12,64]{3,1,2,0:T(8,128)(2,1)}) fusion(bf16[32,64,12,64]{3,1,2,0:T(8,128)(2,1)} %copy.102, bf16[32,12,64,64]{2,3,1,0:T(8,128)(2,1)S(1)} %multiply_convert_fusion.2), kind=kOutput, calls=%fused_computation.26 | convolution fusion | flops 207617280 | bytes 9440256 | tf_op jit(solution)/shard_map/ghqk,gkhe->gqhe/dot_general | solution.py:609
  490.2 17.0 %convolution_convert_fusion = bf16[3072,768]{1,0:T(8,128)(2,1)} fusion(bf16[2048,3072]{1,0:T(8,128)(2,1)} %get-tuple-element.89, f32[2048,768]{1,0:T(8,128)} %copy-done.24), kind=kOutput, calls=%fused_computation.72 | convolution fusion | flops 9667608576 | bytes 23592960 | tf_op jit(solution)/shard_map/dot_general | solution.py:382
  507.2 16.2 %fusion.30 = bf16[768,3072]{1,0:T(8,128)(2,1)} fusion(bf16[2048,3072]{1,0:T(8,128)(2,1)} %get-tuple-element.105, f32[2048,768]{1,0:T(8,128)S(1)} %bitcast.194, f32[768]{0:T(1024)S(1)} %copy-done.56, f32[768]{0:T(1024)S(1)} %mul.222, f32[2048]{0:T(1024)S(1)} %add_rsqrt_fusion.1, f32[2048]{0:T(1024)S(1)} %broadcast_multiply_fusion.5), kind=kOutput, calls=%fused_computation.73 | convolution fusion | flops 9673900032 | bytes 23615488 | tf_op jit(solution)/shard_map/dot_general | solution.py:382
  523.3 1.5 convolution_convert_fusion.6
  524.9 9.3 %copy.121 = bf16[32,64,12,64]{1,0,3,2:T(8,128)(2,1)} copy(bf16[32,64,12,64]{3,1,2,0:T(8,128)(2,1)} %get-tuple-element.103) | data formatting | bytes 6291456 | tf_op jit(solution)/shard_map/convert_element_type | solution.py:606
  534.2 10.0 %reshape.395 = bf16[2048,768]{0,1:T(8,128)(2,1)} reshape(bf16[32,64,12,64]{1,0,3,2:T(8,128)(2,1)} %copy.121) | data formatting | bytes 6291456 | tf_op jit(solution)/shard_map/reshape | solution.py:606
  544.2 6.7 convolution_convert_fusion.3
  550.9 3.7 fusion.52
  554.6 9.3 %copy.115 = bf16[32,64,12,64]{1,0,3,2:T(8,128)(2,1)} copy(bf16[32,64,12,64]{3,1,2,0:T(8,128)(2,1)} %get-tuple-element.101) | data formatting | bytes 6291456 | tf_op jit(solution)/shard_map/convert_element_type | solution.py:612
  563.9 9.9 %reshape.393 = bf16[2048,768]{0,1:T(8,128)(2,1)} reshape(bf16[32,64,12,64]{1,0,3,2:T(8,128)(2,1)} %copy.115) | data formatting | bytes 6291456 | tf_op jit(solution)/shard_map/reshape | solution.py:612
  573.8 6.5 convolution_convert_fusion.5
  580.3 14.5 %fusion.18 = bf16[32,64,12,64]{3,1,2,0:T(8,128)(2,1)} fusion(bf16[32,12,64,64]{2,3,1,0:T(8,128)(2,1)} %copy-done.19, bf16[32,64,12,64]{1,0,3,2:T(8,128)(2,1)} %reshape.374), kind=kOutput, calls=%fused_computation.37 | convolution fusion | flops 204472320 | bytes 9437184 | tf_op jit(solution)/shard_map/ghqk,gqhe->gkhe/dot_general | solution.py:613
  594.8 9.4 %copy.119 = bf16[32,64,12,64]{1,0,3,2:T(8,128)(2,1)} copy(bf16[32,64,12,64]{3,1,2,0:T(8,128)(2,1)} %fusion.18) | data formatting | bytes 6291456 | tf_op jit(solution)/shard_map/convert_element_type | solution.py:616
  604.2 9.9 %reshape.394 = bf16[2048,768]{0,1:T(8,128)(2,1)} reshape(bf16[32,64,12,64]{1,0,3,2:T(8,128)(2,1)} %copy.119) | data formatting | bytes 6291456 | tf_op jit(solution)/shard_map/reshape | solution.py:616
  614.2 6.5 convolution_convert_fusion.4
  620.7 90.3 %shard_map.359 = (f32[24,768]{1,0:T(8,128)}, f32[24,768]{1,0:T(8,128)}, f32[24,768]{1,0:T(8,128)}, f32[24,768]{1,0:T(8,128)}, f32[24,768]{1,0:T(8,128)}, /*index...) custom-call(bf16[2,2,2,4,24,768]{5,4,3,2,1,0:T(8,128)(2,1)} %bitcast.206, ...), custom_call_target="tpu_custom_call" | custom-call | tf_op jit(solution)/shard_map/pallas_call | solution.py:339
  711.0 1.6 fusion.86
  712.6 1.3 slice.79
  713.9 4.8 fusion.91
  718.8 2.8 fusion.92
  721.7 4.9 add_add_fusion
  (205 shorter events, 21.4 us)
Async XLA Ops:
  1.6 0.9 copy-start.2
  2.5 0.9 copy-start.3
  3.4 0.8 copy-start.4
  4.2 0.8 copy-start.5
  94.3 2.1 copy-start.9
  96.4 2.1 copy-start.10
  98.6 1.0 copy-start.13
  99.6 1.0 copy-start.15
  100.6 19.8 %copy-start.11 = (bf16[2,2,2,4,24,768]{5,4,3,2,1,0:T(8,128)(2,1)}, bf16[2,2,2,4,24,768]{5,4,3,2,1,0:T(8,128)(2,1)S(1)}, u32[]{:S(2)}) copy-start(bf16[2,2,2,4,24,768]{5,4,3,2,1,0:T(8,128)(2,1)S(1)} %get-tuple-element.38) | copy-start | bytes 3538948
  100.6 69.8 %copy-start = (bf16[2,2,2,4,24,768]{5,4,3,2,1,0:T(8,128)(2,1)}, bf16[2,2,2,4,24,768]{5,4,3,2,1,0:T(8,128)(2,1)S(1)}, u32[]{:S(2)}) copy-start(bf16[2,2,2,4,24,768]{5,4,3,2,1,0:T(8,128)(2,1)S(1)} %get-tuple-element.35) | copy-start | bytes 3538948
  136.5 9.3 %copy-start.57 = (s32[2,2,8]{2,1,0:T(2,128)S(1)}, s32[2,2,8]{2,1,0:T(2,128)}, u32[]{:S(2)}) copy-start(s32[2,2,8]{2,1,0:T(2,128)} %param.23) | copy-start | bytes 388
  145.9 50.2 %copy-start.38 = (pred[32,64]{1,0:T(8,128)(4,1)}, pred[32,64]{1,0:T(8,128)(4,1)S(1)}, u32[]{:S(2)}) copy-start(pred[32,64]{1,0:T(8,128)(4,1)S(1)} %iota_compare_fusion.1) | copy-start | bytes 6148
  163.4 6.9 copy-start.51
  170.3 25.9 %copy-start.25 = (f32[32,12,64]{2,1,0:T(8,128)}, f32[32,12,64]{2,1,0:T(8,128)S(1)}, u32[]{:S(2)}) copy-start(f32[32,12,64]{2,1,0:T(8,128)S(1)} %log_add_fusion) | copy-start | bytes 294916
  212.3 9.8 %copy-start.50 = (f32[32,24]{1,0:T(8,128)S(1)}, f32[32,24]{1,0:T(8,128)}, u32[]{:S(2)}) copy-start(f32[32,24]{1,0:T(8,128)} %get-tuple-element.71) | copy-start | bytes 9220
  212.3 9.9 %copy-start.16 = (bf16[2,2,2,4,24,768]{5,4,3,2,1,0:T(8,128)(2,1)S(1)}, bf16[2,2,2,4,24,768]{5,4,3,2,1,0:T(8,128)(2,1)}, u32[]{:S(2)}) copy-start(bf16[2,2,2,4,24,768]{5,4,3,2,1,0:T(8,128)(2,1)} %copy-done.15) | copy-start | bytes 3538948
  228.3 2.7 copy-start.22
  228.3 3.6 copy-start.49
  232.1 71.4 %copy-start.55 = (f32[768]{0:T(1024)}, f32[768]{0:T(1024)S(1)}, u32[]{:S(2)}) copy-start(f32[768]{0:T(1024)S(1)} %add.197) | copy-start | bytes 9220
  233.0 70.4 %copy-start.48 = (f32[32,24]{1,0:T(8,128)S(1)}, f32[32,24]{1,0:T(8,128)}, u32[]{:S(2)}) copy-start(f32[32,24]{1,0:T(8,128)} %get-tuple-element.68) | copy-start | bytes 9220
  319.5 2.6 copy-start.18
  319.5 3.5 copy-start.47
  319.5 3.6 copy-start.46
  323.0 5.4 copy-start.45
  323.2 31.8 %copy-start.53 = (s32[2,256]{1,0:T(2,128)S(1)}, s32[2,256]{1,0:T(2,128)}, u32[]{:S(2)}) copy-start(s32[2,256]{1,0:T(2,128)} %param.25) | copy-start | bytes 6148
  323.2 31.8 %copy-start.54 = (s32[2,256]{1,0:T(2,128)S(1)}, s32[2,256]{1,0:T(2,128)}, u32[]{:S(2)}) copy-start(s32[2,256]{1,0:T(2,128)} %param.24) | copy-start | bytes 6148
  323.2 32.8 %copy-start.52 = (s32[2,512]{1,0:T(2,128)S(1)}, s32[2,512]{1,0:T(2,128)}, u32[]{:S(2)}) copy-start(s32[2,512]{1,0:T(2,128)} %constant.114.clone.1) | copy-start | bytes 12292
  326.7 1.7 copy-start.27
  328.4 26.5 %copy-start.34 = (bf16[32,1,768]{2,1,0:T(2,128)(2,1)}, bf16[32,1,768]{2,1,0:T(2,128)(2,1)S(1)}, u32[]{:S(2)}) copy-start(bf16[32,1,768]{2,1,0:T(2,128)(2,1)S(1)} %slice.93) | copy-start | bytes 147460
  357.9 1.4 copy-start.30
  360.1 3.1 copy-start.20
  362.7 7.8 %copy-start.32 = (bf16[32,768]{1,0:T(8,128)(2,1)}, bf16[32,768]{1,0:T(8,128)(2,1)S(1)}, u32[]{:S(2)}) copy-start(bf16[32,768]{1,0:T(8,128)(2,1)S(1)} %get-tuple-element.60) | copy-start | bytes 147460
  365.1 11.5 %slice-start.2 = ((s8[4718592]{0:T(1024)(128)(4,1)}), s8[4194304]{0:T(1024)(128)(4,1)S(1)}, s32[]{:S(2)}) async-start(s8[4718592]{0:T(1024)(128)(4,1)} %bitcast.180), calls=%async_computation.2 | async-start | bytes 8388608
  370.6 6.0 slice-start.3
  370.6 29.5 %slice-start = ((s8[4718592]{0:T(1024)(128)(4,1)}), s8[4194304]{0:T(1024)(128)(4,1)S(1)}, s32[]{:S(2)}) async-start(s8[4718592]{0:T(1024)(128)(4,1)} %bitcast.176), calls=%async_computation | async-start | bytes 8388608
  376.6 23.5 %copy-start.24 = (f32[2048,768]{1,0:T(8,128)}, f32[2048,768]{1,0:T(8,128)S(1)}, u32[]{:S(2)}) copy-start(f32[2048,768]{1,0:T(8,128)S(1)} %get-tuple-element.62) | copy-start | bytes 18874372
  376.6 23.5 %slice-start.1 = ((s8[4718592]{0:T(1024)(128)(4,1)}), s8[524288]{0:T(1024)(128)(4,1)S(1)}, s32[]{:S(2)}) async-start(s8[4718592]{0:T(1024)(128)(4,1)} %bitcast.176), calls=%async_computation.1 | async-start | bytes 1048576
  418.1 8.7 %copy-start.17 = (bf16[2,2,2,4,24,768]{5,4,3,2,1,0:T(8,128)(2,1)S(1)}, bf16[2,2,2,4,24,768]{5,4,3,2,1,0:T(8,128)(2,1)}, u32[]{:S(2)}) copy-start(bf16[2,2,2,4,24,768]{5,4,3,2,1,0:T(8,128)(2,1)} %copy-done.15) | copy-start | bytes 3538948
  424.2 2.6 copy-start.21
  431.0 10.6 %copy-start.26 = (f32[32,12,64]{2,1,0:T(8,128)S(1)}, f32[32,12,64]{2,1,0:T(8,128)}, u32[]{:S(2)}) copy-start(f32[32,12,64]{2,1,0:T(8,128)} %copy-done.25) | copy-start | bytes 294916
  431.0 10.6 %copy-start.39 = (pred[32,64]{1,0:T(8,128)(4,1)S(1)}, pred[32,64]{1,0:T(8,128)(4,1)}, u32[]{:S(2)}) copy-start(pred[32,64]{1,0:T(8,128)(4,1)} %copy-done.38) | copy-start | bytes 6148
  479.5 9.1 %copy-start.19 = (bf16[32,12,64,64]{2,3,1,0:T(8,128)(2,1)}, bf16[32,12,64,64]{2,3,1,0:T(8,128)(2,1)S(1)}, u32[]{:S(2)}) copy-start(bf16[32,12,64,64]{2,3,1,0:T(8,128)(2,1)S(1)} %multiply_convert_fusion.2) | copy-start | bytes 9437188
  479.5 27.6 %slice-start.8 = ((s8[6291456]{0:T(1024)(128)(4,1)}), s8[2097152]{0:T(1024)(128)(4,1)S(1)}, s32[]{:S(2)}) async-start(s8[6291456]{0:T(1024)(128)(4,1)} %bitcast.193), calls=%async_computation.8 | async-start | bytes 4194304
  490.2 17.0 %slice-start.9 = ((s8[6291456]{0:T(1024)(128)(4,1)}), s8[4194304]{0:T(1024)(128)(4,1)S(1)}, s32[]{:S(2)}) async-start(s8[6291456]{0:T(1024)(128)(4,1)} %bitcast.193), calls=%async_computation.9 | async-start | bytes 8388608
  490.2 17.0 %copy-start.56 = (f32[768]{0:T(1024)S(1)}, f32[768]{0:T(1024)}, u32[]{:S(2)}) copy-start(f32[768]{0:T(1024)} %copy-done.55) | copy-start | bytes 9220
  507.1 16.2 %copy-start.33 = (bf16[32,768]{1,0:T(8,128)(2,1)S(1)}, bf16[32,768]{1,0:T(8,128)(2,1)}, u32[]{:S(2)}) copy-start(bf16[32,768]{1,0:T(8,128)(2,1)} %copy-done.32) | copy-start | bytes 147460
  507.2 16.2 %copy-start.35 = (bf16[32,1,768]{2,1,0:T(2,128)(2,1)S(1)}, bf16[32,1,768]{2,1,0:T(2,128)(2,1)}, u32[]{:S(2)}) copy-start(bf16[32,1,768]{2,1,0:T(2,128)(2,1)} %copy-done.34) | copy-start | bytes 147460
  534.2 16.7 %slice-start.4 = ((s8[6291456]{0:T(1024)(128)(4,1)}), s8[2097152]{0:T(1024)(128)(4,1)S(1)}, s32[]{:S(2)}) async-start(s8[6291456]{0:T(1024)(128)(4,1)} %bitcast.189), calls=%async_computation.4 | async-start | bytes 4194304
  544.2 6.7 slice-start.5
  544.2 6.7 copy-start.28
  620.7 93.2 %copy-start.14 = (bf16[2,2,2,4,24,768]{5,4,3,2,1,0:T(8,128)(2,1)S(1)}, bf16[2,2,2,4,24,768]{5,4,3,2,1,0:T(8,128)(2,1)}, u32[]{:S(2)}) copy-start(bf16[2,2,2,4,24,768]{5,4,3,2,1,0:T(8,128)(2,1)} %copy-done.13) | copy-start | bytes 3538948
  713.9 4.8 copy-start.12
  713.9 4.8 copy-start.29
  713.9 7.6 %slice-start.6 = ((s8[6291456]{0:T(1024)(128)(4,1)}), s8[4194304]{0:T(1024)(128)(4,1)S(1)}, s32[]{:S(2)}) async-start(s8[6291456]{0:T(1024)(128)(4,1)} %bitcast.191), calls=%async_computation.6 | async-start | bytes 8388608
  718.7 2.8 copy-start.1
  718.7 2.8 slice-start.7
  718.7 2.9 copy-start.23
  721.6 4.9 copy-start.44
  721.6 5.6 copy-start.43
  721.6 6.2 copy-start.42
  721.6 6.8 copy-start.41
  721.6 7.5 %copy-start.37 = (f32[24,3072]{1,0:T(8,128)S(1)}, f32[24,3072]{1,0:T(8,128)}, u32[]{:S(2)}) copy-start(f32[24,3072]{1,0:T(8,128)} %get-tuple-element.142) | copy-start | bytes 884740
  721.6 8.2 %copy-start.36 = (f32[96,768]{1,0:T(8,128)S(1)}, f32[96,768]{1,0:T(8,128)}, u32[]{:S(2)}) copy-start(f32[96,768]{1,0:T(8,128)} %get-tuple-element.144) | copy-start | bytes 884740
  721.7 8.9 %copy-start.40 = (f32[24,768]{1,0:T(8,128)S(1)}, f32[24,768]{1,0:T(8,128)}, u32[]{:S(2)}) copy-start(f32[24,768]{1,0:T(8,128)} %get-tuple-element.148) | copy-start | bytes 221188
  (4 other events, 3.0 us)

commit v2 on v1

--- a/solution.py
+++ b/solution.py
@@ -390,36 +390,544 @@
     )
 
 
-def norm_forward(row_data, gain_vec, shift_vec):
-    centred = row_data - jnp.mean(row_data, -1, keepdims=True)
-    inverse = lax.rsqrt(jnp.mean(centred * centred, -1, keepdims=True) + LN_EPS)
-    normed = centred * inverse
-    return (normed * gain_vec + shift_vec, normed, inverse)
+def row_mean(value):
+    return jnp.sum(value, -1, keepdims=True) * (1.0 / value.shape[-1])
+
+
+def norm_parts(row_data):
+    centred = row_data - row_mean(row_data)
+    inverse = lax.rsqrt(row_mean(centred * centred) + LN_EPS)
+    return centred * inverse, inverse
 
 
 def norm_backward(upstream, normed, inverse, gain_vec):
     scaled = upstream * gain_vec
-    back = inverse * (
-        scaled
-        - jnp.mean(scaled, -1, keepdims=True)
-        - normed * jnp.mean(scaled * normed, -1, keepdims=True)
-    )
-    return (back, jnp.sum(upstream * normed, 0), jnp.sum(upstream, 0))
-
-
-def gelu_slope(inner_act):
-    return (
-        0.5 * (1.0 + lax.erf(inner_act * 0.7071067811865476))
-        + inner_act * jnp.exp(-0.5 * inner_act * inner_act) * 0.3989422804014327
-    )
-
-
-def attention_scores(queries, key_rows, sent_lengths):
-    seq_len = queries.shape[1]
-    scores = jnp.einsum("gqhe,gkhe->ghqk", queries, key_rows, preferred_element_type=jnp.float32)
-    scores = scores * queries.shape[3] ** (-0.5)
-    key_valid = jnp.arange(seq_len)[None, :] < sent_lengths[:, None]
-    return jnp.where(key_valid[:, None, None, :], scores, MASKED)
+    return inverse * (scaled - row_mean(scaled) - normed * row_mean(scaled * normed))
+
+
+def column_sum(value):
+    return jnp.sum(value, 0, keepdims=True)
+
+
+def gelu_and_slope(inner_act):
+    below = 0.5 * (1.0 + lax.erf(inner_act * 0.7071067811865476))
+    bell = jnp.exp(-0.5 * inner_act * inner_act) * 0.3989422804014327
+    return inner_act * below, below + inner_act * bell
+
+
+GROUP = 4
+SPAN = GROUP * HEAD_DIM
+
+
+def spread(rows, diag):
+    return jnp.concatenate([rows] * GROUP, 0) * diag
+
+
+def fold(square, seq_len):
+    lane = lax.broadcasted_iota(jnp.int32, (seq_len, square.shape[1]), 1)
+    out = square[:seq_len]
+    for head in range(1, GROUP):
+        block = square[head * seq_len : (head + 1) * seq_len]
+        out = jnp.where(lane >= head * HEAD_DIM, block, out)
+    return out
+
+
+def probabilities(keys, wide_queries, length):
+    scores = dot_right_t(keys, wide_queries) * HEAD_DIM ** (-0.5)
+    at = lax.broadcasted_iota(jnp.int32, scores.shape, 0)
+    scores = jnp.where(at < length, scores, MASKED)
+    raised = jnp.exp(scores - jnp.max(scores, 0, keepdims=True))
+    return raised * (1.0 / jnp.sum(raised, 0, keepdims=True))
+
+
+def attend_kernel(
+    seq_len,
+    lengths_ref,
+    x_ref,
+    query_w,
+    key_w,
+    value_w,
+    proj_w,
+    vec_ref,
+    diag_ref,
+    q_ref,
+    k_ref,
+    v_ref,
+    mix_ref,
+    sum_ref,
+    cls_ref,
+):
+    rows, width = x_ref.shape
+    held = rows // seq_len
+    first = pl.program_id(0) * held
+    x = x_ref[...]
+    q_ref[...] = (dot_plain(x, query_w[...]) + vec_ref[0:1, :]).astype(jnp.bfloat16)
+    k_ref[...] = dot_plain(x, key_w[...]).astype(jnp.bfloat16)
+    v_ref[...] = (dot_plain(x, value_w[...]) + vec_ref[1:2, :]).astype(jnp.bfloat16)
+    diag = diag_ref[...]
+
+    def sentence(at):
+        length = lengths_ref[first + at]
+        here = pl.ds(pl.multiple_of(at * seq_len, seq_len), seq_len)
+        for low in range(0, width, SPAN):
+            cols = pl.ds(low, SPAN)
+            wide = spread(q_ref[here, cols], diag)
+            probs = probabilities(k_ref[here, cols], wide, length).astype(jnp.bfloat16)
+            mixed = fold(dot_left_t(probs, v_ref[here, cols]), seq_len)
+            mix_ref[here, cols] = mixed.astype(jnp.bfloat16)
+
+    pl.loop(0, held)(sentence)
+    total = x.astype(jnp.float32) + dot_plain(mix_ref[...], proj_w[...]) + vec_ref[2:3, :]
+    sum_ref[...] = total
+    for at in range(held):
+        cls_ref[0, at : at + 1, :] = total[at * seq_len : at * seq_len + 1]
+
+
+def whole(shape):
+    return pl.BlockSpec(shape, lambda *_: (0,) * len(shape), pipeline_mode=pl.Buffered(1))
+
+
+def attend(x, lengths, weights, vec, diag, seq_len, rows):
+    total, width = x.shape
+    steps = total // rows
+    held = rows // seq_len
+    block = pl.BlockSpec((rows, width), lambda i: (i, 0))
+    narrow = jax.ShapeDtypeStruct((total, width), jnp.bfloat16)
+    return pl.pallas_call(
+        functools.partial(attend_kernel, seq_len),
+        grid=(steps,),
+        out_shape=[
+            narrow,
+            narrow,
+            narrow,
+            narrow,
+            jax.ShapeDtypeStruct((total, width), jnp.float32),
+            jax.ShapeDtypeStruct((steps, held, width), jnp.float32),
+        ],
+        in_specs=[pl.BlockSpec(memory_space=pltpu.SMEM), block]
+        + [whole(w.shape) for w in weights]
+        + [whole(vec.shape), whole(diag.shape)],
+        out_specs=[block] * 5 + [pl.BlockSpec((1, held, width), lambda i: (i, 0, 0))],
+        compiler_params=pltpu.CompilerParams(vmem_limit_bytes=60 * MIB),
+    )(lengths, x, *weights, vec, diag)
+
+
+def feed_kernel(
+    seq_len,
+    blocks,
+    pieces,
+    sum_ref,
+    tok_ref,
+    cls_ref,
+    inner_w,
+    outer_w,
+    vec_ref,
+    bias_ref,
+    out_ref,
+    back_ref,
+    inner_grad,
+    outer_grad,
+    vec_grad,
+    bias_grad,
+    slope,
+    active,
+    inner_b,
+    hidden_b,
+    second_b,
+):
+    step = pl.program_id(0)
+    rows, width = sum_ref.shape
+    piece = active.shape[2]
+
+    @pl.when(step == 0)
+    def _():
+        vec_grad[...] = jnp.zeros_like(vec_grad)
+        bias_grad[...] = jnp.zeros_like(bias_grad)
+
+    @pl.when(step < blocks)
+    def _():
+        here = pl.ds(pl.multiple_of(step * rows, rows), rows)
+        gain_one, shift_one = vec_ref[3:4, :], vec_ref[4:5, :]
+        gain_two, shift_two = vec_ref[6:7, :], vec_ref[7:8, :]
+        normed_one, inverse_one = norm_parts(sum_ref[...])
+        hidden = normed_one * gain_one + shift_one
+        narrow = hidden.astype(jnp.bfloat16)
+        hidden_b[here, :] = narrow
+        second_sum = hidden + vec_ref[5:6, :]
+        for at in range(pieces):
+            cols = slice(at * piece, (at + 1) * piece)
+            value, steep = gelu_and_slope(dot_plain(narrow, inner_w[:, cols]) + bias_ref[:, cols])
+            value = value.astype(jnp.bfloat16)
+            slope[at] = steep
+            active[at, here, :] = value
+            second_sum = second_sum + dot_plain(value, outer_w[cols, :])
+        normed_two, inverse_two = norm_parts(second_sum)
+        out_ref[...] = (normed_two * gain_two + shift_two).astype(jnp.bfloat16)
+        grad = tok_ref[...].astype(jnp.float32).reshape(rows // seq_len, seq_len, width)
+        place = lax.broadcasted_iota(jnp.int32, grad.shape, 1)
+        extra = cls_ref[...].reshape(rows // seq_len, 1, width)
+        grad = (grad + jnp.where(place == 0, extra, 0.0)).reshape(rows, width)
+        vec_grad[6:7, :] += column_sum(grad * normed_two)
+        vec_grad[7:8, :] += column_sum(grad)
+        second = norm_backward(grad, normed_two, inverse_two, gain_two)
+        vec_grad[5:6, :] += column_sum(second)
+        narrow_two = second.astype(jnp.bfloat16)
+        second_b[here, :] = narrow_two
+        hidden_grad = second
+        for at in range(pieces):
+            cols = slice(at * piece, (at + 1) * piece)
+            inner = dot_right_t(narrow_two, outer_w[cols, :]) * slope[at]
+            bias_grad[:, cols] += column_sum(inner)
+            inner = inner.astype(jnp.bfloat16)
+            inner_b[at, here, :] = inner
+            hidden_grad = hidden_grad + dot_right_t(inner, inner_w[:, cols])
+        vec_grad[3:4, :] += column_sum(hidden_grad * normed_one)
+        vec_grad[4:5, :] += column_sum(hidden_grad)
+        first = norm_backward(hidden_grad, normed_one, inverse_one, gain_one)
+        vec_grad[2:3, :] += column_sum(first)
+        back_ref[...] = first
+
+    @pl.when(step >= blocks)
+    def _():
+        at = step - blocks
+        outer_grad[...] = dot_left_t(active[at], second_b[...]).astype(jnp.bfloat16)
+        inner_grad[...] = dot_left_t(hidden_b[...], inner_b[at]).astype(jnp.bfloat16)
+
+
+def feed(first_sum, tokens_grad, cls_grad, inner_w, outer_w, vec, bias, seq_len, rows, piece):
+    total, width = first_sum.shape
+    wide = inner_w.shape[1]
+    blocks, pieces = total // rows, wide // piece
+    held = rows // seq_len
+    cls_grad = cls_grad.reshape(blocks, held, width)
+    block = pl.BlockSpec((rows, width), lambda i: (jnp.minimum(i, blocks - 1), 0))
+    return pl.pallas_call(
+        functools.partial(feed_kernel, seq_len, blocks, pieces),
+        grid=(blocks + pieces,),
+        out_shape=[
+            jax.ShapeDtypeStruct((total, width), jnp.bfloat16),
+            jax.ShapeDtypeStruct((total, width), jnp.float32),
+            jax.ShapeDtypeStruct(inner_w.shape, jnp.bfloat16),
+            jax.ShapeDtypeStruct(outer_w.shape, jnp.bfloat16),
+            jax.ShapeDtypeStruct((8, width), jnp.float32),
+            jax.ShapeDtypeStruct((1, wide), jnp.float32),
+        ],
+        in_specs=[
+            block,
+            block,
+            pl.BlockSpec((1, held, width), lambda i: (jnp.minimum(i, blocks - 1), 0, 0)),
+            whole(inner_w.shape),
+            whole(outer_w.shape),
+            whole(vec.shape),
+            whole(bias.shape),
+        ],
+        out_specs=[
+            block,
+            block,
+            pl.BlockSpec((width, piece), lambda i: (0, jnp.maximum(i - blocks, 0))),
+            pl.BlockSpec((piece, width), lambda i: (jnp.maximum(i - blocks, 0), 0)),
+            pl.BlockSpec((8, width), lambda i: (0, 0)),
+            pl.BlockSpec((1, wide), lambda i: (0, 0)),
+        ],
+        scratch_shapes=[
+            pltpu.VMEM((pieces, rows, piece), jnp.float32),
+            pltpu.VMEM((pieces, total, piece), jnp.bfloat16),
+            pltpu.VMEM((pieces, total, piece), jnp.bfloat16),
+            pltpu.VMEM((total, width), jnp.bfloat16),
+            pltpu.VMEM((total, width), jnp.bfloat16),
+        ],
+        compiler_params=pltpu.CompilerParams(vmem_limit_bytes=62 * MIB),
+    )(first_sum, tokens_grad, cls_grad, inner_w, outer_w, vec, bias)
+
+
+def back_kernel(
+    seq_len,
+    blocks,
+    lengths_ref,
+    x_ref,
+    q_ref,
+    k_ref,
+    v_ref,
+    mix_ref,
+    first_ref,
+    query_w,
+    key_w,
+    value_w,
+    proj_w,
+    diag_ref,
+    in_ref,
+    query_g,
+    key_g,
+    value_g,
+    proj_g,
+    vec_grad,
+    x_all,
+    mix_all,
+    first_all,
+    dq_all,
+    dk_all,
+    dv_all,
+    dmix,
+):
+    step = pl.program_id(0)
+    rows, width = x_ref.shape
+    held = rows // seq_len
+    scale = HEAD_DIM ** (-0.5)
+
+    @pl.when(step == 0)
+    def _():
+        vec_grad[...] = jnp.zeros_like(vec_grad)
+
+    @pl.when(step < blocks)
+    def _():
+        here = pl.ds(pl.multiple_of(step * rows, rows), rows)
+        first = first_ref[...]
+        narrow = first.astype(jnp.bfloat16)
+        first_all[here, :] = narrow
+        x_all[here, :] = x_ref[...]
+        mix_all[here, :] = mix_ref[...]
+        dmix[...] = dot_right_t(narrow, proj_w[...]).astype(jnp.bfloat16)
+        diag = diag_ref[...]
+
+        def sentence(at):
+            length = lengths_ref[step * held + at]
+            near = pl.ds(pl.multiple_of(at * seq_len, seq_len), seq_len)
+            far = pl.ds(pl.multiple_of(step * rows + at * seq_len, seq_len), seq_len)
+            for low in range(0, width, SPAN):
+                cols = pl.ds(low, SPAN)
+                keys = k_ref[near, cols]
+                wide = spread(q_ref[near, cols], diag)
+                wide_grad = spread(dmix[near, cols], diag)
+                probs = probabilities(keys, wide, length)
+                prob_grad = dot_right_t(v_ref[near, cols], wide_grad)
+                dv_all[far, cols] = dot_plain(probs.astype(jnp.bfloat16), wide_grad).astype(
+                    jnp.bfloat16
+                )
+                score_grad = probs * (prob_grad - column_sum(prob_grad * probs))
+                score_grad = score_grad.astype(jnp.bfloat16)
+                dk_all[far, cols] = (dot_plain(score_grad, wide) * scale).astype(jnp.bfloat16)
+                dq_all[far, cols] = (fold(dot_left_t(score_grad, keys), seq_len) * scale).astype(
+                    jnp.bfloat16
+                )
+
+        pl.loop(0, held)(sentence)
+        dq, dk, dv = dq_all[here, :], dk_all[here, :], dv_all[here, :]
+        vec_grad[0:1, :] += column_sum(dq.astype(jnp.float32))
+        vec_grad[1:2, :] += column_sum(dv.astype(jnp.float32))
+        in_ref[...] = (
+            first
+            + dot_right_t(dq, query_w[...])
+            + dot_right_t(dk, key_w[...])
+            + dot_right_t(dv, value_w[...])
+        )
+
+    for at, (left, right, target) in enumerate(
+        (
+            (mix_all, first_all, proj_g),
+            (x_all, dq_all, query_g),
+            (x_all, dk_all, key_g),
+            (x_all, dv_all, value_g),
+        )
+    ):
+
+        @pl.when(step == blocks + at)
+        def _():
+            target[...] = dot_left_t(left[...], right[...]).astype(jnp.bfloat16)
+
+
+def back(x, lengths, saved, first_grad, weights, diag, seq_len, rows):
+    total, width = x.shape
+    blocks = total // rows
+    block = pl.BlockSpec((rows, width), lambda i: (jnp.minimum(i, blocks - 1), 0))
+    square = jax.ShapeDtypeStruct((width, width), jnp.bfloat16)
+    return pl.pallas_call(
+        functools.partial(back_kernel, seq_len, blocks),
+        grid=(blocks + 4,),
+        out_shape=[jax.ShapeDtypeStruct((total, width), jnp.float32)]
+        + [square] * 4
+        + [jax.ShapeDtypeStruct((8, width), jnp.float32)],
+        in_specs=[pl.BlockSpec(memory_space=pltpu.SMEM)]
+        + [block] * 6
+        + [whole(w.shape) for w in weights]
+        + [whole(diag.shape)],
+        out_specs=[block]
+        + [pl.BlockSpec((width, width), lambda i: (0, 0))] * 4
+        + [pl.BlockSpec((8, width), lambda i: (0, 0))],
+        scratch_shapes=[pltpu.VMEM((total, width), jnp.bfloat16)] * 6
+        + [pltpu.VMEM((rows, width), jnp.bfloat16)],
+        compiler_params=pltpu.CompilerParams(vmem_limit_bytes=60 * MIB),
+    )(lengths, x, *saved, first_grad, *weights, diag)
+
+
+def rank_kernel(
+    layout,
+    micros,
+    node_dev,
+    steps,
+    sum_ref,
+    inner_w,
+    outer_w,
+    pool_w,
+    vec_ref,
+    bias_ref,
+    node_ref,
+    cls_grad,
+    pool_grad,
+    shift_grad,
+    hidden,
+    total,
+    mine,
+    units,
+    node_cols,
+    totals,
+    send_sems,
+    recv_sems,
+    local_sem,
+):
+    step = pl.program_id(0)
+    sentences, width = sum_ref.shape
+    own = layout.own()
+
+    @pl.when(step == 0)
+    def _():
+        layout.greet(own)
+        normed, _ = norm_parts(sum_ref[...])
+        start = normed * vec_ref[3:4, :] + vec_ref[4:5, :]
+        hidden[...] = start.astype(jnp.bfloat16)
+        total[...] = start + vec_ref[5:6, :]
+        node_cols[...] = node_ref[...].T
+
+    value, _ = gelu_and_slope(dot_plain(hidden[...], inner_w[...]) + bias_ref[...])
+    total[...] += dot_plain(value.astype(jnp.bfloat16), outer_w[...])
+
+    @pl.when(step == steps - 1)
+    def _():
+        normed, _ = norm_parts(total[...])
+        cls_rows = (normed * vec_ref[6:7, :] + vec_ref[7:8, :]).astype(jnp.bfloat16)
+        pooled = jnp.tanh(dot_plain(cls_rows, pool_w[...]) + vec_ref[8:9, :])
+        scale_inv = lax.rsqrt(jnp.sum(pooled * pooled, -1, keepdims=True) + UNIT_EPS)
+        unit = pooled * scale_inv
+        mine[...] = unit.astype(jnp.bfloat16)
+        job = GatherJob(
+            layout, own, layout.orders[0], mine, units, (send_sems, recv_sems, local_sem)
+        )
+        for stage in range(len(layout.dims) + 1):
+            job.advance(stage)
+        job.finish()
+
+        device = own[0]
+        for size, digit in zip(layout.dims[1:], own[1:]):
+            device = device * size + digit
+        at_home = pl.ds(pl.multiple_of(device * node_dev, node_dev), node_dev)
+        count = layout.count * node_dev
+        band = min(count, 512)
+        every = units[...].reshape(layout.count, sentences, width)
+        grads = []
+
+        def scored(similar, tongue, place, side, tongue_row, place_row, side_row):
+            across = side != side_row
+            include = across & (tongue == tongue_row)
+            positive = jnp.where(across & (place == place_row), 1.0, 0.0)
+            return (
+                jnp.where(include, SIM_SCALE * similar - SIM_SCALE * MARGIN * positive, MASKED),
+                include,
+                positive,
+            )
+
+        half = node_dev // 2
+
+        def sides(shape, dim, offset):
+            return (lax.broadcasted_iota(jnp.int32, shape, dim) + offset) // half % 2
+
+        for micro in range(micros):
+            here = slice(micro * node_dev, (micro + 1) * node_dev)
+            nodes = every[:, here, :].reshape(count, width)
+            tongue, place = node_cols[:, 2 * micro : 2 * micro + 1], node_cols[
+                :, 2 * micro + 1 : 2 * micro + 2
+            ]
+            for low in range(0, count, band):
+                cols = slice(low, low + band)
+                similar = dot_right_t(nodes, nodes[cols])
+                value, _, _ = scored(
+                    similar,
+                    tongue,
+                    place,
+                    sides((count, 1), 0, 0),
+                    node_ref[2 * micro : 2 * micro + 1, cols],
+                    node_ref[2 * micro + 1 : 2 * micro + 2, cols],
+                    sides((1, band), 1, low),
+                )
+                peak = jnp.max(value, 0, keepdims=True)
+                totals[:, cols] = jnp.log(column_sum(jnp.exp(value - peak))) + peak
+            value, include, positive = scored(
+                dot_right_t(mine[here, :], nodes),
+                node_cols[at_home, 2 * micro : 2 * micro + 1],
+                node_cols[at_home, 2 * micro + 1 : 2 * micro + 2],
+                sides((node_dev, 1), 0, 0),
+                node_ref[2 * micro : 2 * micro + 1, :],
+                node_ref[2 * micro + 1 : 2 * micro + 2, :],
+                sides((1, count), 1, 0),
+            )
+            peak = jnp.max(value, -1, keepdims=True)
+            line = jnp.log(jnp.sum(jnp.exp(value - peak), -1, keepdims=True)) + peak
+            grad_sim = jnp.where(
+                include, jnp.exp(value - line) + jnp.exp(value - totals[...]), 0.0
+            )
+            grad_sim = (grad_sim - 2.0 * positive).astype(jnp.bfloat16)
+            grads.append(SIM_SCALE * dot_plain(grad_sim, nodes))
+        unit_grad = jnp.concatenate(grads, 0)
+        pooled_grad = scale_inv * (
+            unit_grad - unit * jnp.sum(unit_grad * unit, -1, keepdims=True)
+        )
+        pre_grad = pooled_grad * (1.0 - pooled * pooled)
+        narrow = pre_grad.astype(jnp.bfloat16)
+        pool_grad[...] = dot_left_t(cls_rows, narrow).astype(jnp.bfloat16)
+        shift_grad[...] = column_sum(pre_grad)
+        cls_grad[...] = dot_right_t(narrow, pool_w[...])
+
+
+def rank(layout, cls_sum, inner_w, outer_w, pool_w, vec, bias, nodes, micros, piece, collective_id):
+    sentences, width = cls_sum.shape
+    wide = inner_w.shape[1]
+    steps = wide // piece
+    node_dev = sentences // micros
+    return pl.pallas_call(
+        functools.partial(rank_kernel, layout, micros, node_dev, steps),
+        grid=(steps,),
+        out_shape=[
+            jax.ShapeDtypeStruct((sentences, width), jnp.float32),
+            jax.ShapeDtypeStruct((width, width), jnp.bfloat16),
+            jax.ShapeDtypeStruct((1, width), jnp.float32),
+        ],
+        in_specs=[
+            whole(cls_sum.shape),
+            pl.BlockSpec((width, piece), lambda i: (0, i)),
+            pl.BlockSpec((piece, width), lambda i: (i, 0)),
+            whole(pool_w.shape),
+            whole(vec.shape),
+            pl.BlockSpec((1, piece), lambda i: (0, i)),
+            whole(nodes.shape),
+        ],
+        out_specs=[
+            pl.BlockSpec((sentences, width), lambda i: (0, 0)),
+            pl.BlockSpec((width, width), lambda i: (0, 0)),
+            pl.BlockSpec((1, width), lambda i: (0, 0)),
+        ],
+        scratch_shapes=[
+            pltpu.VMEM((sentences, width), jnp.bfloat16),
+            pltpu.VMEM((sentences, width), jnp.float32),
+            pltpu.VMEM((sentences, width), jnp.bfloat16),
+            pltpu.VMEM(layout.dims + (sentences, width), jnp.bfloat16),
+            pltpu.VMEM((nodes.shape[1], nodes.shape[0]), jnp.float32),
+            pltpu.VMEM((1, nodes.shape[1]), jnp.float32),
+            pltpu.SemaphoreType.DMA((layout.sends,)),
+            pltpu.SemaphoreType.DMA((layout.sends,)),
+            pltpu.SemaphoreType.DMA,
+        ],
+        compiler_params=pltpu.CompilerParams(
+            collective_id=collective_id, has_side_effects=True, vmem_limit_bytes=60 * MIB
+        ),
+    )(cls_sum, inner_w, outer_w, pool_w, vec, bias, nodes)
 
 
 def on_device(
@@ -453,10 +961,7 @@
     node_dev = sides * pair_dev
     sent_count = micro_count * node_dev
     row_count = sent_count * seq_len
-    head_shape = (sent_count, seq_len, model_width // HEAD_DIM, HEAD_DIM)
-    head_scale = HEAD_DIM ** (-0.5)
     pair_count = partner.shape[1]
-    device = lax.axis_index("dp") * (count // layout.slow) + lax.axis_index("fsdp")
 
     vectors = (
         query_bias,
@@ -489,161 +994,73 @@
         for full, array in zip(gathered, arrays)
     ]
     small_rows = small_full.reshape(count, -1)
-    wide = []
-    at = 0
-    for v in vectors:
-        wide.append(small_rows[:, at : at + v.shape[0]].reshape(-1))
-        at += v.shape[0]
-    (
-        query_shift,
-        value_shift,
-        proj_shift,
-        gain_first,
-        shift_first,
-        outer_shift,
-        gain_second,
-        shift_second,
-        pool_shift,
-        inner_shift,
-    ) = wide
-
-    tokens = hidden_in.reshape(row_count, model_width)
-    sent_lengths = lengths.reshape(sent_count)
-    queries = (dot_plain(tokens, query_full) + query_shift).astype(jnp.bfloat16)
-    queries = queries.reshape(head_shape)
-    key_rows = dot_plain(tokens, key_full).astype(jnp.bfloat16).reshape(head_shape)
-    values = (dot_plain(tokens, value_full) + value_shift).astype(jnp.bfloat16)
-    values = values.reshape(head_shape)
-    scores = attention_scores(queries, key_rows, sent_lengths)
-    peak = jnp.max(scores, -1, keepdims=True)
-    log_totals = jnp.log(jnp.sum(jnp.exp(scores - peak), -1, keepdims=True)) + peak
-    probs_b = jnp.exp(scores - log_totals).astype(jnp.bfloat16)
-    mixture = jnp.einsum("ghqk,gkhe->gqhe", probs_b, values, preferred_element_type=jnp.float32)
-    mixture = mixture.reshape(row_count, model_width).astype(jnp.bfloat16)
-    first_sum = tokens.astype(jnp.float32) + dot_plain(mixture, proj_full) + proj_shift
-    hidden, normed_one, inverse_one = norm_forward(first_sum, gain_first, shift_first)
-    hidden_b = hidden.astype(jnp.bfloat16)
-    inner_act = dot_plain(hidden_b, inner_full) + inner_shift
-    active = jax.nn.gelu(inner_act, approximate=False).astype(jnp.bfloat16)
-    second_sum = hidden + dot_plain(active, outer_full) + outer_shift
-    output, normed_two, inverse_two = norm_forward(second_sum, gain_second, shift_second)
-    block_out = output.astype(jnp.bfloat16).reshape(hidden_in.shape)
-
-    cls_rows = output.reshape(sent_count, seq_len, model_width)[:, 0].astype(jnp.bfloat16)
-    pooled = jnp.tanh(dot_plain(cls_rows, pool_full) + pool_shift)
-    scale_inv = lax.rsqrt(jnp.sum(pooled * pooled, -1, keepdims=True) + UNIT_EPS)
-    unit_vec = pooled * scale_inv
-    unit_b = unit_vec.astype(jnp.bfloat16)
-    (units,) = gather_all(layout, [unit_b], ((0, 0, None),), 1)
-    units = units.reshape(count, micro_count, node_dev, model_width)
-    units = jnp.moveaxis(units, 1, 0).reshape(micro_count, count * node_dev, model_width)
+    share = query_bias.shape[0]
+    rows_of = len(vectors) - 1
+    vec = small_rows[:, : rows_of * share].reshape(count, rows_of, share)
+    vec = jnp.moveaxis(vec, 1, 0).reshape(rows_of, model_width)
+    vec = jnp.pad(vec, ((0, 16 - rows_of), (0, 0)))
+    bias = small_rows[:, rows_of * share : rows_of * share + in_bias.shape[0]]
+    bias = bias.reshape(1, inner_width)
+
     pair_ids = jnp.arange(pair_count, dtype=jnp.int32)
     hit = partner[:, :, None] == pair_ids[None, None, :]
     target_language = jnp.sum(jnp.where(hit, language[:, :, None], 0), 1)
 
-    def nodes(first, second):
-        shape = (micro_count, count, 1, pair_dev)
-        joined = jnp.concatenate([first.reshape(shape), second.reshape(shape)], 2)
-        return joined.reshape(micro_count, count * node_dev)
-
-    tongue = nodes(language, target_language)
-    place = nodes(partner, jnp.broadcast_to(pair_ids, partner.shape))
-    side = nodes(jnp.zeros_like(partner), jnp.ones_like(partner))
-    across = side[:, :, None] != side[:, None, :]
-    positive = across & (place[:, :, None] == place[:, None, :])
-    include = across & (tongue[:, :, None] == tongue[:, None, :])
-    similar = jnp.einsum("mid,mjd->mij", units, units, preferred_element_type=jnp.float32)
-    scored = jnp.where(include, SIM_SCALE * similar - SIM_SCALE * MARGIN * positive, MASKED)
-    totals = jax.nn.logsumexp(scored, axis=2)
-    grad_sim = jnp.where(
-        include,
-        jnp.exp(scored - totals[:, :, None]) + jnp.exp(scored - totals[:, None, :]),
-        0.0,
+    def split(value):
+        return value.reshape(micro_count, count, 1, pair_dev)
+
+    node_rows = jnp.stack(
+        [
+            jnp.concatenate([split(language), split(target_language)], 2),
+            jnp.concatenate(
+                [split(partner), split(jnp.broadcast_to(pair_ids, partner.shape))], 2
+            ),
+        ],
+        1,
     )
-    grad_sim = (grad_sim - 2.0 * positive).astype(jnp.bfloat16)
-    grad_sim = lax.dynamic_slice_in_dim(grad_sim, device * node_dev, node_dev, 1)
-    unit_grad = SIM_SCALE * jnp.einsum(
-        "mij,mjd->mid", grad_sim, units, preferred_element_type=jnp.float32
+    node_rows = node_rows.reshape(2 * micro_count, count * node_dev).astype(jnp.float32)
+    node_rows = jnp.pad(node_rows, ((0, -2 * micro_count % 8), (0, 0)))
+    block_at = jnp.arange(SPAN) // HEAD_DIM
+    diag = (block_at[:, None] == block_at[None, :]).astype(jnp.bfloat16)
+
+    x = hidden_in.reshape(row_count, model_width)
+    sent_lengths = lengths.reshape(sent_count)
+    weights = (query_full, key_full, value_full, proj_full)
+    *saved, first_sum, cls_sum = attend(x, sent_lengths, weights, vec, diag, seq_len, 512)
+    cls_grad, grad_pool, grad_pool_shift = rank(
+        layout,
+        cls_sum.reshape(sent_count, model_width),
+        inner_full,
+        outer_full,
+        pool_full,
+        vec,
+        bias,
+        node_rows,
+        micro_count,
+        384,
+        1,
     )
-    unit_grad = unit_grad.reshape(sent_count, model_width)
-    pooled_grad = scale_inv * (
-        unit_grad - unit_vec * jnp.sum(unit_grad * unit_vec, -1, keepdims=True)
+    block_out, first_grad, grad_inner, grad_outer, vec_grad, grad_bias = feed(
+        first_sum,
+        token_cotangent.reshape(row_count, model_width),
+        cls_grad,
+        inner_full,
+        outer_full,
+        vec,
+        bias,
+        seq_len,
+        256,
+        384,
     )
-    pre_grad = pooled_grad * (1.0 - pooled * pooled)
-    pre_grad_b = pre_grad.astype(jnp.bfloat16)
-    grad_pool = dot_left_t(cls_rows, pre_grad_b)
-    grad_pool_shift = jnp.sum(pre_grad, 0)
-    cls_grad = dot_right_t(pre_grad_b, pool_full)
-    out_grad = token_cotangent.reshape(sent_count, seq_len, model_width).astype(jnp.float32)
-    first = jnp.arange(seq_len)[None, :, None] == 0
-    out_grad = out_grad + jnp.where(first, cls_grad[:, None, :], 0.0)
-    out_grad = out_grad.reshape(row_count, model_width)
-    second_grad, grad_gain_two, grad_shift_two = norm_backward(
-        out_grad, normed_two, inverse_two, gain_second
+    input_grad, grad_query, grad_key, grad_value, grad_proj, vec_grad_two = back(
+        x, sent_lengths, saved, first_grad, weights, diag, seq_len, 256
     )
-    second_b = second_grad.astype(jnp.bfloat16)
-    grad_outer = dot_left_t(active, second_b)
-    grad_outer_shift = jnp.sum(second_grad, 0)
-    inner_grad = dot_right_t(second_b, outer_full) * gelu_slope(inner_act)
-    grad_inner_shift = jnp.sum(inner_grad, 0)
-    inner_b = inner_grad.astype(jnp.bfloat16)
-    grad_inner = dot_left_t(hidden_b, inner_b)
-    hidden_grad = second_grad + dot_right_t(inner_b, inner_full)
-    first_grad, grad_gain_one, grad_shift_one = norm_backward(
-        hidden_grad, normed_one, inverse_one, gain_first
-    )
-    grad_proj_shift = jnp.sum(first_grad, 0)
-    first_b = first_grad.astype(jnp.bfloat16)
-    grad_proj = dot_left_t(mixture, first_b)
-    mixture_grad = dot_right_t(first_b, proj_full).astype(jnp.bfloat16).reshape(head_shape)
-    probs_full = jnp.exp(scores - log_totals)
-    prob_grad = jnp.einsum(
-        "gqhe,gkhe->ghqk", mixture_grad, values, preferred_element_type=jnp.float32
-    )
-    value_grad = jnp.einsum(
-        "ghqk,gqhe->gkhe", probs_b, mixture_grad, preferred_element_type=jnp.float32
-    )
-    value_grad = value_grad.astype(jnp.bfloat16).reshape(row_count, model_width)
-    score_grad = probs_full * (prob_grad - jnp.sum(prob_grad * probs_full, -1, keepdims=True))
-    score_grad = score_grad.astype(jnp.bfloat16)
-    query_grad = jnp.einsum(
-        "ghqk,gkhe->gqhe", score_grad, key_rows, preferred_element_type=jnp.float32
-    )
-    query_grad = (query_grad * head_scale).astype(jnp.bfloat16).reshape(row_count, model_width)
-    key_grad = jnp.einsum(
-        "ghqk,gqhe->gkhe", score_grad, queries, preferred_element_type=jnp.float32
-    )
-    key_grad = (key_grad * head_scale).astype(jnp.bfloat16).reshape(row_count, model_width)
-    grad_query = dot_left_t(tokens, query_grad)
-    grad_key = dot_left_t(tokens, key_grad)
-    grad_value = dot_left_t(tokens, value_grad)
-    grad_query_shift = jnp.sum(query_grad.astype(jnp.float32), 0)
-    grad_value_shift = jnp.sum(value_grad.astype(jnp.float32), 0)
-    token_grad = (
-        first_grad
-        + dot_right_t(query_grad, query_full)
-        + dot_right_t(key_grad, key_full)
-        + dot_right_t(value_grad, value_full)
-    )
-    input_grad = token_grad.reshape(hidden_in.shape)
-
+    block_out = block_out.reshape(hidden_in.shape)
+    input_grad = input_grad.reshape(hidden_in.shape)
+    vec_grad = jnp.concatenate([vec_grad_two[:2], vec_grad[2:8], grad_pool_shift], 0)
+    vec_grad = jnp.moveaxis(vec_grad.reshape(rows_of, count, share), 1, 0)
     small_grad = small_pack(
-        layout,
-        [
-            v.reshape(count, -1)
-            for v in (
-                grad_query_shift,
-                grad_value_shift,
-                grad_proj_shift,
-                grad_gain_one,
-                grad_shift_one,
-                grad_outer_shift,
-                grad_gain_two,
-                grad_shift_two,
-                grad_pool_shift,
-                grad_inner_shift,
-            )
-        ],
+        layout, [vec_grad.reshape(count, -1), grad_bias.reshape(count, -1)]
     )
     partial_sums = [
         grad_query,

time: 741 us -> 477 us (0.64); the launches traced: 732 us -> 476 us
  matrix products: 309 us -> 0 us
  Pallas kernels: 203 us -> 435 us
  local copies, waits for them, and re-layouts: 174 us -> 38.1 us
  other arithmetic: 43.7 us -> 1.77 us
    dot_general x29 -> x0, matrix products: 309 us -> none  [the longest x7 112 us: dot_plain(): return jnp.dot(first_mat, second_mat, preferred_element_type=jnp.float32)]
    pallas_call x0 -> x4, Pallas kernels: none -> 258 us  [the longest x1 103 us: feed(): pl.pallas_call(functools.partial(feed_kernel, seq_len, blocks, pieces), g...]
    reshape x22 -> x13, local copies, waits for them, and re-layouts: 90.6 us -> 4.39 us  [the longest x1 1.56 us: feed(): cls_grad = cls_grad.reshape(blocks, held, width)]
    convert_element_type x5 -> x2, local copies, waits for them, and re-layouts: 45.6 us -> 0.32 us  [on_device(): node_rows.reshape(2 * micro_count, count * node_dev).astype(jnp.float32)]
    reduce_sum x10 -> x0, other arithmetic: 28.7 us -> none  [the longest x2 7.12 us: norm_backward(): return (back, jnp.sum(upstream * normed, 0), jnp.sum(upstream, 0))]
    pallas_call x2 -> x1, Pallas kernels: 113 us -> 87.1 us  [gather_all(): pl.pallas_call(functools.partial(gather_kernel, layout, plan, len(arrays)...]
    convert_element_type x2, other arithmetic: 10.2 us -> 0.77 us  [the longest x1 0.76 us: on_device(): diag = (block_at[:, None] == block_at[None, :]).astype(jnp.bfloat16)]
    unnamed x146 -> x48, local copies, waits for them, and re-layouts: 29.2 us -> 26.9 us
where the time goes in v2:
time: 477 us; the launch traced here: 476 us
  Pallas kernels  435 us (91%)
  local copies, waits for them, and re-layouts  38.1 us (8%)
    pallas_call x1, Pallas kernels, feed(): pl.pallas_call(functools.partial(feed_kernel, seq_len, blocks, pieces), g...  103 us
    pallas_call x1, Pallas kernels, scatter_all(): pl.pallas_call(functools.partial(scatter_kernel, layout, plan, len(arrays...  90.4 us
    pallas_call x1, Pallas kernels, gather_all(): pl.pallas_call(functools.partial(gather_kernel, layout, plan, len(arrays)...  87.1 us
    pallas_call x1, Pallas kernels, back(): pl.pallas_call(functools.partial(back_kernel, seq_len, blocks), grid=(blo...  65.2 us
    pallas_call x1, Pallas kernels, attend(): pl.pallas_call(functools.partial(attend_kernel, seq_len), grid=(steps,),...  49.7 us
    pallas_call x1, Pallas kernels, rank(): pl.pallas_call(functools.partial(rank_kernel, layout, micros, node_dev, s...  39.3 us
    unnamed x48, local copies, waits for them, and re-layouts  26.9 us

profile of v2, /device:TPU:0, one launch (start us, length us, event | category | flops | bytes accessed | tf_op | source)
XLA Modules:
  0.0 475.9 jit_solution(18009512764692725234)
XLA Ops:
  0.7 0.9 concatenate.16
  1.6 0.0 copy-start.7
  1.6 0.9 copy-done.7
  2.5 0.9 copy-done.8
  3.4 0.8 copy-done.9
  4.2 0.8 copy-done.10
  4.9 0.8 copy-done.11
  5.7 0.8 copy-done.12
  6.5 0.8 copy-done.13
  7.2 87.1 %shard_map.357 = (bf16[2,2,2,4,24,768]{5,4,3,2,1,0:T(8,128)(2,1)S(1)}, bf16[2,2,2,4,24,768]{5,4,3,2,1,0:T(8,128)(2,1)S(1)}, bf16[2,2,2,4,24,768]{5,4,3,2,1,0:T(8...) custom-call(bf16[24,768]{1,0:T(8,128)(2,1)S(1)} %copy-done.9, ...), custom_call_target="tpu_custom_call" | custom-call | tf_op jit(solution)/shard_map/pallas_call | solution.py:285
  94.3 0.0 copy-start
  94.3 2.1 copy-done
  96.4 2.1 copy-done.1
  98.6 1.0 copy-done.2
  99.6 1.0 copy-done.3
  100.6 1.0 copy-done.4
  101.6 1.1 copy-done.5
  102.7 1.0 copy-done.6
  103.7 0.1 copy.71
  103.8 0.1 copy.62
  104.0 0.1 reshape.214
  104.1 0.6 pad.18.vec_ref
  104.7 0.8 compare_convert_fusion.diag_ref
  105.5 1.3 reshape.207.lengths_ref
  106.8 49.7 %shard_map.358 = (bf16[2048,768]{1,0:T(8,128)(2,1)}, bf16[2048,768]{1,0:T(8,128)(2,1)}, bf16[2048,768]{1,0:T(8,128)(2,1)}, bf16[2048,768]{1,0:T(8,128)(2,1)}, f32[2048,768]{1,0:T(8,128)}, /*index=5*/f32[4,8,768]{2,1,0:T(8,128)}) custom-call(s32[32]{0:T(128)} %reshape.207.lengths_ref, bf16[2048,768]{1,0:T(8,128)(2,1)} %bitcast.68, bf16[768,768]{1,0:T(8,128)(2,1)} %bitcast.57, ...), custom_call_target="tpu_custom_call" | custom-call | tf_op jit(solution)/shard_map/pallas_call | solution.py:496
  156.4 0.1 slice.57
  156.5 0.7 reshape.220.bias_ref
  157.2 0.0 copy-done.16
  157.2 0.0 copy-done.17
  157.2 0.2 select_reduce_fusion
  157.4 0.1 reshape.222
  157.5 0.1 copy.64
  157.6 0.1 reshape.221
  157.7 0.1 copy.63
  157.7 0.1 reshape.223
  157.8 0.1 copy.65
  157.9 0.1 copy.68
  158.0 0.2 convert_element_type.71
  158.3 0.6 pad.19.node_ref
  158.9 39.3 %shard_map.359 = (f32[32,768]{1,0:T(8,128)}, bf16[768,768]{1,0:T(8,128)(2,1)}, f32[1,768]{1,0:T(1,128)}) custom-call(f32[32,768]{1,0:T(8,128)} %bitcast.84, bf16[768,3072]{1,0:T(8,128)(2,1)} %bitcast.53, bf16[3072,768]{1,0:T(8,128)(2,1)} %bitcast.55, bf16[768,768]{1,0:T(8,128)(2,1)} %bitcast.65, f32[16,768]{1,0:T(8,128)} %pad.18.vec_ref, ...), custom_call_target="tpu_custom_call" | custom-call | tf_op jit(solution)/shard_map/pallas_call | solution.py:894
  198.2 1.6 reshape.227.cls_ref
  199.7 103.5 %shard_map.360 = (bf16[2048,768]{1,0:T(8,128)(2,1)}, f32[2048,768]{1,0:T(8,128)}, bf16[768,3072]{1,0:T(8,128)(2,1)}, bf16[3072,768]{1,0:T(8,128)(2,1)}, f32[8,768]{1,0:T(8,128)}, /*index=5*/f32[1,3072]{1,0:T(1,128)}) custom-call(f32[2048,768]{1,0:T(8,128)} %get-tuple-element.61.sum_ref, bf16[2048,768]{1,0:T(8,128)(2,1)} %bitcast.72, ...), custom_call_target="tpu_custom_call" | custom-call | tf_op jit(solution)/shard_map/pallas_call | solution.py:604
  303.2 0.0 copy-start.18
  303.2 0.0 copy-start.15
  303.2 65.2 %shard_map.361 = (f32[2048,768]{1,0:T(8,128)}, bf16[768,768]{1,0:T(8,128)(2,1)}, bf16[768,768]{1,0:T(8,128)(2,1)}, bf16[768,768]{1,0:T(8,128)(2,1)}, bf16[768,768]{1,0:T(8,128)(2,1)}, /*index=5*/f32[8,768]{1,0:T(8,128)}) custom-call(s32[32]{0:T(128)} %reshape.207.lengths_ref, bf16[2048,768]{1,0:T(8,128)(2,1)} %bitcast.69, ...), custom_call_target="tpu_custom_call" | custom-call | tf_op jit(solution)/shard_map/pallas_call | solution.py:743
  368.4 0.7 slice.44
  369.2 0.1 reshape.237
  369.4 0.1 copy.69
  369.5 0.1 copy.70
  369.5 0.5 broadcast.93
  370.1 0.7 reduce.3
  370.7 0.1 reshape.239
  370.8 0.1 fusion
  370.9 0.7 copy.73
  371.6 90.4 %shard_map.362 = (f32[24,768]{1,0:T(8,128)}, f32[24,768]{1,0:T(8,128)}, f32[24,768]{1,0:T(8,128)}, f32[24,768]{1,0:T(8,128)}, f32[24,768]{1,0:T(8,128)}, /*index...) custom-call(bf16[2,2,2,4,24,768]{5,4,3,2,1,0:T(8,128)(2,1)} %bitcast.74, ...), custom_call_target="tpu_custom_call" | custom-call | tf_op jit(solution)/shard_map/pallas_call | solution.py:339
  462.0 1.6 fusion.1
  463.6 1.3 slice.51
  464.9 1.5 copy.83
  466.4 1.5 copy.84
  467.9 1.5 copy.85
  469.5 1.5 copy.86
  471.0 1.7 copy.87
  472.7 1.7 copy.88
  474.4 1.5 copy.89
  (27 shorter events, 0.1 us)
Async XLA Ops:
  1.6 0.9 copy-start.7
  2.5 0.9 copy-start.8
  3.4 0.8 copy-start.9
  4.2 0.8 copy-start.10
  4.9 0.8 copy-start.11
  5.7 0.8 copy-start.12
  6.5 0.8 copy-start.13
  94.3 2.1 copy-start
  96.4 2.1 copy-start.1
  98.6 1.0 copy-start.2
  99.6 1.0 copy-start.3
  100.6 1.0 copy-start.4
  101.6 1.1 copy-start.5
  102.7 1.0 copy-start.6
  106.8 50.4 %copy-start.16 = (s32[2,256]{1,0:T(2,128)S(1)}, s32[2,256]{1,0:T(2,128)}, u32[]{:S(2)}) copy-start(s32[2,256]{1,0:T(2,128)} %param.25) | copy-start | bytes 6148
  106.8 50.4 %copy-start.17 = (s32[2,256]{1,0:T(2,128)S(1)}, s32[2,256]{1,0:T(2,128)}, u32[]{:S(2)}) copy-start(s32[2,256]{1,0:T(2,128)} %param.24) | copy-start | bytes 6148
  303.2 66.0 %copy-start.14 = (f32[8,768]{1,0:T(8,128)S(1)}, f32[8,768]{1,0:T(8,128)}, u32[]{:S(2)}) copy-start(f32[8,768]{1,0:T(8,128)} %get-tuple-element.82) | copy-start | bytes 73732
  303.2 66.0 %copy-start.18 = (f32[1,768]{1,0:T(1,128)S(1)}, f32[1,768]{1,0:T(1,128)}, u32[]{:S(2)}) copy-start(f32[1,768]{1,0:T(1,128)} %get-tuple-element.83) | copy-start | bytes 9220
  303.2 66.8 %copy-start.15 = (f32[1,3072]{1,0:T(1,128)S(1)}, f32[1,3072]{1,0:T(1,128)}, u32[]{:S(2)}) copy-start(f32[1,3072]{1,0:T(1,128)} %get-tuple-element.84) | copy-start | bytes 36868

commit v3 on v2

--- a/solution.py
+++ b/solution.py
@@ -142,6 +142,80 @@
                 todo.append((job, stage))
         rounds.append(todo)
     return rounds
+
+
+class Sidecar:
+    def __init__(self, jobs, entries, stages, places):
+        self.jobs = jobs
+        self.rounds = []
+        for step in range(max(entries) + stages + 1):
+            todo = []
+            for job, entry in zip(jobs, entries):
+                if 0 <= step - entry <= stages:
+                    todo.append((job, step - entry))
+            self.rounds.append(todo)
+        self.places = places(len(self.rounds))
+
+    def visit(self, step, point):
+        for todo, place in zip(self.rounds, self.places):
+            if place[1] == point:
+
+                @pl.when(step == place[0])
+                def _():
+                    for job, stage in todo:
+                        job.advance(stage)
+
+    def finish(self):
+        for job in self.jobs:
+            job.finish()
+
+
+def evenly(places):
+    return lambda count: [places[at * len(places) // count] for at in range(count)]
+
+
+class SumJob:
+    def __init__(self, layout, own, start, lands, results, sems):
+        self.layout, self.own, self.start = layout, own, start
+        self.lands, self.results = lands, results
+        self.send_sems, self.recv_sems = sems
+        self.order = tuple(range(len(layout.dims)))
+
+    def copies(self, stage):
+        base = self.layout.first_slot(self.order, stage)
+        source = self.start if stage == 0 else self.results[stage - 1]
+        out = []
+        for step in range(1, self.layout.dims[stage]):
+            slot = base + step - 1
+            out.append(
+                pltpu.make_async_remote_copy(
+                    src_ref=source,
+                    dst_ref=self.lands.at[slot],
+                    send_sem=self.send_sems.at[slot],
+                    recv_sem=self.recv_sems.at[slot],
+                    device_id=self.layout.device(self.layout.shifted(self.own, stage, step)),
+                    device_id_type=MESH_ID,
+                )
+            )
+        return out
+
+    def advance(self, stage):
+        if stage > 0:
+            before = stage - 1
+            value = self.start[...] if before == 0 else self.results[before - 1][...]
+            base = self.layout.first_slot(self.order, before)
+            for at, copy in enumerate(self.copies(before)):
+                copy.wait_recv()
+                value = value + self.lands[base + at]
+            self.results[before][...] = value
+        if stage < len(self.order):
+            for copy in self.copies(stage):
+                copy.start()
+
+    def finish(self):
+        for stage in range(len(self.order)):
+            for copy in self.copies(stage):
+                copy.wait_send()
 
 
 class ScatterJob:
@@ -256,12 +330,19 @@
     return sums + lands
 
 
-def gather_kernel(layout, plan, count, *refs):
-    shards, fulls = refs[:count], refs[count : 2 * count]
-    send_sems, recv_sems, local_sems = refs[2 * count :]
-    own = layout.own()
-    layout.greet(own)
-    jobs = [
+ANYWHERE = pl.BlockSpec(memory_space=pltpu.HBM)
+
+
+def job_sems(layout, plan):
+    return [
+        pltpu.SemaphoreType.DMA((len(plan), layout.sends)),
+        pltpu.SemaphoreType.DMA((len(plan), layout.sends)),
+        pltpu.SemaphoreType.DMA((len(plan),)),
+    ]
+
+
+def gather_jobs(layout, own, plan, shards, fulls, send_sems, recv_sems, local_sems):
+    return [
         GatherJob(
             layout,
             own,
@@ -273,38 +354,16 @@
         )
         for at, (which, way, columns) in enumerate(plan)
     ]
-    for todo in run_rounds(jobs, len(layout.dims)):
-        for job, stage in todo:
-            job.advance(stage)
-    for job in jobs:
-        job.finish()
-
-
-def gather_all(layout, arrays, plan, collective_id):
-    anywhere = pl.BlockSpec(memory_space=pl.ANY)
-    return pl.pallas_call(
-        functools.partial(gather_kernel, layout, plan, len(arrays)),
-        out_shape=[jax.ShapeDtypeStruct(layout.dims + a.shape, a.dtype) for a in arrays],
-        in_specs=[anywhere] * len(arrays),
-        out_specs=[anywhere] * len(arrays),
-        scratch_shapes=[
-            pltpu.SemaphoreType.DMA((len(plan), layout.sends)),
-            pltpu.SemaphoreType.DMA((len(plan), layout.sends)),
-            pltpu.SemaphoreType.DMA((len(plan),)),
-        ],
-        compiler_params=pltpu.CompilerParams(
-            collective_id=collective_id, has_side_effects=True, vmem_limit_bytes=16 * MIB
-        ),
-    )(*arrays)
-
-
-def scatter_kernel(layout, plan, count, buffers, *refs):
-    parts, results = refs[:count], refs[count : 2 * count]
-    scratch, (send_sems, recv_sems, local_sems) = refs[2 * count : -3], refs[-3:]
-    own = layout.own()
-    layout.greet(own)
+
+
+def gather_shapes(layout, arrays):
+    return [jax.ShapeDtypeStruct(layout.dims + a.shape, a.dtype) for a in arrays]
+
+
+def scatter_jobs(layout, own, plan, parts, results, scratch, send_sems, recv_sems, local_sems):
+    stages = len(layout.dims)
+    buffers = 2 * stages - 1
     jobs = []
-    stages = len(layout.dims)
     for at, (which, way, columns) in enumerate(plan):
         mine = scratch[at * buffers : (at + 1) * buffers]
         jobs.append(
@@ -320,35 +379,40 @@
                 columns,
             )
         )
-    for todo in run_rounds(jobs, stages):
+    return jobs
+
+
+def scatter_scratch(layout, plan, shapes):
+    scratch = []
+    for which, way, columns in plan:
+        rows, width = shapes[which]
+        width = width if columns is None else columns[1]
+        scratch += scatter_buffers(layout, layout.orders[way][::-1], rows, width, jnp.bfloat16)
+    return scratch
+
+
+def gather_kernel(layout, plan, count, *refs):
+    shards, fulls = refs[:count], refs[count : 2 * count]
+    send_sems, recv_sems, local_sems = refs[2 * count :]
+    own = layout.own()
+    layout.greet(own)
+    jobs = gather_jobs(layout, own, plan, shards, fulls, send_sems, recv_sems, local_sems)
+    for todo in run_rounds(jobs, len(layout.dims)):
         for job, stage in todo:
             job.advance(stage)
     for job in jobs:
         job.finish()
 
 
-def scatter_all(layout, arrays, plan, collective_id):
-    stages = len(layout.dims)
-    scratch = []
-    for which, way, columns in plan:
-        rows, width = arrays[which].shape[-2:]
-        width = width if columns is None else columns[1]
-        scratch += scatter_buffers(
-            layout, layout.orders[way][::-1], rows, width, arrays[which].dtype
-        )
+def gather_all(layout, arrays, plan, collective_id):
     return pl.pallas_call(
-        functools.partial(scatter_kernel, layout, plan, len(arrays), 2 * stages - 1),
-        out_shape=[jax.ShapeDtypeStruct(a.shape[-2:], jnp.float32) for a in arrays],
-        in_specs=[pl.BlockSpec(memory_space=pl.ANY)] * len(arrays),
-        out_specs=[pl.BlockSpec(memory_space=pltpu.VMEM)] * len(arrays),
-        scratch_shapes=scratch
-        + [
-            pltpu.SemaphoreType.DMA((len(plan), layout.sends)),
-            pltpu.SemaphoreType.DMA((len(plan), layout.sends)),
-            pltpu.SemaphoreType.DMA((len(plan),)),
-        ],
+        functools.partial(gather_kernel, layout, plan, len(arrays)),
+        out_shape=gather_shapes(layout, arrays),
+        in_specs=[ANYWHERE] * len(arrays),
+        out_specs=[ANYWHERE] * len(arrays),
+        scratch_shapes=job_sems(layout, plan),
         compiler_params=pltpu.CompilerParams(
-            collective_id=collective_id, has_side_effects=True, vmem_limit_bytes=60 * MIB
+            collective_id=collective_id, has_side_effects=True, vmem_limit_bytes=16 * MIB
         ),
     )(*arrays)
 
@@ -365,6 +429,18 @@
     for at in range(max(len(first), len(second))):
         out += first[at : at + 1] + second[at : at + 1]
     return out
+
+
+def copy_kernel(count, *refs):
+    for source, target in zip(refs[:count], refs[count:]):
+        target[...] = source[...]
+
+
+def copy_all(arrays):
+    return pl.pallas_call(
+        functools.partial(copy_kernel, len(arrays)),
+        out_shape=[jax.ShapeDtypeStruct(a.shape, a.dtype) for a in arrays],
+    )(*arrays)
 
 
 def small_pack(layout, vectors):
@@ -441,7 +517,11 @@
 
 
 def attend_kernel(
+    layout,
     seq_len,
+    plan,
+    count,
+    steps,
     lengths_ref,
     x_ref,
     query_w,
@@ -450,25 +530,34 @@
     proj_w,
     vec_ref,
     diag_ref,
-    q_ref,
-    k_ref,
-    v_ref,
-    mix_ref,
-    sum_ref,
-    cls_ref,
+    *refs,
 ):
+    shards, (q_ref, k_ref, v_ref, mix_ref, sum_ref, cls_ref) = refs[:count], refs[count : count + 6]
+    fulls, sems = refs[count + 6 : 2 * count + 6], refs[2 * count + 6 :]
     rows, width = x_ref.shape
     held = rows // seq_len
-    first = pl.program_id(0) * held
+    step = pl.program_id(0)
+    first = step * held
+    own = layout.own()
+
+    @pl.when(step == 0)
+    def _():
+        layout.greet(own)
+
+    jobs = gather_jobs(layout, own, plan, shards, fulls, *sems)
+    places = [(at, point) for at in range(steps) for point in range(4)]
+    sidecar = Sidecar(jobs, [at // 2 for at in range(len(jobs))], len(layout.dims), evenly(places))
+    sidecar.visit(step, 0)
     x = x_ref[...]
     q_ref[...] = (dot_plain(x, query_w[...]) + vec_ref[0:1, :]).astype(jnp.bfloat16)
     k_ref[...] = dot_plain(x, key_w[...]).astype(jnp.bfloat16)
     v_ref[...] = (dot_plain(x, value_w[...]) + vec_ref[1:2, :]).astype(jnp.bfloat16)
     diag = diag_ref[...]
+    sidecar.visit(step, 1)
 
     def sentence(at):
         length = lengths_ref[first + at]
-        here = pl.ds(pl.multiple_of(at * seq_len, seq_len), seq_len)
+        here = pl.ds(at * seq_len, seq_len)
         for low in range(0, width, SPAN):
             cols = pl.ds(low, SPAN)
             wide = spread(q_ref[here, cols], diag)
@@ -476,25 +565,34 @@
             mixed = fold(dot_left_t(probs, v_ref[here, cols]), seq_len)
             mix_ref[here, cols] = mixed.astype(jnp.bfloat16)
 
-    pl.loop(0, held)(sentence)
+    for at in range(held // 2):
+        sentence(at)
+    sidecar.visit(step, 2)
+    for at in range(held // 2, held):
+        sentence(at)
+    sidecar.visit(step, 3)
     total = x.astype(jnp.float32) + dot_plain(mix_ref[...], proj_w[...]) + vec_ref[2:3, :]
     sum_ref[...] = total
     for at in range(held):
         cls_ref[0, at : at + 1, :] = total[at * seq_len : at * seq_len + 1]
 
+    @pl.when(step == steps - 1)
+    def _():
+        sidecar.finish()
+
 
 def whole(shape):
     return pl.BlockSpec(shape, lambda *_: (0,) * len(shape), pipeline_mode=pl.Buffered(1))
 
 
-def attend(x, lengths, weights, vec, diag, seq_len, rows):
+def attend(layout, x, lengths, weights, vec, diag, arrays, plan, seq_len, rows, collective_id):
     total, width = x.shape
     steps = total // rows
     held = rows // seq_len
     block = pl.BlockSpec((rows, width), lambda i: (i, 0))
     narrow = jax.ShapeDtypeStruct((total, width), jnp.bfloat16)
     return pl.pallas_call(
-        functools.partial(attend_kernel, seq_len),
+        functools.partial(attend_kernel, layout, seq_len, plan, len(arrays), steps),
         grid=(steps,),
         out_shape=[
             narrow,
@@ -503,13 +601,20 @@
             narrow,
             jax.ShapeDtypeStruct((total, width), jnp.float32),
             jax.ShapeDtypeStruct((steps, held, width), jnp.float32),
-        ],
+        ]
+        + gather_shapes(layout, arrays),
         in_specs=[pl.BlockSpec(memory_space=pltpu.SMEM), block]
         + [whole(w.shape) for w in weights]
-        + [whole(vec.shape), whole(diag.shape)],
-        out_specs=[block] * 5 + [pl.BlockSpec((1, held, width), lambda i: (i, 0, 0))],
-        compiler_params=pltpu.CompilerParams(vmem_limit_bytes=60 * MIB),
-    )(lengths, x, *weights, vec, diag)
+        + [whole(vec.shape), whole(diag.shape)]
+        + [ANYWHERE] * len(arrays),
+        out_specs=[block] * 5
+        + [pl.BlockSpec((1, held, width), lambda i: (i, 0, 0))]
+        + [ANYWHERE] * len(arrays),
+        scratch_shapes=job_sems(layout, plan),
+        compiler_params=pltpu.CompilerParams(
+            collective_id=collective_id, has_side_effects=True, vmem_limit_bytes=60 * MIB
+        ),
+    )(lengths, x, *weights, vec, diag, *arrays)
 
 
 def feed_kernel(
@@ -518,6 +623,7 @@
     pieces,
     sum_ref,
     tok_ref,
+    mix_ref,
     cls_ref,
     inner_w,
     outer_w,
@@ -527,6 +633,7 @@
     back_ref,
     inner_grad,
     outer_grad,
+    proj_grad,
     vec_grad,
     bias_grad,
     slope,
@@ -534,6 +641,7 @@
     inner_b,
     hidden_b,
     second_b,
+    proj_sum,
 ):
     step = pl.program_id(0)
     rows, width = sum_ref.shape
@@ -543,6 +651,7 @@
     def _():
         vec_grad[...] = jnp.zeros_like(vec_grad)
         bias_grad[...] = jnp.zeros_like(bias_grad)
+        proj_sum[...] = jnp.zeros_like(proj_sum)
 
     @pl.when(step < blocks)
     def _():
@@ -586,6 +695,11 @@
         first = norm_backward(hidden_grad, normed_one, inverse_one, gain_one)
         vec_grad[2:3, :] += column_sum(first)
         back_ref[...] = first
+        proj_sum[...] += dot_left_t(mix_ref[...], first.astype(jnp.bfloat16))
+
+        @pl.when(step == blocks - 1)
+        def _():
+            proj_grad[...] = proj_sum[...].astype(jnp.bfloat16)
 
     @pl.when(step >= blocks)
     def _():
@@ -594,7 +708,9 @@
         inner_grad[...] = dot_left_t(hidden_b[...], inner_b[at]).astype(jnp.bfloat16)
 
 
-def feed(first_sum, tokens_grad, cls_grad, inner_w, outer_w, vec, bias, seq_len, rows, piece):
+def feed(
+    first_sum, tokens_grad, mixture, cls_grad, inner_w, outer_w, vec, bias, seq_len, rows, piece
+):
     total, width = first_sum.shape
     wide = inner_w.shape[1]
     blocks, pieces = total // rows, wide // piece
@@ -609,10 +725,12 @@
             jax.ShapeDtypeStruct((total, width), jnp.float32),
             jax.ShapeDtypeStruct(inner_w.shape, jnp.bfloat16),
             jax.ShapeDtypeStruct(outer_w.shape, jnp.bfloat16),
+            jax.ShapeDtypeStruct((width, width), jnp.bfloat16),
             jax.ShapeDtypeStruct((8, width), jnp.float32),
             jax.ShapeDtypeStruct((1, wide), jnp.float32),
         ],
         in_specs=[
+            block,
             block,
             block,
             pl.BlockSpec((1, held, width), lambda i: (jnp.minimum(i, blocks - 1), 0, 0)),
@@ -626,6 +744,7 @@
             block,
             pl.BlockSpec((width, piece), lambda i: (0, jnp.maximum(i - blocks, 0))),
             pl.BlockSpec((piece, width), lambda i: (jnp.maximum(i - blocks, 0), 0)),
+            whole((width, width)),
             pl.BlockSpec((8, width), lambda i: (0, 0)),
             pl.BlockSpec((1, wide), lambda i: (0, 0)),
         ],
@@ -635,63 +754,95 @@
             pltpu.VMEM((pieces, total, piece), jnp.bfloat16),
             pltpu.VMEM((total, width), jnp.bfloat16),
             pltpu.VMEM((total, width), jnp.bfloat16),
+            pltpu.VMEM((width, width), jnp.float32),
         ],
-        compiler_params=pltpu.CompilerParams(vmem_limit_bytes=62 * MIB),
-    )(first_sum, tokens_grad, cls_grad, inner_w, outer_w, vec, bias)
+        compiler_params=pltpu.CompilerParams(vmem_limit_bytes=63 * MIB),
+    )(first_sum, tokens_grad, mixture, cls_grad, inner_w, outer_w, vec, bias)
+
+
+def unflat(flat, dims):
+    digits = []
+    for size in reversed(dims):
+        digits.insert(0, flat % size)
+        flat = flat // size
+    return tuple(digits)
 
 
 def back_kernel(
+    layout,
     seq_len,
     blocks,
+    plan,
+    entries,
+    count,
     lengths_ref,
     x_ref,
     q_ref,
     k_ref,
     v_ref,
-    mix_ref,
     first_ref,
     query_w,
     key_w,
     value_w,
     proj_w,
     diag_ref,
-    in_ref,
-    query_g,
-    key_g,
-    value_g,
-    proj_g,
-    vec_grad,
-    x_all,
-    mix_all,
-    first_all,
-    dq_all,
-    dk_all,
-    dv_all,
-    dmix,
+    feed_vec,
+    feed_bias,
+    pool_vec,
+    *refs,
 ):
     step = pl.program_id(0)
     rows, width = x_ref.shape
     held = rows // seq_len
     scale = HEAD_DIM ** (-0.5)
+    stages = len(layout.dims)
+    parts, refs = refs[:count], refs[count:]
+    (in_ref, vec_sum), refs = refs[:2], refs[2:]
+    sums, refs = refs[: count + 3], refs[count + 3 :]
+    (x_all, dq_all, dk_all, dv_all, dmix), refs = refs[:5], refs[5:]
+    own_parts, refs = refs[:3], refs[3:]
+    (vec_grad, vec_lands), refs = refs[:2], refs[2:]
+    vec_steps, refs = refs[: stages - 1], refs[stages - 1 :]
+    own = layout.own()
+    vec_job = SumJob(layout, own, vec_grad, vec_lands, tuple(vec_steps) + (vec_sum,), refs[-2:])
+    jobs = scatter_jobs(layout, own, plan, parts + own_parts, sums, refs[:-5], *refs[-5:-2])
+
+    def places(total):
+        early = [(at // 2, at % 2) for at in range(2 * blocks)]
+        first_own = min(entry for entry, job in zip(entries, plan) if job[0] >= count)
+        out = [early[at * len(early) // first_own] for at in range(first_own)]
+        out += [(blocks + at, 1) for at in range(3)]
+        late = [(blocks + 3 + at, 0) for at in range(1, blocks)] + [(2 * blocks + 2, 1)]
+        rest = total - len(out)
+        stride = max(1, (len(late) - 1) // rest)
+        return out + [late[min(at * stride, len(late) - 1)] for at in range(rest)]
+
+    last_entry = max(entries)
+    sidecar = Sidecar(jobs + [vec_job], list(entries) + [last_entry], stages, places)
 
     @pl.when(step == 0)
     def _():
-        vec_grad[...] = jnp.zeros_like(vec_grad)
+        layout.greet(own)
+        vec_grad[0:2, :] = jnp.zeros_like(vec_grad[0:2, :])
+        vec_grad[2:8, :] = feed_vec[2:8, :]
+        vec_grad[8:9, :] = pool_vec[...]
+        pieces = feed_bias.shape[1] // width
+        vec_grad[9:, :] = jnp.zeros_like(vec_grad[9:, :])
+        for at in range(pieces):
+            vec_grad[9 + at : 10 + at, :] = feed_bias[:, at * width : (at + 1) * width]
 
     @pl.when(step < blocks)
     def _():
         here = pl.ds(pl.multiple_of(step * rows, rows), rows)
-        first = first_ref[...]
-        narrow = first.astype(jnp.bfloat16)
-        first_all[here, :] = narrow
+        sidecar.visit(step, 0)
         x_all[here, :] = x_ref[...]
-        mix_all[here, :] = mix_ref[...]
+        narrow = first_ref[...].astype(jnp.bfloat16)
         dmix[...] = dot_right_t(narrow, proj_w[...]).astype(jnp.bfloat16)
         diag = diag_ref[...]
 
         def sentence(at):
             length = lengths_ref[step * held + at]
-            near = pl.ds(pl.multiple_of(at * seq_len, seq_len), seq_len)
+            near = pl.ds(at * seq_len, seq_len)
             far = pl.ds(pl.multiple_of(step * rows + at * seq_len, seq_len), seq_len)
             for low in range(0, width, SPAN):
                 cols = pl.ds(low, SPAN)
@@ -710,53 +861,98 @@
                     jnp.bfloat16
                 )
 
-        pl.loop(0, held)(sentence)
-        dq, dk, dv = dq_all[here, :], dk_all[here, :], dv_all[here, :]
-        vec_grad[0:1, :] += column_sum(dq.astype(jnp.float32))
-        vec_grad[1:2, :] += column_sum(dv.astype(jnp.float32))
-        in_ref[...] = (
-            first
-            + dot_right_t(dq, query_w[...])
-            + dot_right_t(dk, key_w[...])
-            + dot_right_t(dv, value_w[...])
-        )
-
-    for at, (left, right, target) in enumerate(
-        (
-            (mix_all, first_all, proj_g),
-            (x_all, dq_all, query_g),
-            (x_all, dk_all, key_g),
-            (x_all, dv_all, value_g),
-        )
-    ):
+        for at in range(held // 2):
+            sentence(at)
+        sidecar.visit(step, 1)
+        for at in range(held // 2, held):
+            sentence(at)
+        vec_grad[0:1, :] += column_sum(dq_all[here, :].astype(jnp.float32))
+        vec_grad[1:2, :] += column_sum(dv_all[here, :].astype(jnp.float32))
+
+    for at, (right, part) in enumerate(zip((dq_all, dk_all, dv_all), own_parts)):
 
         @pl.when(step == blocks + at)
         def _():
-            target[...] = dot_left_t(left[...], right[...]).astype(jnp.bfloat16)
-
-
-def back(x, lengths, saved, first_grad, weights, diag, seq_len, rows):
+            value = dot_left_t(x_all[...], right[...])
+            share = part.shape[-2]
+            for device in range(layout.count):
+                piece = value[device * share : (device + 1) * share]
+                part[unflat(device, layout.dims)] = piece.astype(jnp.bfloat16)
+            sidecar.visit(step, 1)
+
+    @pl.when(step >= blocks + 3)
+    def _():
+        sidecar.visit(step, 0)
+        here = pl.ds(pl.multiple_of((step - blocks - 3) * rows, rows), rows)
+        in_ref[...] = (
+            first_ref[...]
+            + dot_right_t(dq_all[here, :], query_w[...])
+            + dot_right_t(dk_all[here, :], key_w[...])
+            + dot_right_t(dv_all[here, :], value_w[...])
+        )
+        sidecar.visit(step, 1)
+
+    @pl.when(step == 2 * blocks + 2)
+    def _():
+        sidecar.finish()
+
+
+def back(
+    layout,
+    x,
+    lengths,
+    saved,
+    first_grad,
+    weights,
+    diag,
+    vectors,
+    arrays,
+    plan,
+    entries,
+    seq_len,
+    rows,
+    collective_id,
+):
     total, width = x.shape
     blocks = total // rows
+    stages = len(layout.dims)
+    share = width // layout.count
+    shapes = [a.shape[-2:] for a in arrays] + [(share, width)] * 3
     block = pl.BlockSpec((rows, width), lambda i: (jnp.minimum(i, blocks - 1), 0))
-    square = jax.ShapeDtypeStruct((width, width), jnp.bfloat16)
+    twice = pl.BlockSpec(
+        (rows, width),
+        lambda i: (jnp.where(i < blocks, i, jnp.maximum(i - blocks - 3, 0)), 0),
+    )
+    out_block = pl.BlockSpec((rows, width), lambda i: (jnp.maximum(i - blocks - 3, 0), 0))
+    small = pltpu.VMEM((16, width), jnp.float32)
     return pl.pallas_call(
-        functools.partial(back_kernel, seq_len, blocks),
-        grid=(blocks + 4,),
-        out_shape=[jax.ShapeDtypeStruct((total, width), jnp.float32)]
-        + [square] * 4
-        + [jax.ShapeDtypeStruct((8, width), jnp.float32)],
+        functools.partial(back_kernel, layout, seq_len, blocks, plan, entries, len(arrays)),
+        grid=(2 * blocks + 3,),
+        out_shape=[
+            jax.ShapeDtypeStruct((total, width), jnp.float32),
+            jax.ShapeDtypeStruct((16, width), jnp.float32),
+        ]
+        + [jax.ShapeDtypeStruct(s, jnp.float32) for s in shapes],
         in_specs=[pl.BlockSpec(memory_space=pltpu.SMEM)]
-        + [block] * 6
+        + [block] * 4
+        + [twice]
         + [whole(w.shape) for w in weights]
-        + [whole(diag.shape)],
-        out_specs=[block]
-        + [pl.BlockSpec((width, width), lambda i: (0, 0))] * 4
-        + [pl.BlockSpec((8, width), lambda i: (0, 0))],
-        scratch_shapes=[pltpu.VMEM((total, width), jnp.bfloat16)] * 6
-        + [pltpu.VMEM((rows, width), jnp.bfloat16)],
-        compiler_params=pltpu.CompilerParams(vmem_limit_bytes=60 * MIB),
-    )(lengths, x, *saved, first_grad, *weights, diag)
+        + [whole(diag.shape)]
+        + [whole(v.shape) for v in vectors]
+        + [ANYWHERE] * len(arrays),
+        out_specs=[out_block, whole((16, width))] + [whole(s) for s in shapes],
+        scratch_shapes=[pltpu.VMEM((total, width), jnp.bfloat16)] * 4
+        + [pltpu.VMEM((rows, width), jnp.bfloat16)]
+        + [pltpu.VMEM(layout.dims + (share, width), jnp.bfloat16)] * 3
+        + [small, pltpu.VMEM((layout.sends, 16, width), jnp.float32)]
+        + [small] * (stages - 1)
+        + scatter_scratch(layout, plan, shapes)
+        + job_sems(layout, plan)
+        + [pltpu.SemaphoreType.DMA((layout.sends,))] * 2,
+        compiler_params=pltpu.CompilerParams(
+            collective_id=collective_id, has_side_effects=True, vmem_limit_bytes=63 * MIB
+        ),
+    )(lengths, x, *saved, first_grad, *weights, diag, *vectors, *arrays)
 
 
 def rank_kernel(
@@ -962,6 +1158,7 @@
     sent_count = micro_count * node_dev
     row_count = sent_count * seq_len
     pair_count = partner.shape[1]
+    device = lax.axis_index("dp") * (count // layout.slow) + lax.axis_index("fsdp")
 
     vectors = (
         query_bias,
@@ -976,23 +1173,16 @@
         in_bias,
     )
     small = small_pack(layout, [v[None] for v in vectors])[0]
-    arrays = [
-        query_weight,
-        key_weight,
-        value_weight,
-        attn_out_weight,
-        small,
-        pool_weight,
-        in_weight,
-        out_weight,
-    ]
-    plan = [(4, 0, None), (0, 1, None), (1, 0, None), (2, 1, None), (3, 0, None), (5, 1, None)]
-    plan += weave(cut(6, 0, inner_width, 4), cut(7, 1, model_width, 3))
+    arrays = [query_weight, key_weight, value_weight, attn_out_weight, small]
+    plan = [(4, 0, None)]
+    plan += weave(cut(0, 0, model_width, 2), cut(1, 1, model_width, 2))
+    plan += weave(cut(2, 0, model_width, 2), cut(3, 1, model_width, 2))
     gathered = gather_all(layout, arrays, tuple(plan), 0)
-    query_full, key_full, value_full, proj_full, small_full, pool_full, inner_full, outer_full = [
-        full.reshape((count * array.shape[0],) + array.shape[1:])
-        for full, array in zip(gathered, arrays)
-    ]
+
+    def joined(full, array):
+        return full.reshape((count * array.shape[0],) + array.shape[1:])
+
+    *weights, small_full = map(joined, gathered, arrays)
     small_rows = small_full.reshape(count, -1)
     share = query_bias.shape[0]
     rows_of = len(vectors) - 1
@@ -1025,8 +1215,12 @@
 
     x = hidden_in.reshape(row_count, model_width)
     sent_lengths = lengths.reshape(sent_count)
-    weights = (query_full, key_full, value_full, proj_full)
-    *saved, first_sum, cls_sum = attend(x, sent_lengths, weights, vec, diag, seq_len, 512)
+    arrays = [in_weight, out_weight, pool_weight]
+    plan = weave(cut(0, 0, inner_width, 4), cut(1, 1, model_width, 3)) + [(2, 1, None)]
+    queries, keys, values, mixture, first_sum, cls_sum, *gathered = attend(
+        layout, x, sent_lengths, weights, vec, diag, arrays, tuple(plan), seq_len, 512, 1
+    )
+    inner_full, outer_full, pool_full = map(joined, gathered, arrays)
     cls_grad, grad_pool, grad_pool_shift = rank(
         layout,
         cls_sum.reshape(sent_count, model_width),
@@ -1038,11 +1232,12 @@
         node_rows,
         micro_count,
         384,
-        1,
+        2,
     )
-    block_out, first_grad, grad_inner, grad_outer, vec_grad, grad_bias = feed(
+    block_out, first_grad, grad_inner, grad_outer, grad_proj, vec_grad, grad_bias = feed(
         first_sum,
         token_cotangent.reshape(row_count, model_width),
+        mixture,
         cls_grad,
         inner_full,
         outer_full,
@@ -1050,41 +1245,42 @@
         bias,
         seq_len,
         256,
-        384,
+        768,
     )
-    input_grad, grad_query, grad_key, grad_value, grad_proj, vec_grad_two = back(
-        x, sent_lengths, saved, first_grad, weights, diag, seq_len, 256
+
+    def apart(part):
+        return part.reshape(layout.dims + (-1, part.shape[1]))
+
+    parts = list(map(apart, (grad_inner, grad_outer, grad_pool, grad_proj)))
+    plan = weave(cut(0, 0, inner_width, 4), cut(1, 1, model_width, 3))
+    plan += [(2, 1, None), (3, 0, None)]
+    entries = [at // 2 for at in range(len(plan))]
+    for which in (4, 5, 6):
+        halves = cut(which, 0, model_width, 2)[:1] + cut(which, 1, model_width, 2)[1:]
+        entries += [entries[-1] + 1] * len(halves)
+        plan += halves
+    input_grad, vec_sum, *sums = back(
+        layout,
+        x,
+        sent_lengths,
+        (queries, keys, values),
+        first_grad,
+        weights,
+        diag,
+        (vec_grad, grad_bias, grad_pool_shift),
+        parts,
+        tuple(plan),
+        tuple(entries),
+        seq_len,
+        256,
+        3,
     )
     block_out = block_out.reshape(hidden_in.shape)
     input_grad = input_grad.reshape(hidden_in.shape)
-    vec_grad = jnp.concatenate([vec_grad_two[:2], vec_grad[2:8], grad_pool_shift], 0)
-    vec_grad = jnp.moveaxis(vec_grad.reshape(rows_of, count, share), 1, 0)
-    small_grad = small_pack(
-        layout, [vec_grad.reshape(count, -1), grad_bias.reshape(count, -1)]
-    )
-    partial_sums = [
-        grad_query,
-        grad_key,
-        grad_value,
-        grad_proj,
-        grad_pool,
-        grad_inner,
-        grad_outer,
-    ]
-    parts = [
-        part.astype(jnp.bfloat16).reshape(layout.dims + (-1, part.shape[1]))
-        for part in partial_sums
-    ]
-    parts.append(small_grad.reshape(layout.dims + small_grad.shape[1:]))
-    plan = weave(cut(5, 0, inner_width, 4), cut(6, 1, model_width, 3))
-    plan += [(3, 1, None), (4, 0, None), (0, 1, None), (1, 0, None), (2, 1, None), (7, 0, None)]
-    sums = scatter_all(layout, parts, tuple(plan), 2)
-    small_sum = sums[7].reshape(-1)
-    narrow = []
-    at = 0
-    for v in vectors:
-        narrow.append(small_sum[at : at + v.shape[0]])
-        at += v.shape[0]
+    sums = copy_all(sums)
+    vec_own = lax.dynamic_slice_in_dim(vec_sum[:rows_of], device * share, share, 1)
+    bias_sum = vec_sum[rows_of : rows_of + inner_width // model_width].reshape(-1)
+    bias_own = lax.dynamic_slice_in_dim(bias_sum, device * in_bias.shape[0], in_bias.shape[0])
     (
         sum_query_shift,
         sum_value_shift,
@@ -1095,27 +1291,26 @@
         sum_gain_two,
         sum_shift_two,
         sum_pool_shift,
-        sum_inner_shift,
-    ) = narrow
+    ) = vec_own
     return (
         block_out,
         input_grad,
-        sums[0],
-        sums[1],
-        sums[2],
+        sums[4],
+        sums[5],
+        sums[6],
         sums[3],
         sum_query_shift,
         sum_value_shift,
         sum_proj_shift,
         sum_gain_one,
         sum_shift_one,
-        sums[5],
-        sum_inner_shift,
-        sums[6],
+        sums[0],
+        bias_own,
+        sums[1],
         sum_outer_shift,
         sum_gain_two,
         sum_shift_two,
-        sums[4],
+        sums[2],
         sum_pool_shift,
     )
 

time: 477 us -> 395 us (0.83)
  Pallas kernels: 435 us -> 368 us
  local copies, waits for them, and re-layouts: 38.1 us -> 23.2 us
    pallas_call x1, Pallas kernels: 87.1 us -> 43.1 us  [gather_all(): pl.pallas_call(functools.partial(gather_kernel, layout, plan, len(arrays)...]
    pallas_call x1, Pallas kernels: 103 us -> 84.9 us  [feed(): pl.pallas_call(functools.partial(feed_kernel, seq_len, blocks, pieces), g...]
    unnamed x48 -> x23, local copies, waits for them, and re-layouts: 26.9 us -> 13.5 us
where the time goes in v3:
time: 395 us; the launch traced here: 393 us
  Pallas kernels  368 us (93%)
  local copies, waits for them, and re-layouts  23.2 us (6%)
    pallas_call x1, Pallas kernels, back(): pl.pallas_call(functools.partial(back_kernel, layout, seq_len, blocks, pl...  127 us
    pallas_call x1, Pallas kernels, feed(): pl.pallas_call(functools.partial(feed_kernel, seq_len, blocks, pieces), g...  84.9 us
    pallas_call x1, Pallas kernels, attend(): pl.pallas_call(functools.partial(attend_kernel, layout, seq_len, plan, le...  73.7 us
    pallas_call x1, Pallas kernels, gather_all(): pl.pallas_call(functools.partial(gather_kernel, layout, plan, len(arrays)...  43.1 us
    pallas_call x1, Pallas kernels, rank(): pl.pallas_call(functools.partial(rank_kernel, layout, micros, node_dev, s...  36.6 us
    unnamed x23, local copies, waits for them, and re-layouts  13.5 us

profile of v3, /device:TPU:0, one launch (start us, length us, event | category | flops | bytes accessed | tf_op | source)
XLA Modules:
  0.0 393.0 jit_solution(4728074210636709865)
XLA Ops:
  0.7 0.9 concatenate.10
  1.6 0.0 copy-start.4
  1.6 0.8 copy-done.4
  2.3 0.0 copy-start.5
  2.3 0.8 copy-done.5
  3.1 0.0 copy-start.6
  3.1 0.8 copy-done.6
  3.9 0.0 copy-start.7
  3.9 0.8 copy-done.7
  4.6 43.1 %shard_map.357 = (bf16[2,2,2,4,24,768]{5,4,3,2,1,0:T(8,128)(2,1)S(1)}, bf16[2,2,2,4,24,768]{5,4,3,2,1,0:T(8,128)(2,1)S(1)}, bf16[2,2,2,4,24,768]{5,4,3,2,1,0:T(8...) custom-call(bf16[24,768]{1,0:T(8,128)(2,1)S(1)} %copy-done.4, ...), custom_call_target="tpu_custom_call" | custom-call | tf_op jit(solution)/shard_map/pallas_call | solution.py:408
  47.7 0.0 copy-start
  47.7 1.0 copy-done
  48.8 0.0 copy-start.1
  48.8 1.0 copy-done.1
  49.8 0.0 copy-start.2
  49.8 1.0 copy-done.2
  50.8 0.0 copy-start.3
  50.8 1.1 copy-done.3
  51.9 0.1 copy.63
  52.0 0.1 copy.56
  52.1 0.1 reshape.196
  52.2 0.6 pad.14.vec_ref
  52.9 0.8 compare_convert_fusion.diag_ref
  53.6 1.3 reshape.189.lengths_ref
  54.9 0.0 copy-start.8
  54.9 0.0 copy-start.9
  54.9 73.7 %shard_map.358 = (bf16[2048,768]{1,0:T(8,128)(2,1)}, bf16[2048,768]{1,0:T(8,128)(2,1)}, bf16[2048,768]{1,0:T(8,128)(2,1)}, bf16[2048,768]{1,0:T(8,128)(2,1)}, f3...) custom-call(s32[32]{0:T(128)} %reshape.189.lengths_ref, ...), custom_call_target="tpu_custom_call" | custom-call | tf_op jit(solution)/shard_map/pallas_call | solution.py:594
  128.6 0.1 slice.17
  128.7 0.7 reshape.202.bias_ref
  129.4 0.0 copy-done.8
  129.4 0.0 copy-done.9
  129.4 0.2 select_reduce_fusion
  129.6 0.1 reshape.204
  129.7 0.1 copy.58
  129.7 0.1 reshape.203
  129.8 0.1 copy.57
  129.9 0.1 reshape.205
  130.0 0.1 copy.59
  130.1 0.1 copy.62
  130.2 0.2 convert_element_type.69
  130.4 0.6 pad.15.node_ref
  131.0 36.6 %shard_map.359 = (f32[32,768]{1,0:T(8,128)}, bf16[768,768]{1,0:T(8,128)(2,1)}, f32[1,768]{1,0:T(1,128)}) custom-call(f32[32,768]{1,0:T(8,128)} %bitcast.88, bf16[768,3072]{1,0:T(8,128)(2,1)} %bitcast.72, bf16[3072,768]{1,0:T(8,128)(2,1)} %bitcast.74, bf16[768,768]{1,0:T(8,128)(2,1)} %bitcast.82, f32[16,768]{1,0:T(8,128)} %pad.14.vec_ref, ...), custom_call_target="tpu_custom_call" | custom-call | tf_op jit(solution)/shard_map/pallas_call | solution.py:1090
  167.6 1.6 reshape.209.cls_ref
  169.2 84.9 %shard_map.360 = (bf16[2048,768]{1,0:T(8,128)(2,1)}, f32[2048,768]{1,0:T(8,128)}, bf16[768,3072]{1,0:T(8,128)(2,1)}, bf16[3072,768]{1,0:T(8,128)(2,1)}, bf16[768...) custom-call(f32[2048,768]{1,0:T(8,128)} %get-tuple-element.64.sum_ref, bf16[2048,768]{1,0:T(8,128)(2,1)} %bitcast.81, ...), custom_call_target="tpu_custom_call" | custom-call | tf_op jit(solution)/shard_map/pallas_call | solution.py:720
  254.1 127.5 %shard_map.361 = (f32[2048,768]{1,0:T(8,128)}, f32[16,768]{1,0:T(8,128)}, f32[24,3072]{1,0:T(8,128)}, f32[96,768]{1,0:T(8,128)}, f32[24,768]{1,0:T(8,128)}, /*in...) custom-call(s32[32]{0:T(128)} %reshape.189.lengths_ref, ...), custom_call_target="tpu_custom_call" | custom-call | tf_op jit(solution)/shard_map/pallas_call | solution.py:928
  381.6 2.1 shard_map.362
  383.7 0.7 slice.15
  384.5 0.6 dynamic_slice.7
  385.1 1.6 dynamic-slice_bitcast_fusion
  386.7 6.2 %copy.68 = f32[2,2,8,64,768]{4,3,2,1,0:T(8,128)} copy(f32[2,2,8,64,768]{4,3,2,1,0:T(8,128)} %bitcast.78) | data formatting | bytes 12582912
  (8 shorter events, 0.1 us)
Async XLA Ops:
  1.6 0.8 copy-start.4
  2.3 0.8 copy-start.5
  3.1 0.8 copy-start.6
  3.9 0.8 copy-start.7
  47.7 1.0 copy-start
  48.8 1.0 copy-start.1
  49.8 1.0 copy-start.2
  50.8 1.1 copy-start.3
  54.9 74.4 %copy-start.8 = (s32[2,256]{1,0:T(2,128)S(1)}, s32[2,256]{1,0:T(2,128)}, u32[]{:S(2)}) copy-start(s32[2,256]{1,0:T(2,128)} %param.25) | copy-start | bytes 6148
  54.9 74.4 %copy-start.9 = (s32[2,256]{1,0:T(2,128)S(1)}, s32[2,256]{1,0:T(2,128)}, u32[]{:S(2)}) copy-start(s32[2,256]{1,0:T(2,128)} %param.24) | copy-start | bytes 6148

commit v4 on v3

--- a/solution.py
+++ b/solution.py
@@ -145,19 +145,22 @@
 
 
 class Sidecar:
-    def __init__(self, jobs, entries, stages, places):
+    def __init__(self, jobs, entries, stages, lag, place):
         self.jobs = jobs
+        events = []
+        for at, (job, entry) in enumerate(zip(jobs, entries)):
+            for stage in range(stages + 1):
+                events.append((entry + lag * stage, at, job, stage))
+        events.sort(key=lambda event: event[:2])
         self.rounds = []
-        for step in range(max(entries) + stages + 1):
-            todo = []
-            for job, entry in zip(jobs, entries):
-                if 0 <= step - entry <= stages:
-                    todo.append((job, step - entry))
-            self.rounds.append(todo)
-        self.places = places(len(self.rounds))
+        for when, _, job, stage in events:
+            here = place(when, events[-1][0])
+            if not self.rounds or self.rounds[-1][0] != here:
+                self.rounds.append((here, []))
+            self.rounds[-1][1].append((job, stage))
 
     def visit(self, step, point):
-        for todo, place in zip(self.rounds, self.places):
+        for place, todo in self.rounds:
             if place[1] == point:
 
                 @pl.when(step == place[0])
@@ -171,7 +174,7 @@
 
 
 def evenly(places):
-    return lambda count: [places[at * len(places) // count] for at in range(count)]
+    return lambda when, last: places[min(int(when * len(places) / last), len(places) - 1)]
 
 
 class SumJob:
@@ -397,7 +400,7 @@
     own = layout.own()
     layout.greet(own)
     jobs = gather_jobs(layout, own, plan, shards, fulls, send_sems, recv_sems, local_sems)
-    for todo in run_rounds(jobs, len(layout.dims)):
+    for todo in run_rounds(jobs, len(layout.dims), 4):
         for job, stage in todo:
             job.advance(stage)
     for job in jobs:
@@ -412,7 +415,7 @@
         out_specs=[ANYWHERE] * len(arrays),
         scratch_shapes=job_sems(layout, plan),
         compiler_params=pltpu.CompilerParams(
-            collective_id=collective_id, has_side_effects=True, vmem_limit_bytes=16 * MIB
+            collective_id=collective_id, has_side_effects=True, vmem_limit_bytes=63 * MIB
         ),
     )(*arrays)
 
@@ -491,6 +494,7 @@
     return inner_act * below, below + inner_act * bell
 
 
+LAG_OUT, LAG_IN = 1.5, 1.5
 GROUP = 4
 SPAN = GROUP * HEAD_DIM
 
@@ -520,6 +524,7 @@
     layout,
     seq_len,
     plan,
+    entries,
     count,
     steps,
     lengths_ref,
@@ -546,7 +551,7 @@
 
     jobs = gather_jobs(layout, own, plan, shards, fulls, *sems)
     places = [(at, point) for at in range(steps) for point in range(4)]
-    sidecar = Sidecar(jobs, [at // 2 for at in range(len(jobs))], len(layout.dims), evenly(places))
+    sidecar = Sidecar(jobs, entries, len(layout.dims), LAG_OUT, evenly(places))
     sidecar.visit(step, 0)
     x = x_ref[...]
     q_ref[...] = (dot_plain(x, query_w[...]) + vec_ref[0:1, :]).astype(jnp.bfloat16)
@@ -585,14 +590,16 @@
     return pl.BlockSpec(shape, lambda *_: (0,) * len(shape), pipeline_mode=pl.Buffered(1))
 
 
-def attend(layout, x, lengths, weights, vec, diag, arrays, plan, seq_len, rows, collective_id):
+def attend(
+    layout, x, lengths, weights, vec, diag, arrays, plan, entries, seq_len, rows, collective_id
+):
     total, width = x.shape
     steps = total // rows
     held = rows // seq_len
     block = pl.BlockSpec((rows, width), lambda i: (i, 0))
     narrow = jax.ShapeDtypeStruct((total, width), jnp.bfloat16)
     return pl.pallas_call(
-        functools.partial(attend_kernel, layout, seq_len, plan, len(arrays), steps),
+        functools.partial(attend_kernel, layout, seq_len, plan, entries, len(arrays), steps),
         grid=(steps,),
         out_shape=[
             narrow,
@@ -612,7 +619,7 @@
         + [ANYWHERE] * len(arrays),
         scratch_shapes=job_sems(layout, plan),
         compiler_params=pltpu.CompilerParams(
-            collective_id=collective_id, has_side_effects=True, vmem_limit_bytes=60 * MIB
+            collective_id=collective_id, has_side_effects=True, vmem_limit_bytes=63 * MIB
         ),
     )(lengths, x, *weights, vec, diag, *arrays)
 
@@ -807,18 +814,20 @@
     vec_job = SumJob(layout, own, vec_grad, vec_lands, tuple(vec_steps) + (vec_sum,), refs[-2:])
     jobs = scatter_jobs(layout, own, plan, parts + own_parts, sums, refs[:-5], *refs[-5:-2])
 
-    def places(total):
-        early = [(at // 2, at % 2) for at in range(2 * blocks)]
-        first_own = min(entry for entry, job in zip(entries, plan) if job[0] >= count)
-        out = [early[at * len(early) // first_own] for at in range(first_own)]
-        out += [(blocks + at, 1) for at in range(3)]
-        late = [(blocks + 3 + at, 0) for at in range(1, blocks)] + [(2 * blocks + 2, 1)]
-        rest = total - len(out)
-        stride = max(1, (len(late) - 1) // rest)
-        return out + [late[min(at * stride, len(late) - 1)] for at in range(rest)]
+    own_at = sorted({entry for entry, job in zip(entries, plan) if job[0] >= count})
+
+    def place(when, last):
+        if when < own_at[0]:
+            half = int(when * 2 * blocks / own_at[0])
+            return (half // 2, half % 2)
+        for at, entry in enumerate(own_at):
+            if when <= entry:
+                return (blocks + at, 1)
+        half = int((when - own_at[-1]) * blocks / (last - own_at[-1]))
+        return (blocks + 3 + half, 0) if half < blocks else (2 * blocks + 2, 1)
 
     last_entry = max(entries)
-    sidecar = Sidecar(jobs + [vec_job], list(entries) + [last_entry], stages, places)
+    sidecar = Sidecar(jobs + [vec_job], list(entries) + [last_entry], stages, LAG_IN, place)
 
     @pl.when(step == 0)
     def _():
@@ -978,7 +987,7 @@
     totals,
     send_sems,
     recv_sems,
-    local_sem,
+    local_sems,
 ):
     step = pl.program_id(0)
     sentences, width = sum_ref.shape
@@ -1004,12 +1013,14 @@
         scale_inv = lax.rsqrt(jnp.sum(pooled * pooled, -1, keepdims=True) + UNIT_EPS)
         unit = pooled * scale_inv
         mine[...] = unit.astype(jnp.bfloat16)
-        job = GatherJob(
-            layout, own, layout.orders[0], mine, units, (send_sems, recv_sems, local_sem)
-        )
+        step_cols = width // len(layout.orders)
+        plan = [(0, way, (way * step_cols, step_cols)) for way in range(len(layout.orders))]
+        jobs = gather_jobs(layout, own, plan, [mine], [units], send_sems, recv_sems, local_sems)
         for stage in range(len(layout.dims) + 1):
-            job.advance(stage)
-        job.finish()
+            for job in jobs:
+                job.advance(stage)
+        for job in jobs:
+            job.finish()
 
         device = own[0]
         for size, digit in zip(layout.dims[1:], own[1:]):
@@ -1116,12 +1127,10 @@
             pltpu.VMEM(layout.dims + (sentences, width), jnp.bfloat16),
             pltpu.VMEM((nodes.shape[1], nodes.shape[0]), jnp.float32),
             pltpu.VMEM((1, nodes.shape[1]), jnp.float32),
-            pltpu.SemaphoreType.DMA((layout.sends,)),
-            pltpu.SemaphoreType.DMA((layout.sends,)),
-            pltpu.SemaphoreType.DMA,
-        ],
+        ]
+        + job_sems(layout, layout.orders),
         compiler_params=pltpu.CompilerParams(
-            collective_id=collective_id, has_side_effects=True, vmem_limit_bytes=60 * MIB
+            collective_id=collective_id, has_side_effects=True, vmem_limit_bytes=63 * MIB
         ),
     )(cls_sum, inner_w, outer_w, pool_w, vec, bias, nodes)
 
@@ -1216,9 +1225,16 @@
     x = hidden_in.reshape(row_count, model_width)
     sent_lengths = lengths.reshape(sent_count)
     arrays = [in_weight, out_weight, pool_weight]
-    plan = weave(cut(0, 0, inner_width, 4), cut(1, 1, model_width, 3)) + [(2, 1, None)]
+
+    def halves(which):
+        return cut(which, 0, model_width, 2)[:1] + cut(which, 1, model_width, 2)[1:]
+
+    first_cuts, second_cuts = cut(0, 0, inner_width, 8), cut(1, 1, model_width, 6)
+    plan = weave(first_cuts[:6], second_cuts)
+    plan += weave(first_cuts[6:], halves(2))
+    entries = tuple(at // 2 for at in range(len(plan)))
     queries, keys, values, mixture, first_sum, cls_sum, *gathered = attend(
-        layout, x, sent_lengths, weights, vec, diag, arrays, tuple(plan), seq_len, 512, 1
+        layout, x, sent_lengths, weights, vec, diag, arrays, tuple(plan), entries, seq_len, 512, 1
     )
     inner_full, outer_full, pool_full = map(joined, gathered, arrays)
     cls_grad, grad_pool, grad_pool_shift = rank(
@@ -1252,13 +1268,12 @@
         return part.reshape(layout.dims + (-1, part.shape[1]))
 
     parts = list(map(apart, (grad_inner, grad_outer, grad_pool, grad_proj)))
-    plan = weave(cut(0, 0, inner_width, 4), cut(1, 1, model_width, 3))
-    plan += [(2, 1, None), (3, 0, None)]
+    plan = weave(first_cuts[:6], second_cuts)
+    plan += weave(first_cuts[6:], halves(2)[::-1]) + halves(3)
     entries = [at // 2 for at in range(len(plan))]
     for which in (4, 5, 6):
-        halves = cut(which, 0, model_width, 2)[:1] + cut(which, 1, model_width, 2)[1:]
-        entries += [entries[-1] + 1] * len(halves)
-        plan += halves
+        entries += [entries[-1] + 1] * 2
+        plan += halves(which)
     input_grad, vec_sum, *sums = back(
         layout,
         x,

time: 395 us -> 365 us (0.924)
  Pallas kernels: 368 us -> 344 us
  local copies, waits for them, and re-layouts: 23.2 us -> 16.9 us
    pallas_call x1, Pallas kernels: 127 us -> 116 us  [back(): pl.pallas_call(functools.partial(back_kernel, layout, seq_len, blocks, pl...]
    unnamed x23 -> x7, local copies, waits for them, and re-layouts: 13.5 us -> 7.21 us
    pallas_call x1, Pallas kernels: 36.6 us -> 31.9 us  [rank(): pl.pallas_call(functools.partial(rank_kernel, layout, micros, node_dev, s...]
where the time goes in v4:
time: 365 us; the launch traced here: 363 us
  Pallas kernels  344 us (94%)
  local copies, waits for them, and re-layouts  16.9 us (5%)
    pallas_call x1, Pallas kernels, back(): pl.pallas_call(functools.partial(back_kernel, layout, seq_len, blocks, pl...  116 us
    pallas_call x1, Pallas kernels, feed(): pl.pallas_call(functools.partial(feed_kernel, seq_len, blocks, pieces), g...  84.8 us
    pallas_call x1, Pallas kernels, attend(): pl.pallas_call(functools.partial(attend_kernel, layout, seq_len, plan, en...  69.7 us
    pallas_call x1, Pallas kernels, gather_all(): pl.pallas_call(functools.partial(gather_kernel, layout, plan, len(arrays)...  39.4 us
    pallas_call x1, Pallas kernels, rank(): pl.pallas_call(functools.partial(rank_kernel, layout, micros, node_dev, s...  31.9 us

profile of v4, /device:TPU:0, one launch (start us, length us, event | category | flops | bytes accessed | tf_op | source)
XLA Modules:
  0.0 363.3 jit_solution(16939216995954388503)
XLA Ops:
  0.7 0.9 concatenate.10
  1.5 0.6 pad_convert_fusion
  2.1 39.4 %shard_map.357 = (bf16[2,2,2,4,24,768]{5,4,3,2,1,0:T(8,128)(2,1)}, bf16[2,2,2,4,24,768]{5,4,3,2,1,0:T(8,128)(2,1)}, bf16[2,2,2,4,24,768]{5,4,3,2,1,0:T(8,128)(2,...) custom-call(bf16[24,768]{1,0:T(8,128)(2,1)} %refs_0_.2, bf16[24,768]{1,0:T(8,128)(2,1)} %refs_1_.2, ...), custom_call_target="tpu_custom_call" | custom-call | tf_op jit(solution)/shard_map/pallas_call | solution.py:411
  41.6 0.9 copy.66
  42.5 0.1 copy.63
  42.6 0.1 copy.56
  42.7 0.1 reshape.196
  42.9 0.6 pad.14.vec_ref
  43.5 0.8 compare_convert_fusion.diag_ref
  44.3 1.3 reshape.189.lengths_ref
  45.5 0.0 copy-start
  45.5 0.0 copy-start.1
  45.5 69.7 %shard_map.358 = (bf16[2048,768]{1,0:T(8,128)(2,1)}, bf16[2048,768]{1,0:T(8,128)(2,1)}, bf16[2048,768]{1,0:T(8,128)(2,1)}, bf16[2048,768]{1,0:T(8,128)(2,1)}, f3...) custom-call(s32[32]{0:T(128)} %reshape.189.lengths_ref, ...), custom_call_target="tpu_custom_call" | custom-call | tf_op jit(solution)/shard_map/pallas_call | solution.py:601
  115.3 0.1 slice.17
  115.4 0.7 reshape.202.bias_ref
  116.0 0.0 copy-done
  116.0 0.0 copy-done.1
  116.0 0.2 select_reduce_fusion
  116.3 0.1 reshape.204
  116.4 0.1 copy.58
  116.4 0.1 reshape.203
  116.5 0.1 copy.57
  116.6 0.1 reshape.205
  116.7 0.1 copy.59
  116.8 0.1 copy.62
  116.9 0.2 convert_element_type.69
  117.1 0.6 pad.15.node_ref
  117.7 31.9 %shard_map.359 = (f32[32,768]{1,0:T(8,128)}, bf16[768,768]{1,0:T(8,128)(2,1)}, f32[1,768]{1,0:T(1,128)}) custom-call(f32[32,768]{1,0:T(8,128)} %bitcast.87, bf16[768,3072]{1,0:T(8,128)(2,1)} %bitcast.62, bf16[3072,768]{1,0:T(8,128)(2,1)} %bitcast.64, bf16[768,768]{1,0:T(8,128)(2,1)} %bitcast.80, f32[16,768]{1,0:T(8,128)} %pad.14.vec_ref, ...), custom_call_target="tpu_custom_call" | custom-call | tf_op jit(solution)/shard_map/pallas_call | solution.py:1101
  149.6 1.6 reshape.209.cls_ref
  151.2 84.8 %shard_map.360 = (bf16[2048,768]{1,0:T(8,128)(2,1)}, f32[2048,768]{1,0:T(8,128)}, bf16[768,3072]{1,0:T(8,128)(2,1)}, bf16[3072,768]{1,0:T(8,128)(2,1)}, bf16[768...) custom-call(f32[2048,768]{1,0:T(8,128)} %get-tuple-element.64.sum_ref, bf16[2048,768]{1,0:T(8,128)(2,1)} %bitcast.79, ...), custom_call_target="tpu_custom_call" | custom-call | tf_op jit(solution)/shard_map/pallas_call | solution.py:727
  236.0 115.8 %shard_map.361 = (f32[2048,768]{1,0:T(8,128)}, f32[16,768]{1,0:T(8,128)}, f32[24,3072]{1,0:T(8,128)}, f32[96,768]{1,0:T(8,128)}, f32[24,768]{1,0:T(8,128)}, /*in...) custom-call(s32[32]{0:T(128)} %reshape.189.lengths_ref, ...), custom_call_target="tpu_custom_call" | custom-call | tf_op jit(solution)/shard_map/pallas_call | solution.py:937
  351.9 2.1 shard_map.362
  354.0 0.7 slice.15
  354.8 0.6 dynamic_slice.7
  355.3 1.6 dynamic-slice_bitcast_fusion
  357.0 6.2 %copy.68 = f32[2,2,8,64,768]{4,3,2,1,0:T(8,128)} copy(f32[2,2,8,64,768]{4,3,2,1,0:T(8,128)} %bitcast.68) | data formatting | bytes 12582912
  (6 shorter events, 0.0 us)
Async XLA Ops:
  45.5 70.5 %copy-start = (s32[2,256]{1,0:T(2,128)S(1)}, s32[2,256]{1,0:T(2,128)}, u32[]{:S(2)}) copy-start(s32[2,256]{1,0:T(2,128)} %param.25) | copy-start | bytes 6148
  45.5 70.5 %copy-start.1 = (s32[2,256]{1,0:T(2,128)S(1)}, s32[2,256]{1,0:T(2,128)}, u32[]{:S(2)}) copy-start(s32[2,256]{1,0:T(2,128)} %param.24) | copy-start | bytes 6148

commit v5 on v4

--- a/solution.py
+++ b/solution.py
@@ -145,12 +145,13 @@
 
 
 class Sidecar:
-    def __init__(self, jobs, entries, stages, lag, place):
+    def __init__(self, jobs, entries, stages, offsets, place):
         self.jobs = jobs
         events = []
         for at, (job, entry) in enumerate(zip(jobs, entries)):
             for stage in range(stages + 1):
-                events.append((entry + lag * stage, at, job, stage))
+                after = offsets[stage] if len(offsets) == stages + 1 else 1.5 * stage
+                events.append((entry + after, at, job, stage))
         events.sort(key=lambda event: event[:2])
         self.rounds = []
         for when, _, job, stage in events:
@@ -494,7 +495,8 @@
     return inner_act * below, below + inner_act * bell
 
 
-LAG_OUT, LAG_IN = 1.5, 1.5
+GATHER_TIMES = (0, 1, 2, 3.5, 4.25)
+SCATTER_TIMES = (0, 0.75, 2.75, 3.75, 6.75)
 GROUP = 4
 SPAN = GROUP * HEAD_DIM
 
@@ -551,7 +553,7 @@
 
     jobs = gather_jobs(layout, own, plan, shards, fulls, *sems)
     places = [(at, point) for at in range(steps) for point in range(4)]
-    sidecar = Sidecar(jobs, entries, len(layout.dims), LAG_OUT, evenly(places))
+    sidecar = Sidecar(jobs, entries, len(layout.dims), GATHER_TIMES, evenly(places))
     sidecar.visit(step, 0)
     x = x_ref[...]
     q_ref[...] = (dot_plain(x, query_w[...]) + vec_ref[0:1, :]).astype(jnp.bfloat16)
@@ -827,7 +829,7 @@
         return (blocks + 3 + half, 0) if half < blocks else (2 * blocks + 2, 1)
 
     last_entry = max(entries)
-    sidecar = Sidecar(jobs + [vec_job], list(entries) + [last_entry], stages, LAG_IN, place)
+    sidecar = Sidecar(jobs + [vec_job], list(entries) + [last_entry], stages, SCATTER_TIMES, place)
 
     @pl.when(step == 0)
     def _():
@@ -1231,8 +1233,8 @@
 
     first_cuts, second_cuts = cut(0, 0, inner_width, 8), cut(1, 1, model_width, 6)
     plan = weave(first_cuts[:6], second_cuts)
-    plan += weave(first_cuts[6:], halves(2))
-    entries = tuple(at // 2 for at in range(len(plan)))
+    plan += halves(2) + first_cuts[6:]
+    entries = tuple(0.4 * at for at in range(len(plan)))
     queries, keys, values, mixture, first_sum, cls_sum, *gathered = attend(
         layout, x, sent_lengths, weights, vec, diag, arrays, tuple(plan), entries, seq_len, 512, 1
     )
@@ -1247,7 +1249,7 @@
         bias,
         node_rows,
         micro_count,
-        384,
+        768,
         2,
     )
     block_out, first_grad, grad_inner, grad_outer, grad_proj, vec_grad, grad_bias = feed(
@@ -1268,11 +1270,12 @@
         return part.reshape(layout.dims + (-1, part.shape[1]))
 
     parts = list(map(apart, (grad_inner, grad_outer, grad_pool, grad_proj)))
-    plan = weave(first_cuts[:6], second_cuts)
-    plan += weave(first_cuts[6:], halves(2)[::-1]) + halves(3)
-    entries = [at // 2 for at in range(len(plan))]
+    first_cuts, second_cuts = cut(0, 0, inner_width, 4), cut(1, 1, model_width, 3)
+    plan = weave(first_cuts[:3], second_cuts) + first_cuts[3:]
+    plan += weave(halves(2)[::-1], halves(3)[::-1])
+    entries = [0.75 * (at // 2) for at in range(len(plan))]
     for which in (4, 5, 6):
-        entries += [entries[-1] + 1] * 2
+        entries += [entries[-1] + 0.75] * 2
         plan += halves(which)
     input_grad, vec_sum, *sums = back(
         layout,

time: 365 us -> 357 us (0.978)
  Pallas kernels: 344 us -> 334 us
    pallas_call x1, Pallas kernels: 116 us -> 110 us  [back(): pl.pallas_call(functools.partial(back_kernel, layout, seq_len, blocks, pl...]
where the time goes in v5:
time: 357 us; the launch traced here: 354 us
  Pallas kernels  334 us (94%)
  local copies, waits for them, and re-layouts  16.9 us (5%)
    pallas_call x1, Pallas kernels, back(): pl.pallas_call(functools.partial(back_kernel, layout, seq_len, blocks, pl...  110 us
    pallas_call x1, Pallas kernels, feed(): pl.pallas_call(functools.partial(feed_kernel, seq_len, blocks, pieces), g...  84.8 us
    pallas_call x1, Pallas kernels, attend(): pl.pallas_call(functools.partial(attend_kernel, layout, seq_len, plan, en...  67.4 us
    pallas_call x1, Pallas kernels, gather_all(): pl.pallas_call(functools.partial(gather_kernel, layout, plan, len(arrays)...  39.4 us
    pallas_call x1, Pallas kernels, rank(): pl.pallas_call(functools.partial(rank_kernel, layout, micros, node_dev, s...  30.8 us
    unnamed x7, local copies, waits for them, and re-layouts  7.21 us

profile of v5, /device:TPU:0, one launch (start us, length us, event | category | flops | bytes accessed | tf_op | source)
XLA Modules:
  0.0 354.0 jit_solution(6715023889907687332)
XLA Ops:
  0.7 0.9 concatenate.10
  1.5 0.6 pad_convert_fusion
  2.1 39.4 %shard_map.357 = (bf16[2,2,2,4,24,768]{5,4,3,2,1,0:T(8,128)(2,1)}, bf16[2,2,2,4,24,768]{5,4,3,2,1,0:T(8,128)(2,1)}, bf16[2,2,2,4,24,768]{5,4,3,2,1,0:T(8,128)(2,...) custom-call(bf16[24,768]{1,0:T(8,128)(2,1)} %refs_0_.2, bf16[24,768]{1,0:T(8,128)(2,1)} %refs_1_.2, ...), custom_call_target="tpu_custom_call" | custom-call | tf_op jit(solution)/shard_map/pallas_call | solution.py:412
  41.6 0.9 copy.66
  42.5 0.1 copy.63
  42.6 0.1 copy.56
  42.7 0.1 reshape.196
  42.9 0.6 pad.14.vec_ref
  43.5 0.8 compare_convert_fusion.diag_ref
  44.3 1.3 reshape.189.lengths_ref
  45.5 0.0 copy-start
  45.5 0.0 copy-start.1
  45.5 67.4 %shard_map.358 = (bf16[2048,768]{1,0:T(8,128)(2,1)}, bf16[2048,768]{1,0:T(8,128)(2,1)}, bf16[2048,768]{1,0:T(8,128)(2,1)}, bf16[2048,768]{1,0:T(8,128)(2,1)}, f3...) custom-call(s32[32]{0:T(128)} %reshape.189.lengths_ref, ...), custom_call_target="tpu_custom_call" | custom-call | tf_op jit(solution)/shard_map/pallas_call | solution.py:603
  112.9 0.1 slice.17
  113.0 0.7 reshape.202.bias_ref
  113.7 0.0 copy-done
  113.7 0.0 copy-done.1
  113.7 0.2 select_reduce_fusion
  113.9 0.1 reshape.204
  114.0 0.1 copy.58
  114.0 0.1 reshape.203
  114.1 0.1 copy.57
  114.2 0.1 reshape.205
  114.3 0.1 copy.59
  114.4 0.1 copy.62
  114.5 0.2 convert_element_type.69
  114.7 0.6 pad.15.node_ref
  115.4 30.8 %shard_map.359 = (f32[32,768]{1,0:T(8,128)}, bf16[768,768]{1,0:T(8,128)(2,1)}, f32[1,768]{1,0:T(1,128)}) custom-call(f32[32,768]{1,0:T(8,128)} %bitcast.87, bf16[768,3072]{1,0:T(8,128)(2,1)} %bitcast.62, bf16[3072,768]{1,0:T(8,128)(2,1)} %bitcast.64, bf16[768,768]{1,0:T(8,128)(2,1)} %bitcast.80, f32[16,768]{1,0:T(8,128)} %pad.14.vec_ref, ...), custom_call_target="tpu_custom_call" | custom-call | tf_op jit(solution)/shard_map/pallas_call | solution.py:1103
  146.2 1.6 reshape.209.cls_ref
  147.7 84.8 %shard_map.360 = (bf16[2048,768]{1,0:T(8,128)(2,1)}, f32[2048,768]{1,0:T(8,128)}, bf16[768,3072]{1,0:T(8,128)(2,1)}, bf16[3072,768]{1,0:T(8,128)(2,1)}, bf16[768...) custom-call(f32[2048,768]{1,0:T(8,128)} %get-tuple-element.64.sum_ref, bf16[2048,768]{1,0:T(8,128)(2,1)} %bitcast.79, ...), custom_call_target="tpu_custom_call" | custom-call | tf_op jit(solution)/shard_map/pallas_call | solution.py:729
  232.6 109.9 %shard_map.361 = (f32[2048,768]{1,0:T(8,128)}, f32[16,768]{1,0:T(8,128)}, f32[24,3072]{1,0:T(8,128)}, f32[96,768]{1,0:T(8,128)}, f32[24,768]{1,0:T(8,128)}, /*in...) custom-call(s32[32]{0:T(128)} %reshape.189.lengths_ref, ...), custom_call_target="tpu_custom_call" | custom-call | tf_op jit(solution)/shard_map/pallas_call | solution.py:939
  342.5 2.1 shard_map.362
  344.6 0.7 slice.15
  345.4 0.6 dynamic_slice.7
  346.0 1.6 dynamic-slice_bitcast_fusion
  347.6 6.2 %copy.68 = f32[2,2,8,64,768]{4,3,2,1,0:T(8,128)} copy(f32[2,2,8,64,768]{4,3,2,1,0:T(8,128)} %bitcast.68) | data formatting | bytes 12582912
  (6 shorter events, 0.0 us)
Async XLA Ops:
  45.5 68.1 %copy-start = (s32[2,256]{1,0:T(2,128)S(1)}, s32[2,256]{1,0:T(2,128)}, u32[]{:S(2)}) copy-start(s32[2,256]{1,0:T(2,128)} %param.25) | copy-start | bytes 6148
  45.5 68.1 %copy-start.1 = (s32[2,256]{1,0:T(2,128)S(1)}, s32[2,256]{1,0:T(2,128)}, u32[]{:S(2)}) copy-start(s32[2,256]{1,0:T(2,128)} %param.24) | copy-start | bytes 6148

commit v6 on v5

--- a/solution.py
+++ b/solution.py
@@ -401,7 +401,7 @@
     own = layout.own()
     layout.greet(own)
     jobs = gather_jobs(layout, own, plan, shards, fulls, send_sems, recv_sems, local_sems)
-    for todo in run_rounds(jobs, len(layout.dims), 4):
+    for todo in run_rounds(jobs, len(layout.dims), 5):
         for job, stage in todo:
             job.advance(stage)
     for job in jobs:
@@ -724,7 +724,6 @@
     wide = inner_w.shape[1]
     blocks, pieces = total // rows, wide // piece
     held = rows // seq_len
-    cls_grad = cls_grad.reshape(blocks, held, width)
     block = pl.BlockSpec((rows, width), lambda i: (jnp.minimum(i, blocks - 1), 0))
     return pl.pallas_call(
         functools.partial(feed_kernel, seq_len, blocks, pieces),
@@ -1092,10 +1091,15 @@
         narrow = pre_grad.astype(jnp.bfloat16)
         pool_grad[...] = dot_left_t(cls_rows, narrow).astype(jnp.bfloat16)
         shift_grad[...] = column_sum(pre_grad)
-        cls_grad[...] = dot_right_t(narrow, pool_w[...])
-
-
-def rank(layout, cls_sum, inner_w, outer_w, pool_w, vec, bias, nodes, micros, piece, collective_id):
+        value = dot_right_t(narrow, pool_w[...])
+        held = cls_grad.shape[1]
+        for at in range(cls_grad.shape[0]):
+            cls_grad[at] = value[at * held : (at + 1) * held]
+
+
+def rank(
+    layout, cls_sum, inner_w, outer_w, pool_w, vec, bias, nodes, micros, piece, held, collective_id
+):
     sentences, width = cls_sum.shape
     wide = inner_w.shape[1]
     steps = wide // piece
@@ -1104,7 +1108,7 @@
         functools.partial(rank_kernel, layout, micros, node_dev, steps),
         grid=(steps,),
         out_shape=[
-            jax.ShapeDtypeStruct((sentences, width), jnp.float32),
+            jax.ShapeDtypeStruct((sentences // held, held, width), jnp.float32),
             jax.ShapeDtypeStruct((width, width), jnp.bfloat16),
             jax.ShapeDtypeStruct((1, width), jnp.float32),
         ],
@@ -1118,7 +1122,7 @@
             whole(nodes.shape),
         ],
         out_specs=[
-            pl.BlockSpec((sentences, width), lambda i: (0, 0)),
+            whole((sentences // held, held, width)),
             pl.BlockSpec((width, width), lambda i: (0, 0)),
             pl.BlockSpec((1, width), lambda i: (0, 0)),
         ],
@@ -1250,6 +1254,7 @@
         node_rows,
         micro_count,
         768,
+        256 // seq_len,
         2,
     )
     block_out, first_grad, grad_inner, grad_outer, grad_proj, vec_grad, grad_bias = feed(

time: 357 us -> 351 us (0.983)
  no operation moved by 1% of the time
where the time goes in v6:
time: 351 us; the launch traced here: 349 us
  Pallas kernels  331 us (94%)
  local copies, waits for them, and re-layouts  15.3 us (4%)
    pallas_call x1, Pallas kernels, back(): pl.pallas_call(functools.partial(back_kernel, layout, seq_len, blocks, pl...  109 us
    pallas_call x1, Pallas kernels, feed(): pl.pallas_call(functools.partial(feed_kernel, seq_len, blocks, pieces), g...  84.9 us
    pallas_call x1, Pallas kernels, attend(): pl.pallas_call(functools.partial(attend_kernel, layout, seq_len, plan, en...  68.2 us
    pallas_call x1, Pallas kernels, gather_all(): pl.pallas_call(functools.partial(gather_kernel, layout, plan, len(arrays)...  36 us
    pallas_call x1, Pallas kernels, rank(): pl.pallas_call(functools.partial(rank_kernel, layout, micros, node_dev, s...  30.3 us
    unnamed x7, local copies, waits for them, and re-layouts  7.21 us

profile of v6, /device:TPU:0, one launch (start us, length us, event | category | flops | bytes accessed | tf_op | source)
XLA Modules:
  0.0 348.7 jit_solution(1428580135141506133)
XLA Ops:
  0.7 0.9 concatenate.10
  1.5 0.6 pad_convert_fusion
  2.1 36.0 %shard_map.357 = (bf16[2,2,2,4,24,768]{5,4,3,2,1,0:T(8,128)(2,1)}, bf16[2,2,2,4,24,768]{5,4,3,2,1,0:T(8,128)(2,1)}, bf16[2,2,2,4,24,768]{5,4,3,2,1,0:T(8,128)(2,...) custom-call(bf16[24,768]{1,0:T(8,128)(2,1)} %refs_0_.2, bf16[24,768]{1,0:T(8,128)(2,1)} %refs_1_.2, ...), custom_call_target="tpu_custom_call" | custom-call | tf_op jit(solution)/shard_map/pallas_call | solution.py:412
  38.1 0.9 copy.66
  39.1 0.1 copy.63
  39.2 0.1 copy.56
  39.3 0.1 reshape.193
  39.4 0.6 pad.14.vec_ref
  40.1 0.8 compare_convert_fusion.diag_ref
  40.8 1.3 reshape.186.lengths_ref
  42.1 0.0 copy-start
  42.1 0.0 copy-start.1
  42.1 68.2 %shard_map.358 = (bf16[2048,768]{1,0:T(8,128)(2,1)}, bf16[2048,768]{1,0:T(8,128)(2,1)}, bf16[2048,768]{1,0:T(8,128)(2,1)}, bf16[2048,768]{1,0:T(8,128)(2,1)}, f3...) custom-call(s32[32]{0:T(128)} %reshape.186.lengths_ref, ...), custom_call_target="tpu_custom_call" | custom-call | tf_op jit(solution)/shard_map/pallas_call | solution.py:603
  110.3 0.1 slice.17
  110.4 0.7 reshape.199.bias_ref
  111.1 0.0 copy-done
  111.1 0.0 copy-done.1
  111.1 0.2 select_reduce_fusion
  111.3 0.1 reshape.201
  111.4 0.1 copy.58
  111.4 0.1 reshape.200
  111.5 0.1 copy.57
  111.6 0.1 reshape.202
  111.7 0.1 copy.59
  111.8 0.1 copy.62
  111.9 0.2 convert_element_type.69
  112.1 0.6 pad.15.node_ref
  112.7 30.3 %shard_map.359 = (f32[8,4,768]{2,1,0:T(4,128)}, bf16[768,768]{1,0:T(8,128)(2,1)}, f32[1,768]{1,0:T(1,128)}) custom-call(f32[32,768]{1,0:T(8,128)} %bitcast.87, bf16[768,3072]{1,0:T(8,128)(2,1)} %bitcast.62, bf16[3072,768]{1,0:T(8,128)(2,1)} %bitcast.64, bf16[768,768]{1,0:T(8,128)(2,1)} %bitcast.80, f32[16,768]{1,0:T(8,128)} %pad.14.vec_ref, ...), custom_call_target="tpu_custom_call" | custom-call | tf_op jit(solution)/shard_map/pallas_call | solution.py:1107
  143.1 84.9 %shard_map.360 = (bf16[2048,768]{1,0:T(8,128)(2,1)}, f32[2048,768]{1,0:T(8,128)}, bf16[768,3072]{1,0:T(8,128)(2,1)}, bf16[3072,768]{1,0:T(8,128)(2,1)}, bf16[768...) custom-call(f32[2048,768]{1,0:T(8,128)} %get-tuple-element.64.sum_ref, bf16[2048,768]{1,0:T(8,128)(2,1)} %bitcast.79, ...), custom_call_target="tpu_custom_call" | custom-call | tf_op jit(solution)/shard_map/pallas_call | solution.py:728
  227.9 109.3 %shard_map.361 = (f32[2048,768]{1,0:T(8,128)}, f32[16,768]{1,0:T(8,128)}, f32[24,3072]{1,0:T(8,128)}, f32[96,768]{1,0:T(8,128)}, f32[24,768]{1,0:T(8,128)}, /*in...) custom-call(s32[32]{0:T(128)} %reshape.186.lengths_ref, ...), custom_call_target="tpu_custom_call" | custom-call | tf_op jit(solution)/shard_map/pallas_call | solution.py:938
  337.3 2.1 shard_map.362
  339.4 0.7 slice.15
  340.2 0.6 dynamic_slice.7
  340.7 1.6 dynamic-slice_bitcast_fusion
  342.4 6.2 %copy.68 = f32[2,2,8,64,768]{4,3,2,1,0:T(8,128)} copy(f32[2,2,8,64,768]{4,3,2,1,0:T(8,128)} %bitcast.68) | data formatting | bytes 12582912
  (6 shorter events, 0.0 us)
Async XLA Ops:
  42.1 69.0 %copy-start = (s32[2,256]{1,0:T(2,128)S(1)}, s32[2,256]{1,0:T(2,128)}, u32[]{:S(2)}) copy-start(s32[2,256]{1,0:T(2,128)} %param.25) | copy-start | bytes 6148
  42.1 69.0 %copy-start.1 = (s32[2,256]{1,0:T(2,128)S(1)}, s32[2,256]{1,0:T(2,128)}, u32[]{:S(2)}) copy-start(s32[2,256]{1,0:T(2,128)} %param.24) | copy-start | bytes 6148
